TPU v7x, 32 devices: a whole 2x2x4 slice. The times are simulated.
32 devices in a mesh: section: 2 (over core), dp: 8 (over z, y), mp: 2 (over x).
Axes of the slice: x: 2, y: 2, z: 4, core: 2. Of those that a mesh axis runs over, the one named last changes fastest.
Arguments:
- tokens: bfloat16 [2, 8, 256, 768], P(None, 'dp', 'mp'), may hold values from -6 to 6
- clip_lengths: int32 [2, 8], P(None, 'dp'), may hold values from 156 to 157
- clip_cells: int32 [2, 8, 256], P(None, 'dp'), may hold values from 0 to 1567, as said below
- enc_qkv: bfloat16 [768, 3, 768], P(None, None, 'mp'), may hold values from -0.21875 to 0.21875
- enc_attn_out: bfloat16 [768, 768], P('mp'), may hold values from -0.875 to 0.875
- enc_up: bfloat16 [768, 3072], P(None, 'mp'), may hold values from -0.21875 to 0.21875
- enc_down: bfloat16 [3072, 768], P('mp'), may hold values from -0.109375 to 0.109375
- enc_gain_one: float32 [768], replicated, may hold values from 0.1 to 1.9
- enc_gain_two: float32 [768], replicated, may hold values from 0.1 to 1.9
- bridge_weight: bfloat16 [768, 384], replicated, may hold values from -0.21875 to 0.21875
- mask_token: float32 [384], replicated, may hold values from -6 to 6
- position_embed: float32 [1568, 384], P('mp'), may hold values from -6 to 6
- dec_qkv: bfloat16 [384, 3, 384], P(None, None, 'mp'), may hold values from -0.3125 to 0.3125
- dec_attn_out: bfloat16 [384, 384], P('mp'), may hold values from -1.75 to 1.75
- dec_up: bfloat16 [384, 1536], P(None, 'mp'), may hold values from -0.875 to 0.875
- dec_down: bfloat16 [1536, 384], P('mp'), may hold values from -0.15625 to 0.15625
- dec_gain_one: float32 [384], replicated, may hold values from 0.1 to 1.9
- dec_gain_two: float32 [384], replicated, may hold values from 0.1 to 1.9
- cotangent: bfloat16 [2, 8, 1568, 384], P(None, 'dp', 'mp'), may hold values from -6 to 6
Outputs:
- decoded: float32 [2, 8, 1568, 384], P(None, 'dp', 'mp', 'section')
- tokens_grad: float32 [2, 8, 256, 768], P(None, 'dp', 'mp', 'section')
- enc_qkv_grad: float32 [768, 3, 768], P(('section', 'dp'), None, 'mp')
- enc_attn_out_grad: float32 [768, 768], P('mp', ('section', 'dp'))
- enc_up_grad: float32 [768, 3072], P(('section', 'dp'), 'mp')
- enc_down_grad: float32 [3072, 768], P('mp', ('section', 'dp'))
- enc_gain_one_grad: float32 [768], replicated
- enc_gain_two_grad: float32 [768], replicated
- bridge_grad: float32 [768, 384], replicated
- mask_grad: float32 [384], replicated
- position_grad: float32 [1568, 384], P('mp', ('section', 'dp'))
- dec_qkv_grad: float32 [384, 3, 384], P(('section', 'dp'), None, 'mp')
- dec_attn_out_grad: float32 [384, 384], P('mp', ('section', 'dp'))
- dec_up_grad: float32 [384, 1536], P(('section', 'dp'), 'mp')
- dec_down_grad: float32 [1536, 384], P('mp', ('section', 'dp'))
- dec_gain_one_grad: float32 [384], replicated
- dec_gain_two_grad: float32 [384], replicated
Inputs may be any that keep to these rules, and one draw needn't show every extreme that they name: `clip_cells`: within each row of 256 slots the entries are distinct.
All inputs are finite; a program needn't handle non-finite values.
Results may differ from a plain program's by a relative error of at most 0.03.
Values may be sent and summed in bfloat16 or wider, within the bound.
A program may use at most 256 MiB of HBM per device.

v0:
```python
import jax
import jax.numpy as jnp
from jax import lax
from jax.sharding import PartitionSpec as P

HEAD = 64
LDEC = 1568


EPS = 1e-06
NEG = -1e30
HIGH = lax.Precision.HIGHEST
FLOAT = jnp.float32
BRAIN = jnp.bfloat16


def from_behind(value, axis, steps):
    count = lax.axis_size(axis)
    first, last = (max(0, -steps), min(count, count - steps))
    return lax.ppermute(value, axis, [(source, source + steps) for source in range(first, last)])


def only(active, compute):
    return lax.cond(active, compute, lambda: jax.tree.map(jnp.zeros_like, compute()))


def contract(first_op, second_op, dim_first, dim_second):
    return lax.dot_general(
        first_op, second_op, (((dim_first,), (dim_second,)), ((), ())), preferred_element_type=FLOAT
    )


def layer_norm(stream, norm_gain):
    centre = stream - jnp.mean(stream, -1, keepdims=True)
    spread = jnp.mean(centre * centre, -1, keepdims=True)
    return centre * lax.rsqrt(spread + EPS) * norm_gain


def widen(shard_rows):
    return lax.all_gather(shard_rows, "mp", axis=0, tiled=True)


def narrow(operand, weight, along, active):
    return lax.psum_scatter(
        only(active, lambda: contract(operand, weight, 1, along)),
        "mp",
        scatter_dimension=0,
        tiled=True,
    )


def attend(queries, keys_all, values, usable):
    seq_len = queries.shape[0]
    head_count = queries.shape[1]
    blocks = 2 if seq_len >= 1024 and seq_len % 2 == 0 else 1
    score_scale = HEAD ** (-0.5)

    def one_block(query_block):
        scores = (
            jnp.einsum("qhd,khd->hqk", query_block, keys_all, preferred_element_type=FLOAT)
            * score_scale
        )
        scores = jnp.where(usable[None, None, :], scores, NEG)
        highest = jnp.max(scores, -1, keepdims=True)
        raised = jnp.exp(scores - highest)
        summed = jnp.sum(raised, -1, keepdims=True)
        weights = (raised / summed).astype(BRAIN)
        blended = jnp.einsum("hqk,khd->qhd", weights, values, preferred_element_type=FLOAT)
        return (blended, (highest + jnp.log(summed))[..., 0])

    blended, log_total = lax.map(
        one_block, queries.reshape(blocks, seq_len // blocks, head_count, HEAD)
    )
    return (blended.reshape(seq_len, head_count * HEAD), log_total)


def attend_back(queries, keys_all, values, usable, log_total, grad_out):
    seq_len = queries.shape[0]
    head_count = queries.shape[1]
    blocks = log_total.shape[0]
    block_len = seq_len // blocks
    score_scale = HEAD ** (-0.5)

    def one_block(carry, items):
        key_grad, value_grad = carry
        query_block, grad_block, lse_block = items
        scores = (
            jnp.einsum("qhd,khd->hqk", query_block, keys_all, preferred_element_type=FLOAT)
            * score_scale
        )
        scores = jnp.where(usable[None, None, :], scores, NEG)
        weights = jnp.exp(scores - lse_block[..., None])
        weight_grad = jnp.einsum("qhd,khd->hqk", grad_block, values, preferred_element_type=FLOAT)
        score_grad = (
            weights * (weight_grad - jnp.sum(weights * weight_grad, -1, keepdims=True))
        ).astype(BRAIN)
        query_grad = (
            jnp.einsum("hqk,khd->qhd", score_grad, keys_all, preferred_element_type=FLOAT)
            * score_scale
        )
        key_grad = (
            key_grad
            + jnp.einsum("hqk,qhd->khd", score_grad, query_block, preferred_element_type=FLOAT)
            * score_scale
        )
        value_grad = value_grad + jnp.einsum(
            "hqk,qhd->khd", weights.astype(BRAIN), grad_block, preferred_element_type=FLOAT
        )
        return ((key_grad, value_grad), query_grad)

    zero_grad = jnp.zeros(keys_all.shape, FLOAT)
    shaped_queries = queries.reshape(blocks, block_len, head_count, HEAD)
    shaped_grads = grad_out.reshape(blocks, block_len, head_count, HEAD)
    (key_grad, value_grad), query_grad = lax.scan(
        one_block, (zero_grad, zero_grad), (shaped_queries, shaped_grads, log_total)
    )
    return (query_grad.reshape(seq_len, head_count, HEAD), key_grad, value_grad)


def block_forward(stream, params, active, usable):
    qkv_weight, out_weight, up_weight, down_weight, gain_one, gain_two = params
    feature_dim = stream.shape[1]
    head_count = qkv_weight.shape[2] // HEAD
    flat_qkv = qkv_weight.reshape(feature_dim, -1)
    normed = widen(layer_norm(stream, gain_one).astype(BRAIN))
    seq_len = normed.shape[0]
    triple = only(active, lambda: jnp.dot(normed, flat_qkv, preferred_element_type=FLOAT))
    triple = triple.astype(BRAIN).reshape(seq_len, 3, head_count, HEAD)
    blended, log_total = only(
        active, lambda: attend(triple[:, 0], triple[:, 1], triple[:, 2], usable)
    )
    blended = blended.astype(BRAIN)
    middle = stream + narrow(blended, out_weight, 0, active)
    normed_two = widen(layer_norm(middle, gain_two).astype(BRAIN))
    before = only(active, lambda: jnp.dot(normed_two, up_weight, preferred_element_type=FLOAT))
    hidden = jax.nn.gelu(before, approximate=False).astype(BRAIN)
    result = middle + narrow(hidden, down_weight, 0, active)
    return (
        result,
        (stream, middle, normed, triple, blended, log_total, normed_two, before, hidden),
    )


def block_backward(out_grad, saved, params, active, usable):
    stream, middle, normed, triple, blended, log_total, normed_two, before, hidden = saved
    qkv_weight, out_weight, up_weight, down_weight, gain_one, gain_two = params
    feature_dim = stream.shape[1]
    seq_len = normed.shape[0]
    head_count = qkv_weight.shape[2] // HEAD
    down_in = widen(out_grad.astype(BRAIN))
    hidden_grad = only(active, lambda: contract(down_in, down_weight, 1, 1))
    down_grad = only(active, lambda: contract(hidden, down_in, 0, 0))
    gelu_value, gelu_pull = jax.vjp(lambda inner: jax.nn.gelu(inner, approximate=False), before)
    before_grad = gelu_pull(hidden_grad)[0].astype(BRAIN)
    up_grad = only(active, lambda: contract(normed_two, before_grad, 0, 0))
    normed_two_grad = narrow(before_grad, up_weight, 1, active)
    norm_value, norm_pull = jax.vjp(layer_norm, middle, gain_two)
    middle_part, gain_two_grad = norm_pull(normed_two_grad)
    middle_grad = out_grad + middle_part
    attn_in = widen(middle_grad.astype(BRAIN))
    out_weight_grad = only(active, lambda: contract(blended, attn_in, 0, 0))
    blended_grad = only(active, lambda: contract(attn_in, out_weight, 1, 1))
    blended_grad = blended_grad.astype(BRAIN).reshape(seq_len, head_count, HEAD)
    query_grad, key_grad, value_grad = only(
        active,
        lambda: attend_back(
            triple[:, 0], triple[:, 1], triple[:, 2], usable, log_total, blended_grad
        ),
    )
    triple_grad = (
        jnp.stack([query_grad, key_grad, value_grad], 1).astype(BRAIN).reshape(seq_len, -1)
    )
    qkv_grad = only(active, lambda: contract(normed, triple_grad, 0, 0)).reshape(feature_dim, 3, -1)
    normed_grad = narrow(triple_grad, qkv_weight.reshape(feature_dim, -1), 1, active)
    norm_value_one, norm_pull_one = jax.vjp(layer_norm, stream, gain_one)
    stream_part, gain_one_grad = norm_pull_one(normed_grad)
    return (
        middle_grad + stream_part,
        (qkv_grad, out_weight_grad, up_grad, down_grad),
        (gain_one_grad, gain_two_grad),
    )


def add_tree(total_tree, new_tree):
    if total_tree is None:
        return new_tree
    return jax.tree.map(jnp.add, total_tree, new_tree)


def per_device(
    tokens,
    clip_lengths,
    clip_cells,
    enc_qkv,
    enc_attn_out,
    enc_up,
    enc_down,
    enc_gain_one,
    enc_gain_two,
    bridge_weight,
    mask_token,
    position_embed,
    dec_qkv,
    dec_attn_out,
    dec_up,
    dec_down,
    dec_gain_one,
    dec_gain_two,
    cotangent,
):
    encoder_on = lax.axis_index("section") == 0
    decoder_on = jnp.logical_not(encoder_on)
    enc_params = (enc_qkv, enc_attn_out, enc_up, enc_down, enc_gain_one, enc_gain_two)
    dec_params = (dec_qkv, dec_attn_out, dec_up, dec_down, dec_gain_one, dec_gain_two)
    micro = tokens.shape[0]
    slot_count = clip_cells.shape[2]
    cell_count = position_embed.shape[0]
    slot_ids = jnp.arange(slot_count, dtype=jnp.int32)
    cell_ids = lax.axis_index("mp") * cell_count + jnp.arange(cell_count, dtype=jnp.int32)
    dec_usable = jnp.ones((LDEC,), bool)
    kept = []
    decoded = []
    for step in range(micro):
        length_one = clip_lengths[step, 0]
        cells_one = clip_cells[step, 0]
        enc_usable = slot_ids < length_one
        enc_in = tokens[step, 0].astype(FLOAT)
        enc_result, enc_saved = block_forward(enc_in, enc_params, encoder_on, enc_usable)
        enc_rounded = enc_result.astype(BRAIN)
        visible = only(
            encoder_on, lambda: jnp.dot(enc_rounded, bridge_weight, preferred_element_type=FLOAT)
        ).astype(BRAIN)
        visible_all = lax.all_gather(visible, "mp", axis=0, tiled=True)
        fill_place = (
            (cells_one[None, :] == cell_ids[:, None]) & (slot_ids[None, :] < length_one)
        ).astype(BRAIN)
        fill_seen_count = jnp.sum(fill_place.astype(FLOAT), 1, keepdims=True)
        placed = only(
            encoder_on, lambda: jnp.dot(fill_place, visible_all, preferred_element_type=FLOAT)
        )
        filled = placed + (1.0 - fill_seen_count) * mask_token + position_embed
        place = fill_place
        seen_count = fill_seen_count
        dec_in = from_behind(filled, "section", 1)
        dec_result, dec_saved = block_forward(dec_in, dec_params, decoder_on, dec_usable)
        decoded.append(
            lax.psum_scatter(
                jnp.where(decoder_on, dec_result, 0.0), "section", scatter_dimension=1, tiled=True
            )
        )
        enc_saved = None
        dec_saved = None
        kept.append(
            (enc_in, enc_usable, enc_rounded, enc_saved, dec_in, dec_saved, place, seen_count)
        )
    token_grads = []
    enc_weights = None
    enc_gains = None
    dec_weights = None
    dec_gains = None
    other_grads = None
    for step in range(micro):
        enc_in, enc_usable, enc_rounded, enc_saved, dec_in, dec_saved, place, seen_count = kept[
            step
        ]
        dec_unused, dec_saved = block_forward(dec_in, dec_params, decoder_on, dec_usable)
        grad_top = jnp.where(decoder_on, cotangent[step, 0].astype(FLOAT), 0.0)
        dec_in_grad, dec_weight_grads, dec_gain_grads = block_backward(
            grad_top, dec_saved, dec_params, decoder_on, dec_usable
        )
        arrived = from_behind(dec_in_grad, "section", -1)
        grad_used = jnp.where(encoder_on, arrived, 0.0)
        spread_back = only(
            encoder_on,
            lambda: lax.dot_general(
                place.astype(FLOAT),
                grad_used,
                (((0,), (0,)), ((), ())),
                precision=HIGH,
                preferred_element_type=FLOAT,
            ),
        )
        fill_visible_grad = lax.psum_scatter(
            spread_back, "mp", scatter_dimension=0, tiled=True
        ).astype(BRAIN)
        visible_grad = fill_visible_grad
        mask_part = jnp.sum((1.0 - seen_count) * grad_used, 0)
        enc_result, enc_saved = block_forward(enc_in, enc_params, encoder_on, enc_usable)
        enc_rounded = enc_result.astype(BRAIN)
        bridge_part = only(encoder_on, lambda: contract(enc_rounded, visible_grad, 0, 0))
        enc_out_grad = only(encoder_on, lambda: contract(visible_grad, bridge_weight, 1, 1))
        enc_in_grad, enc_weight_grads, enc_gain_grads = block_backward(
            enc_out_grad, enc_saved, enc_params, encoder_on, enc_usable
        )
        token_grads.append(
            lax.psum_scatter(
                jnp.where(encoder_on, enc_in_grad, 0.0), "section", scatter_dimension=1, tiled=True
            )
        )
        enc_weights = add_tree(enc_weights, enc_weight_grads)
        enc_gains = add_tree(enc_gains, enc_gain_grads)
        dec_weights = add_tree(dec_weights, dec_weight_grads)
        dec_gains = add_tree(dec_gains, dec_gain_grads)
        other_grads = add_tree(other_grads, (bridge_part, mask_part, grad_used))
    summed_big = (
        lax.psum_scatter(enc_weights[0], ("section", "dp"), scatter_dimension=0, tiled=True),
        lax.psum_scatter(enc_weights[1], ("section", "dp"), scatter_dimension=1, tiled=True),
        lax.psum_scatter(enc_weights[2], ("section", "dp"), scatter_dimension=0, tiled=True),
        lax.psum_scatter(enc_weights[3], ("section", "dp"), scatter_dimension=1, tiled=True),
        lax.psum_scatter(dec_weights[0], ("section", "dp"), scatter_dimension=0, tiled=True),
        lax.psum_scatter(dec_weights[1], ("section", "dp"), scatter_dimension=1, tiled=True),
        lax.psum_scatter(dec_weights[2], ("section", "dp"), scatter_dimension=0, tiled=True),
        lax.psum_scatter(dec_weights[3], ("section", "dp"), scatter_dimension=1, tiled=True),
        lax.psum_scatter(other_grads[2], ("section", "dp"), scatter_dimension=1, tiled=True),
    )
    enc_final = summed_big[0:4]
    dec_final = summed_big[4:8]
    position_final = summed_big[8]
    summed_small = lax.psum(
        (enc_gains[0], enc_gains[1], dec_gains[0], dec_gains[1], other_grads[0], other_grads[1]),
        ("section", "dp", "mp"),
    )
    return (
        jnp.stack(decoded)[:, None],
        jnp.stack(token_grads)[:, None],
        enc_final[0],
        enc_final[1],
        enc_final[2],
        enc_final[3],
        summed_small[0],
        summed_small[1],
        summed_small[4],
        summed_small[5],
        position_final,
        dec_final[0],
        dec_final[1],
        dec_final[2],
        dec_final[3],
        summed_small[2],
        summed_small[3],
    )


def solution(mesh):
    return jax.shard_map(
        per_device,
        mesh=mesh,
        in_specs=(
            P(None, "dp", "mp", None),
            P(None, "dp"),
            P(None, "dp", None),
            P(None, None, "mp"),
            P("mp", None),
            P(None, "mp"),
            P("mp", None),
            P(),
            P(),
            P(),
            P(),
            P("mp", None),
            P(None, None, "mp"),
            P("mp", None),
            P(None, "mp"),
            P("mp", None),
            P(),
            P(),
            P(None, "dp", "mp", None),
        ),
        out_specs=(
            P(None, "dp", "mp", "section"),
            P(None, "dp", "mp", "section"),
            P(("section", "dp"), None, "mp"),
            P("mp", ("section", "dp")),
            P(("section", "dp"), "mp"),
            P("mp", ("section", "dp")),
            P(),
            P(),
            P(),
            P(),
            P("mp", ("section", "dp")),
            P(("section", "dp"), None, "mp"),
            P("mp", ("section", "dp")),
            P(("section", "dp"), "mp"),
            P("mp", ("section", "dp")),
            P(),
            P(),
        ),
        check_vma=False,
    )
```

profile of v0, /device:TPU:17, one launch (start us, length us, event | category | flops | bytes accessed | tf_op | source)
XLA Modules:
  0.0 2227.3 jit_solution(1102968736947734890)
XLA Ops:
  39.2 11.6 reduce-scatter.75.cloned.1.call-done
  50.8 20.4 reduce-scatter.85.cloned.1.call-done
  71.2 19.7 reduce-scatter.65.cloned.1.call-done
  90.9 19.7 reduce-scatter.69.cloned.1.call-done
  152.2 20.2 reduce-scatter.67.cloned.1.call-done
  196.3 22.7 %all-gather.11.cloned.1.call-done = bf16[1568,384]{1,0:T(8,128)(2,1)} async-done(((bf16[784,384]{1,0:T(8,128)(2,1)}), bf16[1568,384]{1,0:T(8,128)(2,1)}) %all-gather.11.cloned.1.call-update) | async-done | bytes 1204240 | tf_op jit(solution)/shard_map/all_gather | solution.py:40
  222.7 55.4 %conditional.109 = (f32[2,3,784]{2,1,0:T(4,128)}, bf16[1568,192]{0,1:T(8,128)(2,1)}) conditional(s32[]{:T(128)} %convert_element_type.488, () %tuple.699, bf16[1568,3,3,64]{0,3,2,1:T(8,128)(2,1)} %get-tuple-element.1161), branch_computations={%region_90.91_spmd, %region_91.96_spmd} | conditional | flops 977300672 | bytes 54999652 | solution.py:24
  225.5 50.6 %while.78 = (s32[]{:T(128)}, bf16[2,784,3,64]{1,3,2,0:T(8,128)(2,1)S(1)}, f32[2,3,784]{2,1,0:T(4,128)}, bf16[2,784,3,64]{1,3,2,0:T(8,128)(2,1)S(1)}, bf16[1568,3...) while((s32[]{:T(128)}, bf16[2,784,3,64]{1,3,2,0:T(8,128)(2,1)S(1)}, ...), condition=%wide.region_95.95_spmd, body=%wide.region_92.94_spmd.sunk | while | flops 977300672 | bytes 46570004 | solution.py:71
  284.1 32.1 %reduce-scatter.121.cloned.1.call-done = f32[784,384]{1,0:T(8,128)} async-done(((f32[1568,384]{1,0:T(8,128)}), f32[784,384]{1,0:T(8,128)}) %reduce-scatter.121.cloned.1.call-update) | async-done | bytes 1204240 | tf_op jit(solution)/shard_map/reduce_scatter | solution.py:44
  319.4 22.2 all-gather.21.cloned.1.call-done
  346.5 19.6 all-gather.19.cloned.1.call-done
  370.9 12.5 multiply_convert_fusion.5
  391.2 34.8 %reduce-scatter.123.cloned.1.call-done = f32[784,384]{1,0:T(8,128)} async-done(((f32[1568,384]{1,0:T(8,128)}), f32[784,384]{1,0:T(8,128)}) %reduce-scatter.123.cloned.1.call-update) | async-done | bytes 1204240 | tf_op jit(solution)/shard_map/reduce_scatter | solution.py:44
  431.3 23.1 %all-gather.23.cloned.1.call-done = bf16[1568,384]{1,0:T(8,128)(2,1)} async-done(((bf16[784,384]{1,0:T(8,128)(2,1)}), bf16[1568,384]{1,0:T(8,128)(2,1)}) %all-gather.23.cloned.1.call-update) | async-done | bytes 1204240 | tf_op jit(solution)/shard_map/all_gather | solution.py:40
  456.4 91.2 %conditional.115 = (bf16[1568,1,3,64]{0,3,2,1:T(8,128)(2,1)}, bf16[1568,1,3,64]{0,3,2,1:T(8,128)(2,1)}, bf16[1568,1,3,64]{0,3,2,1:T(8,128)(2,1)}) conditional(s32[]{:T(128)} %convert_element_type.488, () %tuple.707, (bf16[1568,3,3,64]{0,3,2,1:T(8,128)(2,1)}, bf16[1568,192]{0,1:T(8,128)(2,1)S(1)}, f32[2,3,784]{2,1,0:T(4,128)}) %tuple.710), branch_computations={%region_112.113_spmd, %region_113.117_spmd} | conditional | flops 2406789888 | bytes 261827424 | solution.py:24
  462.4 78.1 %while.80 = (s32[]{:T(128)}, f32[1568,3,64]{0,2,1:T(8,128)S(1)}, f32[1568,3,64]{0,2,1:T(8,128)S(1)}, bf16[2,784,3,64]{1,3,2,0:T(8,128)(2,1)}, bf16[2,784,3,64]{1...) while((s32[]{:T(128)}, f32[1568,3,64]{0,2,1:T(8,128)S(1)}, ...), condition=%wide.region_116.116_spmd.clone, body=%wide.region_114.115_spmd.clone.sunk | while | flops 2406187776 | bytes 247376624 | solution.py:114
  466.5 9.1 multiply_reduce_fusion.38
  476.0 9.9 multiply_convert_fusion.21
  505.5 9.1 multiply_reduce_fusion.38
  515.0 9.9 multiply_convert_fusion.21
  557.9 49.0 %conditional.92 = (bf16[1568,192]{0,1:T(8,128)(2,1)}) conditional(s32[]{:T(128)} %convert_element_type.488, () %tuple.663, bf16[1568,3,3,64]{0,3,2,1:T(8,128)(2,1)S(1)} %get-tuple-element.2722), branch_computations={%region_27.28_spmd, %region_28.33_spmd} | conditional | flops 977308544 | bytes 132906880 | solution.py:24
  559.7 45.2 %while.76 = (s32[]{:T(128)}, bf16[2,784,3,64]{1,3,2,0:T(8,128)(2,1)S(1)}, bf16[2,784,3,64]{1,3,2,0:T(8,128)(2,1)S(1)}, bf16[1568,3,64]{0,2,1:T(8,128)(2,1)S(1)}, bf16[1568,3,64]{0,2,1:T(8,128)(2,1)}, /*index=5*/s32[]{:T(128)}) while((s32[]{:T(128)}, bf16[2,784,3,64]{1,3,2,0:T(8,128)(2,1)S(1)}, bf16[2,784,3,64]{1,3,2,0:T(8,128)(2,1)S(1)}, ...), condition=%wide.region_32.32_spmd, body=%wide.region_29.31_spmd.sunk | while | flops 977308544 | bytes 124477248 | solution.py:71
  567.4 14.8 fusion.694
  590.1 14.8 fusion.694
  619.2 25.8 %reduce-scatter.109.cloned.1.call-done = f32[784,384]{1,0:T(8,128)} async-done(((f32[1568,384]{1,0:T(8,128)}), f32[784,384]{1,0:T(8,128)}) %reduce-scatter.109.cloned.1.call-update) | async-done | bytes 1204240 | tf_op jit(solution)/shard_map/reduce_scatter | solution.py:44
  649.6 23.2 %all-gather.15.cloned.1.call-done = bf16[1568,384]{1,0:T(8,128)(2,1)} async-done(((bf16[784,384]{1,0:T(8,128)(2,1)}), bf16[1568,384]{1,0:T(8,128)(2,1)}) %all-gather.15.cloned.1.call-update) | async-done | bytes 1204240 | tf_op jit(solution)/shard_map/all_gather | solution.py:40
  676.7 55.1 %conditional.129 = (f32[2,3,784]{2,1,0:T(4,128)}, bf16[1568,192]{0,1:T(8,128)(2,1)}) conditional(s32[]{:T(128)} %convert_element_type.488, () %tuple.736, bf16[1568,3,3,64]{0,3,2,1:T(8,128)(2,1)} %get-tuple-element.1173), branch_computations={%region_160.161_spmd, %region_161.166_spmd} | conditional | flops 977300672 | bytes 54999652 | solution.py:24
  679.1 50.6 %while.79 = (s32[]{:T(128)}, bf16[2,784,3,64]{1,3,2,0:T(8,128)(2,1)S(1)}, f32[2,3,784]{2,1,0:T(4,128)}, bf16[2,784,3,64]{1,3,2,0:T(8,128)(2,1)S(1)}, bf16[1568,3...) while((s32[]{:T(128)}, bf16[2,784,3,64]{1,3,2,0:T(8,128)(2,1)S(1)}, ...), condition=%wide.region_165.165_spmd, body=%wide.region_162.164_spmd.sunk | while | flops 977300672 | bytes 46570004 | solution.py:71
  735.8 34.2 %reduce-scatter.127.cloned.1.call-done = f32[784,384]{1,0:T(8,128)} async-done(((f32[1568,384]{1,0:T(8,128)}), f32[784,384]{1,0:T(8,128)}) %reduce-scatter.127.cloned.1.call-update) | async-done | bytes 1204240 | tf_op jit(solution)/shard_map/reduce_scatter | solution.py:44
  773.1 21.5 all-gather.27.cloned.1.call-done
  799.5 20.2 all-gather.25.cloned.1.call-done
  824.5 12.6 multiply_convert_fusion.4
  846.4 33.3 %reduce-scatter.129.cloned.1.call-done = f32[784,384]{1,0:T(8,128)} async-done(((f32[1568,384]{1,0:T(8,128)}), f32[784,384]{1,0:T(8,128)}) %reduce-scatter.129.cloned.1.call-update) | async-done | bytes 1204240 | tf_op jit(solution)/shard_map/reduce_scatter | solution.py:44
  886.2 23.2 %all-gather.29.cloned.1.call-done = bf16[1568,384]{1,0:T(8,128)(2,1)} async-done(((bf16[784,384]{1,0:T(8,128)(2,1)}), bf16[1568,384]{1,0:T(8,128)(2,1)}) %all-gather.29.cloned.1.call-update) | async-done | bytes 1204240 | tf_op jit(solution)/shard_map/all_gather | solution.py:40
  911.3 91.2 %conditional.135 = (bf16[1568,1,3,64]{0,3,2,1:T(8,128)(2,1)}, bf16[1568,1,3,64]{0,3,2,1:T(8,128)(2,1)}, bf16[1568,1,3,64]{0,3,2,1:T(8,128)(2,1)}) conditional(s32[]{:T(128)} %convert_element_type.488, () %tuple.744, (bf16[1568,3,3,64]{0,3,2,1:T(8,128)(2,1)}, bf16[1568,192]{0,1:T(8,128)(2,1)S(1)}, f32[2,3,784]{2,1,0:T(4,128)}) %tuple.747), branch_computations={%region_182.183_spmd, %region_183.187_spmd} | conditional | flops 2406789888 | bytes 261827424 | solution.py:24
  917.4 78.1 %while.86 = (s32[]{:T(128)}, f32[1568,3,64]{0,2,1:T(8,128)S(1)}, f32[1568,3,64]{0,2,1:T(8,128)S(1)}, bf16[2,784,3,64]{1,3,2,0:T(8,128)(2,1)}, bf16[2,784,3,64]{1...) while((s32[]{:T(128)}, f32[1568,3,64]{0,2,1:T(8,128)S(1)}, ...), condition=%wide.region_186.186_spmd.clone, body=%wide.region_184.185_spmd.clone.sunk | while | flops 2406187776 | bytes 247376624 | solution.py:114
  931.0 9.9 multiply_convert_fusion.20
  970.1 9.9 multiply_convert_fusion.20
  1012.7 49.0 %conditional.104 = (bf16[1568,192]{0,1:T(8,128)(2,1)}) conditional(s32[]{:T(128)} %convert_element_type.488, () %tuple.686, bf16[1568,3,3,64]{0,3,2,1:T(8,128)(2,1)S(1)} %get-tuple-element.2734), branch_computations={%region_71.72_spmd, %region_72.77_spmd} | conditional | flops 977308544 | bytes 132906880 | solution.py:24
  1014.5 45.2 %while.77 = (s32[]{:T(128)}, bf16[2,784,3,64]{1,3,2,0:T(8,128)(2,1)S(1)}, bf16[2,784,3,64]{1,3,2,0:T(8,128)(2,1)S(1)}, bf16[1568,3,64]{0,2,1:T(8,128)(2,1)S(1)}, bf16[1568,3,64]{0,2,1:T(8,128)(2,1)}, /*index=5*/s32[]{:T(128)}) while((s32[]{:T(128)}, bf16[2,784,3,64]{1,3,2,0:T(8,128)(2,1)S(1)}, bf16[2,784,3,64]{1,3,2,0:T(8,128)(2,1)S(1)}, ...), condition=%wide.region_76.76_spmd, body=%wide.region_73.75_spmd.sunk | while | flops 977308544 | bytes 124477248 | solution.py:71
  1022.2 14.9 fusion.687
  1044.9 14.8 fusion.687
  1070.0 29.9 %reduce-scatter.115.cloned.1.call-done = f32[784,384]{1,0:T(8,128)} async-done(((f32[1568,384]{1,0:T(8,128)}), f32[784,384]{1,0:T(8,128)}) %reduce-scatter.115.cloned.1.call-update) | async-done | bytes 1204240 | tf_op jit(solution)/shard_map/reduce_scatter | solution.py:44
  1154.0 21.8 reduce-scatter.87.cloned.1.call-done
  1206.7 12.5 fusion.230
  1225.7 14.4 reduce-scatter.103.cloned.1.call-done
  1240.1 20.4 reduce-scatter.101.cloned.1.call-done
  1274.8 10.6 all-gather.17.cloned.1.call-done
  1291.5 10.9 all_gather.85
  1304.6 12.5 fusion.233
  1345.8 19.6 reduce-scatter.79.cloned.1.call-done
  1372.7 30.3 %reduce-scatter.117.cloned.1.call-done = f32[784,384]{1,0:T(8,128)} async-done(((f32[1568,384]{1,0:T(8,128)}), f32[784,384]{1,0:T(8,128)}) %reduce-scatter.117.cloned.1.call-update) | async-done | bytes 1204240 | tf_op jit(solution)/shard_map/reduce_scatter | solution.py:44
  1470.6 29.1 %all-reduce.8.cloned.1.call-done = f32[384,3,192]{2,1,0:T(4,128)} async-done(((f32[384,3,192]{2,1,0:T(4,128)}), f32[384,3,192]{2,1,0:T(4,128)}) %all-reduce.8.cloned.1.call-update) | async-done | bytes 884752
  1501.7 10.7 reduce-scatter.113.cloned.1.call-done
  1513.8 39.9 %all-reduce.2 = (f32[768]{0:T(1024)}, f32[768]{0:T(1024)}, f32[384]{0:T(512)}, f32[384]{0:T(512)}, f32[384]{0:T(512)}) all-reduce(f32[768]{0:T(1024)S(1)} %add.497, f32[768]{0:T(1024)S(1)} %add.498, f32[384]{0:T(512)S(1)} %add.502, f32[384]{0:T(512)S(1)} %add.508, ...), channel_id=1, replica_groups=mesh['section'=2,'dp'=8,'mp'=2] {'section','dp','mp'}, use_global_device_ids=true, to_apply=%region_250.251 | all-reduce | flops 2688 | bytes 21504 | tf_op jit(solution)/shard_map/psum | solution.py:319
  1558.5 49.5 %reduce-scatter.105.cloned.1.call-done = f32[24,768]{1,0:T(8,128)} async-done(((f32[384,768]{1,0:T(8,128)}), f32[24,768]{1,0:T(8,128)}) %reduce-scatter.105.cloned.1.call-update) | async-done | bytes 73744 | tf_op jit(solution)/shard_map/reduce_scatter | solution.py:312
  1608.1 61.3 %reduce-scatter.107.cloned.1.call-done = f32[768,24]{0,1:T(8,128)} async-done(((f32[768,384]{0,1:T(8,128)}), f32[768,24]{0,1:T(8,128)}) %reduce-scatter.107.cloned.1.call-update) | async-done | bytes 73744 | tf_op jit(solution)/shard_map/reduce_scatter | solution.py:313
  1669.4 58.8 %reduce-scatter.133.cloned.1.call-done = f32[24,192]{1,0:T(8,128)} async-done(((f32[384,192]{1,0:T(8,128)}), f32[24,192]{1,0:T(8,128)}) %reduce-scatter.133.cloned.1.call-update) | async-done | bytes 18448
  1728.1 61.9 %reduce-scatter.135.cloned.1.call-done = f32[784,24]{0,1:T(8,128)} async-done(((f32[784,384]{0,1:T(8,128)}), f32[784,24]{0,1:T(8,128)}) %reduce-scatter.135.cloned.1.call-update) | async-done | bytes 75280
  1790.0 136.9 %all-reduce.6.cloned.1.call-done = f32[768,384]{1,0:T(8,128)} async-done(((f32[768,384]{1,0:T(8,128)}), f32[768,384]{1,0:T(8,128)}) %all-reduce.6.cloned.1.call-update) | async-done | bytes 1179664 | tf_op jit(solution)/shard_map/psum | solution.py:319
  1926.9 61.1 %reduce-scatter.95.cloned.1.call-done = f32[384,48]{0,1:T(8,128)} async-done(((f32[384,768]{0,1:T(8,128)}), f32[384,48]{0,1:T(8,128)}) %reduce-scatter.95.cloned.1.call-update) | async-done | bytes 73744 | tf_op jit(solution)/shard_map/reduce_scatter | solution.py:307
  1988.0 71.8 %reduce-scatter.93.cloned.1.call-done = f32[48,3,384]{2,0,1:T(8,128)} async-done(((f32[768,3,384]{2,0,1:T(8,128)}), f32[48,3,384]{2,0,1:T(8,128)}) %reduce-scatter.93.cloned.1.call-update) | async-done | bytes 221200 | tf_op jit(solution)/shard_map/reduce_scatter | solution.py:306
  2059.9 78.7 %reduce-scatter.99.cloned.1.call-done = f32[1536,48]{0,1:T(8,128)} async-done(((f32[1536,768]{0,1:T(8,128)}), f32[1536,48]{0,1:T(8,128)}) %reduce-scatter.99.cloned.1.call-update) | async-done | bytes 294928 | tf_op jit(solution)/shard_map/reduce_scatter | solution.py:309
  2138.5 79.4 %reduce-scatter.97.cloned.1.call-done = f32[48,1536]{1,0:T(8,128)} async-done(((f32[768,1536]{1,0:T(8,128)}), f32[48,1536]{1,0:T(8,128)}) %reduce-scatter.97.cloned.1.call-update) | async-done | bytes 294928 | tf_op jit(solution)/shard_map/reduce_scatter | solution.py:308
  (909 shorter events, 851.5 us)
Async XLA Ops:
  7.2 43.6 %reduce-scatter.75.cloned.1.call-start = ((), (), s32[]{:S(2)}) async-start(), calls=%async_computation.48 | async-start | bytes 1179648 | tf_op jit(solution)/shard_map/reduce_scatter | solution.py:44
  22.8 120.9 %copy-start.154 = (pred[256]{0:T(512)(128)(4,1)}, pred[256]{0:T(512)(128)(4,1)S(1)}, u32[]{:S(2)}) copy-start(pred[256]{0:T(512)(128)(4,1)S(1)} %iota_compare_fusion.1) | copy-start | bytes 772
  26.0 45.2 %reduce-scatter.85.cloned.1.call-start = ((), (), s32[]{:S(2)}) async-start(), calls=%async_computation.56 | async-start | bytes 1179648 | tf_op jit(solution)/shard_map/reduce_scatter | solution.py:44
  34.5 109.3 %copy-start.156 = (pred[256]{0:T(512)(128)(4,1)}, pred[256]{0:T(512)(128)(4,1)S(1)}, u32[]{:S(2)}) copy-start(pred[256]{0:T(512)(128)(4,1)S(1)} %iota_compare_fusion) | copy-start | bytes 772
  36.8 54.1 %reduce-scatter.65.cloned.1.call-start = ((), (), s32[]{:S(2)}) async-start(), calls=%async_computation.36 | async-start | bytes 1179648 | tf_op jit(solution)/shard_map/reduce_scatter | solution.py:44
  38.0 72.6 %reduce-scatter.69.cloned.1.call-start = ((), (), s32[]{:S(2)}) async-start(), calls=%async_computation.40 | async-start | bytes 1179648 | tf_op jit(solution)/shard_map/reduce_scatter | solution.py:44
  38.2 72.4 %copy-start.14 = (bf16[2,1,128,768]{3,2,1,0:T(8,128)(2,1)S(1)}, bf16[2,1,128,768]{3,2,1,0:T(8,128)(2,1)}, u32[]{:S(2)}) copy-start(bf16[2,1,128,768]{3,2,1,0:T(8,128)(2,1)} %param.199) | copy-start | bytes 1179652
  39.2 113.0 %reduce-scatter.71.cloned.1.call-start = ((), (), s32[]{:S(2)}) async-start(), calls=%async_computation.41 | async-start | bytes 1179648 | tf_op jit(solution)/shard_map/reduce_scatter | solution.py:44
  39.2 75.0 %copy-start.121 = (f32[768]{0:T(1024)S(1)}, f32[768]{0:T(1024)}, u32[]{:S(2)}) copy-start(f32[768]{0:T(1024)} %param.207) | copy-start | bytes 9220
  129.5 42.9 %reduce-scatter.67.cloned.1.call-start = ((), (), s32[]{:S(2)}) async-start(), calls=%async_computation.37 | async-start | bytes 1179648 | tf_op jit(solution)/shard_map/reduce_scatter | solution.py:44
  143.2 75.8 %all-gather.11.cloned.1.call-start = ((), (), s32[]{:S(2)}) async-start(), calls=%async_computation.38 | async-start | bytes 1806336 | tf_op jit(solution)/shard_map/all_gather | solution.py:40
  143.8 39.4 %copy-start.134 = (f32[784]{0:T(1024)}, f32[784]{0:T(1024)S(1)}, u32[]{:S(2)}) copy-start(f32[784]{0:T(1024)S(1)} %get-tuple-element.2231) | copy-start | bytes 9412
  143.8 39.4 %copy-start.136 = (f32[784]{0:T(1024)}, f32[784]{0:T(1024)S(1)}, u32[]{:S(2)}) copy-start(f32[784]{0:T(1024)S(1)} %get-tuple-element.2230) | copy-start | bytes 9412
  144.9 37.2 %copy-start.79 = (bf16[784,256]{1,0:T(8,128)(2,1)}, bf16[784,256]{1,0:T(8,128)(2,1)S(1)}, u32[]{:S(2)}) copy-start(bf16[784,256]{1,0:T(8,128)(2,1)S(1)} %get-tuple-element.2221) | copy-start | bytes 1204228
  185.8 7.5 collective-permute-start
  196.2 120.1 %reduce-scatter.121.cloned.1.call-start = ((), (), s32[]{:S(2)}) async-start(), calls=%async_computation.75 | async-start | bytes 3612672 | tf_op jit(solution)/shard_map/reduce_scatter | solution.py:44
  222.7 55.4 %copy-start.66 = (bf16[192,384]{1,0:T(8,128)(2,1)S(1)}, bf16[192,384]{1,0:T(8,128)(2,1)}, u32[]{:S(2)}) copy-start(bf16[192,384]{1,0:T(8,128)(2,1)} %param.212) | copy-start | bytes 442372
  281.4 60.2 %all-gather.21.cloned.1.call-start = ((), (), s32[]{:S(2)}) async-start(), calls=%async_computation.45 | async-start | bytes 1806336 | tf_op jit(solution)/shard_map/all_gather | solution.py:40
  283.9 82.2 %all-gather.19.cloned.1.call-start = ((), (), s32[]{:S(2)}) async-start(), calls=%async_computation.44 | async-start | bytes 1806336 | tf_op jit(solution)/shard_map/all_gather | solution.py:40
  319.3 106.7 %reduce-scatter.123.cloned.1.call-start = ((), (), s32[]{:S(2)}) async-start(), calls=%async_computation.76 | async-start | bytes 3612672 | tf_op jit(solution)/shard_map/reduce_scatter | solution.py:44
  391.2 63.3 %all-gather.23.cloned.1.call-start = ((), (), s32[]{:S(2)}) async-start(), calls=%async_computation.46 | async-start | bytes 1806336 | tf_op jit(solution)/shard_map/all_gather | solution.py:40
  431.3 185.2 %reduce-scatter.125.cloned.1.call-start = ((), (), s32[]{:S(2)}) async-start(), calls=%async_computation.77 | async-start | bytes 3612672 | tf_op jit(solution)/shard_map/reduce_scatter | solution.py:44
  554.9 90.1 %reduce-scatter.109.cloned.1.call-start = ((), (), s32[]{:S(2)}) async-start(), calls=%async_computation.69 | async-start | bytes 3612672 | tf_op jit(solution)/shard_map/reduce_scatter | solution.py:44
  557.9 49.0 %copy-start.67 = (bf16[192,384]{1,0:T(8,128)(2,1)S(1)}, bf16[192,384]{1,0:T(8,128)(2,1)}, u32[]{:S(2)}) copy-start(bf16[192,384]{1,0:T(8,128)(2,1)} %param.212) | copy-start | bytes 442372
  610.2 62.6 %all-gather.15.cloned.1.call-start = ((), (), s32[]{:S(2)}) async-start(), calls=%async_computation.42 | async-start | bytes 1806336 | tf_op jit(solution)/shard_map/all_gather | solution.py:40
  610.2 5.1 collective-permute-start.1
  619.1 53.6 %copy-start.176 = (bf16[384,3,192]{0,2,1:T(8,128)(2,1)S(1)}, bf16[384,3,192]{0,2,1:T(8,128)(2,1)}, u32[]{:S(2)}) copy-start(bf16[384,3,192]{0,2,1:T(8,128)(2,1)} %param.211) | copy-start | bytes 1327108
  649.5 120.5 %reduce-scatter.127.cloned.1.call-start = ((), (), s32[]{:S(2)}) async-start(), calls=%async_computation.78 | async-start | bytes 3612672 | tf_op jit(solution)/shard_map/reduce_scatter | solution.py:44
  676.7 55.1 %copy-start.68 = (bf16[192,384]{1,0:T(8,128)(2,1)S(1)}, bf16[192,384]{1,0:T(8,128)(2,1)}, u32[]{:S(2)}) copy-start(bf16[192,384]{1,0:T(8,128)(2,1)} %param.212) | copy-start | bytes 442372
  735.1 59.4 %all-gather.27.cloned.1.call-start = ((), (), s32[]{:S(2)}) async-start(), calls=%async_computation.53 | async-start | bytes 1806336 | tf_op jit(solution)/shard_map/all_gather | solution.py:40
  735.8 84.0 %all-gather.25.cloned.1.call-start = ((), (), s32[]{:S(2)}) async-start(), calls=%async_computation.52 | async-start | bytes 1806336 | tf_op jit(solution)/shard_map/all_gather | solution.py:40
  773.0 106.6 %reduce-scatter.129.cloned.1.call-start = ((), (), s32[]{:S(2)}) async-start(), calls=%async_computation.79 | async-start | bytes 3612672 | tf_op jit(solution)/shard_map/reduce_scatter | solution.py:44
  844.8 64.6 %all-gather.29.cloned.1.call-start = ((), (), s32[]{:S(2)}) async-start(), calls=%async_computation.54 | async-start | bytes 1806336 | tf_op jit(solution)/shard_map/all_gather | solution.py:40
  886.2 181.4 %reduce-scatter.131.cloned.1.call-start = ((), (), s32[]{:S(2)}) async-start(), calls=%async_computation.80 | async-start | bytes 3612672 | tf_op jit(solution)/shard_map/reduce_scatter | solution.py:44
  1009.9 90.0 %reduce-scatter.115.cloned.1.call-start = ((), (), s32[]{:S(2)}) async-start(), calls=%async_computation.72 | async-start | bytes 3612672 | tf_op jit(solution)/shard_map/reduce_scatter | solution.py:44
  1012.7 49.1 %copy-start.69 = (bf16[192,384]{1,0:T(8,128)(2,1)S(1)}, bf16[192,384]{1,0:T(8,128)(2,1)}, u32[]{:S(2)}) copy-start(bf16[192,384]{1,0:T(8,128)(2,1)} %param.212) | copy-start | bytes 442372
  1065.0 63.3 %reduce-scatter.83.cloned.1.call-start = ((), (), s32[]{:S(2)}) async-start(), calls=%async_computation.55 | async-start | bytes 589824 | tf_op jit(solution)/shard_map/reduce_scatter | solution.py:283
  1065.0 41.2 %collective-permute-start.2 = (f32[784,384]{1,0:T(8,128)}, f32[784,384]{1,0:T(8,128)}, u32[]{:S(2)}, u32[]{:S(2)}) collective-permute-start(f32[784,384]{1,0:T(8,128)} %get-tuple-element.2195), channel_id=1, source_target_pairs={{16,0},{17,1},{18,2},{19,3},{20,4},{21,5},{22,6},{23,7},{24,8},{25... | collective-permute-start | bytes 3612680 | tf_op jit(solution)/shard_map/ppermute | solution.py:20
  1103.6 5.1 collective-permute-start.3
  1111.6 34.1 %reduce-scatter.73.cloned.1.call-start = ((), (), s32[]{:S(2)}) async-start(), calls=%async_computation.47 | async-start | bytes 589824 | tf_op jit(solution)/shard_map/reduce_scatter | solution.py:283
  1119.2 56.7 %reduce-scatter.87.cloned.1.call-start = ((), (), s32[]{:S(2)}) async-start(), calls=%async_computation.57 | async-start | bytes 1179648 | tf_op jit(solution)/shard_map/reduce_scatter | solution.py:44
  1141.6 58.6 %all-gather.13.cloned.1.call-start = ((), (), s32[]{:S(2)}) async-start(), calls=%async_computation.39 | async-start | bytes 1806336 | tf_op jit(solution)/shard_map/all_gather | solution.py:40
  1142.2 82.3 %reduce-scatter.77.cloned.1.call-start = ((), (), s32[]{:S(2)}) async-start(), calls=%async_computation.49 | async-start | bytes 1179648 | tf_op jit(solution)/shard_map/reduce_scatter | solution.py:44
  1193.5 46.6 %reduce-scatter.103.cloned.1.call-start = ((), (), s32[]{:S(2)}) async-start(), calls=%async_computation.65 | async-start | bytes 1179648 | tf_op jit(solution)/shard_map/reduce_scatter | solution.py:44
  1194.6 65.9 %reduce-scatter.101.cloned.1.call-start = ((), (), s32[]{:S(2)}) async-start(), calls=%async_computation.64 | async-start | bytes 1179648 | tf_op jit(solution)/shard_map/reduce_scatter | solution.py:44
  1195.9 89.5 %all-gather.17.cloned.1.call-start = ((), (), s32[]{:S(2)}) async-start(), calls=%async_computation.43 | async-start | bytes 1806336 | tf_op jit(solution)/shard_map/all_gather | solution.py:40
  1206.6 127.2 %reduce-scatter.111.cloned.1.call-start = ((), (), s32[]{:S(2)}) async-start(), calls=%async_computation.70 | async-start | bytes 3612672 | tf_op jit(solution)/shard_map/reduce_scatter | solution.py:44
  1223.8 122.0 %reduce-scatter.89.cloned.1.call-start = ((), (), s32[]{:S(2)}) async-start(), calls=%async_computation.58 | async-start | bytes 1179648 | tf_op jit(solution)/shard_map/reduce_scatter | solution.py:44
  1274.8 90.6 %reduce-scatter.79.cloned.1.call-start = ((), (), s32[]{:S(2)}) async-start(), calls=%async_computation.50 | async-start | bytes 1179648 | tf_op jit(solution)/shard_map/reduce_scatter | solution.py:44
  1304.6 98.4 %reduce-scatter.117.cloned.1.call-start = ((), (), s32[]{:S(2)}) async-start(), calls=%async_computation.73 | async-start | bytes 3612672 | tf_op jit(solution)/shard_map/reduce_scatter | solution.py:44
  1321.8 177.9 %all-reduce.8.cloned.1.call-start = ((), (), s32[]{:S(2)}) async-start(), calls=%async_computation.82 | async-start | bytes 3145728
  1333.8 178.6 %reduce-scatter.113.cloned.1.call-start = ((), (), s32[]{:S(2)}) async-start(), calls=%async_computation.71 | async-start | bytes 2064384
  1339.3 214.3 %reduce-scatter.81.cloned.1.call-start = ((), (), s32[]{:S(2)}) async-start(), calls=%async_computation.51 | async-start | bytes 589824 | tf_op jit(solution)/shard_map/reduce_scatter | solution.py:296
  1370.6 183.1 %reduce-scatter.91.cloned.1.call-start = ((), (), s32[]{:S(2)}) async-start(), calls=%async_computation.59 | async-start | bytes 589824 | tf_op jit(solution)/shard_map/reduce_scatter | solution.py:296
  1372.6 182.8 %reduce-scatter.119.cloned.1.call-start = ((), (), s32[]{:S(2)}) async-start(), calls=%async_computation.74 | async-start | bytes 2064384
  1406.0 202.1 %reduce-scatter.105.cloned.1.call-start = ((), (), s32[]{:S(2)}) async-start(), calls=%async_computation.67 | async-start | bytes 1253376 | tf_op jit(solution)/shard_map/reduce_scatter | solution.py:312
  1413.7 255.6 %reduce-scatter.107.cloned.1.call-start = ((), (), s32[]{:S(2)}) async-start(), calls=%async_computation.68 | async-start | bytes 1253376 | tf_op jit(solution)/shard_map/reduce_scatter | solution.py:313
  1421.5 306.7 %reduce-scatter.133.cloned.1.call-start = ((), (), s32[]{:S(2)}) async-start(), calls=%async_computation.81 | async-start | bytes 417792
  1426.1 363.9 %reduce-scatter.135.cloned.1.call-start = ((), (), s32[]{:S(2)}) async-start(), calls=%async_computation.83 | async-start | bytes 1462272
  1428.1 498.8 %all-reduce.6.cloned.1.call-start = ((), (), s32[]{:S(2)}) async-start(), calls=%async_computation.66 | async-start | bytes 2359296 | tf_op jit(solution)/shard_map/psum | solution.py:319
  1430.3 557.7 %reduce-scatter.95.cloned.1.call-start = ((), (), s32[]{:S(2)}) async-start(), calls=%async_computation.61 | async-start | bytes 1253376 | tf_op jit(solution)/shard_map/reduce_scatter | solution.py:307
  1431.7 628.1 %reduce-scatter.93.cloned.1.call-start = ((), (), s32[]{:S(2)}) async-start(), calls=%async_computation.60 | async-start | bytes 3760128 | tf_op jit(solution)/shard_map/reduce_scatter | solution.py:306
  1441.2 697.4 %reduce-scatter.99.cloned.1.call-start = ((), (), s32[]{:S(2)}) async-start(), calls=%async_computation.63 | async-start | bytes 5013504 | tf_op jit(solution)/shard_map/reduce_scatter | solution.py:309
  1455.2 762.7 %reduce-scatter.97.cloned.1.call-start = ((), (), s32[]{:S(2)}) async-start(), calls=%async_computation.62 | async-start | bytes 5013504 | tf_op jit(solution)/shard_map/reduce_scatter | solution.py:308
  (180 other events, 1642.8 us)
Sparse Core Ops, SparseCore 0:
  26.1 24.5 reduce-scatter.74
  53.7 17.4 reduce-scatter.84
  73.5 17.4 reduce-scatter.64
  93.1 17.4 reduce-scatter.68
  129.6 22.5 reduce-scatter.70
  155.0 17.4 reduce-scatter.66
  196.3 22.5 all-gather.10
  281.5 34.7 reduce-scatter.120
  318.5 23.0 all-gather.20
  343.0 23.0 all-gather.18
  391.3 34.7 reduce-scatter.122
  431.4 23.0 all-gather.22
  555.0 34.7 reduce-scatter.124
  610.2 34.7 reduce-scatter.108
  649.6 23.0 all-gather.14
  735.3 34.7 reduce-scatter.126
  771.5 23.0 all-gather.26
  796.6 23.0 all-gather.24
  844.9 34.7 reduce-scatter.128
  886.3 23.0 all-gather.28
  1010.0 34.7 reduce-scatter.130
  1065.1 34.8 reduce-scatter.114
  1111.7 16.4 reduce-scatter.82
  1131.1 14.5 reduce-scatter.72
  1148.5 27.2 reduce-scatter.86
  1177.3 22.8 all-gather.12
  1202.9 17.4 reduce-scatter.76
  1222.7 17.4 reduce-scatter.102
  1243.0 17.4 reduce-scatter.100
  1261.9 23.4 all-gather.16
  1287.7 38.4 reduce-scatter.110
  1328.5 17.2 reduce-scatter.88
  1347.9 17.4 reduce-scatter.78
  1367.7 35.2 reduce-scatter.116
  1406.4 93.2 all-reduce.7
  1501.8 10.5 reduce-scatter.112
  1514.6 8.9 reduce-scatter.80
  1526.4 8.9 reduce-scatter.90
  1538.2 9.9 reduce-scatter.118
  1552.4 55.6 reduce-scatter.104
  1612.3 57.0 reduce-scatter.106
  1673.5 54.6 reduce-scatter.132
  1732.7 57.1 reduce-scatter.134
  1796.3 130.5 all-reduce.5
  1931.5 56.4 reduce-scatter.94
  1992.3 67.4 reduce-scatter.92
  2064.1 74.3 reduce-scatter.98
  2143.3 74.5 reduce-scatter.96
where the time goes:
time: 2240 us; the launch traced here: 2230 us
  waiting for transfers between devices  1310 us (58%)
  matrix products  349 us (16%)
  other arithmetic  286 us (13%)
  local copies, waits for them, and re-layouts  133 us (6%)
  blocking collectives  114 us (5%)
    reduce_scatter x22, waiting for transfers between devices, narrow(): lax.psum_scatter(only(active, lambda: contract(operand, weight, 1, along)...  402 us
    all_gather x10, waiting for transfers between devices, widen(): return lax.all_gather(shard_rows, 'mp', axis=0, tiled=True)  190 us
    unnamed x53, waiting for transfers between devices  162 us
    psum x1, waiting for transfers between devices, per_device(): lax.psum((enc_gains[0], enc_gains[1], dec_gains[0], dec_gains[1], other_g...  137 us
    dot_general x8, matrix products, one_block(): jnp.einsum('hqk,khd->qhd', weights, values, preferred_element_type=FLOAT)  94.1 us
    reduce_scatter x1, waiting for transfers between devices, per_device(): lax.psum_scatter(enc_weights[2], ('section', 'dp'), scatter_dimension=0,...  79.4 us
    reduce_scatter x1, waiting for transfers between devices, per_device(): lax.psum_scatter(enc_weights[3], ('section', 'dp'), scatter_dimension=1,...  78.7 us
    convert_element_type x8, other arithmetic, block_forward(): hidden = jax.nn.gelu(before, approximate=False).astype(BRAIN)  71.8 us
  transfers between devices with their start and end apart: 52, of which 44 were waited for; matrix products, arithmetic and copies ran while one was open for 14% of the time, Pallas kernels for 0%

commit v1 on v0

v1 whole, which is shorter than its diff:
```python
import functools

import jax
import jax.numpy as jnp
from jax import lax
from jax.experimental import pallas as pl
from jax.experimental.pallas import tpu as pltpu
from jax.sharding import PartitionSpec as P

HEAD = 64
LONGEST = 157
EPS = 1e-06
NEG = -1e30
F32 = jnp.float32
B16 = jnp.bfloat16
MESH = pl.DeviceIdType.MESH
VMEM = pltpu.VMEM
LIMIT = 56 * 1024 * 1024


def place_of():
    return lax.axis_index("section"), lax.axis_index("dp"), lax.axis_index("mp")


def greet(partners):
    barrier = pltpu.get_barrier_semaphore()
    for partner in partners:
        pl.semaphore_signal(barrier, inc=1, device_id=partner, device_id_type=MESH)
    pl.semaphore_wait(barrier, len(partners))


def send(src, dst, send_sem, recv_sem, partner):
    return pltpu.make_async_remote_copy(
        src_ref=src,
        dst_ref=dst,
        send_sem=send_sem,
        recv_sem=recv_sem,
        device_id=partner,
        device_id_type=MESH,
    )


def remote_params(ident):
    return pltpu.CompilerParams(
        collective_id=ident, has_side_effects=True, vmem_limit_bytes=LIMIT
    )


def swap_kernel(kind, count, *refs):
    ins, outs, (send_sem, recv_sem) = refs[:count], refs[count : 2 * count], refs[2 * count :]
    s, d, m = place_of()
    partner = (1 - s, d, m) if kind == "core" else (s, d, 1 - m)
    greet([partner])
    copies = [
        send(ins[i], outs[i], send_sem.at[i], recv_sem.at[i], partner) for i in range(count)
    ]
    for copy in copies:
        copy.start()
    for copy in copies:
        copy.wait()


def swap(arrays, kind, ident):
    count = len(arrays)
    return pl.pallas_call(
        functools.partial(swap_kernel, kind, count),
        out_shape=[jax.ShapeDtypeStruct(a.shape, a.dtype) for a in arrays],
        in_specs=[pl.BlockSpec(memory_space=pl.ANY)] * count,
        out_specs=[pl.BlockSpec(memory_space=pl.ANY)] * count,
        scratch_shapes=[pltpu.SemaphoreType.DMA((count,)), pltpu.SemaphoreType.DMA((count,))],
        compiler_params=remote_params(ident),
        name=f"swap_{kind}_{ident}",
    )(*arrays)


def route_kernel(x_ref, out_ref, send_sem, recv_sem, local_sem):
    s, d, m = place_of()
    greet([(1 - s, d, m), (s, d, 1 - m), (1 - s, d, 1 - m)])
    stays = s == m

    @pl.when(stays)
    def _():
        mine = pltpu.make_async_copy(x_ref.at[s], out_ref.at[m], local_sem)
        mine.start()
        out = send(x_ref.at[1 - s], out_ref.at[m], send_sem.at[0], recv_sem.at[m], (1 - s, d, m))
        out.start()
        mine.wait()
        out.wait_send()

    @pl.when(jnp.logical_not(stays))
    def _():
        near = send(x_ref.at[s], out_ref.at[m], send_sem.at[0], recv_sem.at[m], (s, d, 1 - m))
        far = send(
            x_ref.at[1 - s], out_ref.at[m], send_sem.at[1], recv_sem.at[m], (1 - s, d, 1 - m)
        )
        near.start()
        far.start()
        near.wait_send()
        far.wait_send()

    pltpu.make_async_copy(out_ref.at[1 - m], out_ref.at[1 - m], recv_sem.at[1 - m]).wait()

    @pl.when(jnp.logical_not(stays))
    def _():
        pltpu.make_async_copy(out_ref.at[m], out_ref.at[m], recv_sem.at[m]).wait()


def route(x, ident):
    return pl.pallas_call(
        route_kernel,
        out_shape=jax.ShapeDtypeStruct(x.shape, x.dtype),
        in_specs=[pl.BlockSpec(memory_space=pl.ANY)],
        out_specs=pl.BlockSpec(memory_space=pl.ANY),
        scratch_shapes=[
            pltpu.SemaphoreType.DMA((2,)),
            pltpu.SemaphoreType.DMA((2,)),
            pltpu.SemaphoreType.DMA,
        ],
        compiler_params=remote_params(ident),
        name=f"route_{ident}",
    )(x)


def scatter_kernel(n, across, g_ref, out_ref, near, work, far, over, sems):
    near_send, near_recv, far_send, far_recv, over_send, over_recv = sems
    s, d, m = place_of()
    sibling, facing = (1 - s, d, m), (s, d, 1 - m)
    greet([sibling] + [facing] * across + [(s, lax.rem(d + k, n), m) for k in range(1, n)])
    order = [*range(1, n), 0]
    sides = 1 + across
    first = {}
    for side in reversed(range(sides)):
        for k in order:
            to = lax.rem(d + k, n)
            first[side, k] = send(
                g_ref.at[side, (1 - s) * n + to],
                near.at[side, to],
                near_send.at[side, k],
                near_recv.at[side, k],
                sibling,
            )
            first[side, k].start()

    def summed(side, k):
        to = lax.rem(d + k, n)
        first[side, k].wait()
        return to, g_ref[side, s * n + to].astype(F32) + near[side, to].astype(F32)

    second = {}
    if across:
        for k in order:
            to, part = summed(1, k)
            work[1, to] = part.astype(B16)
            second[k] = send(work.at[1, to], over.at[to], over_send.at[k], over_recv.at[k], facing)
            second[k].start()
    third = []
    for k in order:
        to, part = summed(0, k)
        if across:
            second[k].wait()
            part = part + over[to].astype(F32)
        if k:
            work[0, to] = part.astype(B16)
            copy = send(work.at[0, to], far.at[d], far_send.at[k], far_recv.at[k], (s, to, m))
            copy.start()
            third.append((k, copy))
    for k, copy in third:
        copy.wait()
        part = part + far[lax.rem(d + n - k, n)].astype(F32)
    out_ref[...] = part


def scatter(g, ident):
    sides, owners, rows, cols = g.shape
    n = owners // 2
    across = sides - 1
    kernel = functools.partial(scatter_kernel, n, across)

    def body(g_ref, out_ref, near, work, far, over, *sems):
        kernel(g_ref, out_ref, near, work, far, over, sems)

    pieces = (n, rows, cols)
    return pl.pallas_call(
        body,
        out_shape=jax.ShapeDtypeStruct((rows, cols), F32),
        in_specs=[pl.BlockSpec(memory_space=VMEM)],
        out_specs=pl.BlockSpec(memory_space=VMEM),
        scratch_shapes=[
            VMEM((sides,) + pieces, B16),
            VMEM((sides,) + pieces, B16),
            VMEM(pieces, B16),
            VMEM(pieces if across else (8, 128), B16),
            pltpu.SemaphoreType.DMA((sides, n)),
            pltpu.SemaphoreType.DMA((sides, n)),
            pltpu.SemaphoreType.DMA((n,)),
            pltpu.SemaphoreType.DMA((n,)),
            pltpu.SemaphoreType.DMA((n,)),
            pltpu.SemaphoreType.DMA((n,)),
        ],
        compiler_params=remote_params(ident),
        name=f"scatter_{ident}",
    )(g)


def gather_kernel(n, x_ref, out_ref, local_sem, send_sem, recv_sem):
    s, d, m = place_of()
    steps = [(a, k, b) for k in range(n) for a in range(2) for b in range(2) if a or k or b]

    def partner(step):
        a, k, b = step
        return (lax.rem(s + a, 2), lax.rem(d + k, n), lax.rem(m + b, 2))

    greet([partner(step) for step in steps])
    slot = (s * n + d) * 2 + m
    mine = pltpu.make_async_copy(x_ref, out_ref.at[slot], local_sem)
    mine.start()
    copies = [
        send(x_ref, out_ref.at[slot], send_sem.at[i], recv_sem.at[i], partner(step))
        for i, step in enumerate(steps)
    ]
    for copy in copies:
        copy.start()
    mine.wait()
    for copy in copies:
        copy.wait()


def gather(x, n, ident):
    count = 4 * n
    return pl.pallas_call(
        functools.partial(gather_kernel, n),
        out_shape=jax.ShapeDtypeStruct((count,) + x.shape, x.dtype),
        in_specs=[pl.BlockSpec(memory_space=VMEM)],
        out_specs=pl.BlockSpec(memory_space=VMEM),
        scratch_shapes=[
            pltpu.SemaphoreType.DMA,
            pltpu.SemaphoreType.DMA((count - 1,)),
            pltpu.SemaphoreType.DMA((count - 1,)),
        ],
        compiler_params=remote_params(ident),
        name=f"gather_{ident}",
    )(x)


def dot_nt(a, b):
    return lax.dot_general(a, b, (((1,), (1,)), ((), ())), preferred_element_type=F32)


def dot_nn(a, b):
    return lax.dot_general(a, b, (((1,), (0,)), ((), ())), preferred_element_type=F32)


def dot_tn(a, b):
    return lax.dot_general(a, b, (((0,), (0,)), ((), ())), preferred_element_type=F32)


def chunks_of(length, most=256):
    units = length // 16
    count = -(-length // most)
    cuts = [16 * (units * i // count) for i in range(count)] + [length]
    return [(a, b - a) for a, b in zip(cuts, cuts[1:])]


def head_masks():
    lanes = lax.broadcasted_iota(jnp.int32, (1, 2 * HEAD), 1)
    return (lanes < HEAD, lanes >= HEAD)


def attend_kernel(q_ref, k_ref, v_ref, o_ref, p_ref):
    masks = head_masks()
    k = k_ref[...]
    v = v_ref[...]
    for start, size in chunks_of(q_ref.shape[0], 128):
        rows = pl.ds(start, size)
        q = q_ref[rows] * jnp.asarray(HEAD**-0.5, B16)
        halves = []
        for head in range(2):
            scores = dot_nt(jnp.where(masks[head], q, 0), k)
            top = jnp.max(scores, -1, keepdims=True)
            raised = jnp.exp(scores - top)
            whole = jnp.sum(raised, -1, keepdims=True)
            p = (raised * (1.0 / whole)).astype(B16)
            p_ref[head, rows] = p
            halves.append(dot_nn(p, v))
        o_ref[rows] = jnp.where(masks[0], halves[0], halves[1]).astype(B16)


def attend(q, k, v):
    length, width = q.shape
    keys = k.shape[0]
    pairs = width // (2 * HEAD)
    return pl.pallas_call(
        attend_kernel,
        grid=(pairs,),
        out_shape=[
            jax.ShapeDtypeStruct((length, width), B16),
            jax.ShapeDtypeStruct((2 * pairs, length, keys), B16),
        ],
        in_specs=[
            pl.BlockSpec((length, 2 * HEAD), lambda i: (0, i)),
            pl.BlockSpec((keys, 2 * HEAD), lambda i: (0, i)),
            pl.BlockSpec((keys, 2 * HEAD), lambda i: (0, i)),
        ],
        out_specs=[
            pl.BlockSpec((length, 2 * HEAD), lambda i: (0, i)),
            pl.BlockSpec((2, length, keys), lambda i: (i, 0, 0)),
        ],
        compiler_params=pltpu.CompilerParams(vmem_limit_bytes=LIMIT),
        name="attend",
    )(q, k, v)


def attend_back_kernel(q_ref, k_ref, v_ref, o_ref, do_ref, p_ref, dq_ref, dk_ref, dv_ref, dk_t, dv_t):
    masks = head_masks()
    k = k_ref[...]
    v = v_ref[...]
    scale = HEAD**-0.5
    for index, (start, size) in enumerate(chunks_of(q_ref.shape[0], 256)):
        rows = pl.ds(start, size)
        q = q_ref[rows]
        do = do_ref[rows]
        both = do.astype(F32) * o_ref[rows].astype(F32)
        dq = []
        for head in range(2):
            do_head = jnp.where(masks[head], do, 0)
            delta = jnp.sum(jnp.where(masks[head], both, 0.0), -1, keepdims=True)
            p = p_ref[head, rows]
            dp = dot_nt(do_head, v)
            ds = (p.astype(F32) * (dp - delta)).astype(B16)
            dq.append(dot_nn(ds, k))
            feats = pl.ds(head * HEAD, HEAD)
            dv_part = dot_tn(do[:, head * HEAD : (head + 1) * HEAD], p)
            dk_part = dot_tn(q[:, head * HEAD : (head + 1) * HEAD], ds)
            if index:
                dv_part = dv_part + dv_t[feats]
                dk_part = dk_part + dk_t[feats]
            dv_t[feats] = dv_part
            dk_t[feats] = dk_part
        dq_ref[rows] = (jnp.where(masks[0], dq[0], dq[1]) * scale).astype(B16)
    dk_ref[...] = (jnp.transpose(dk_t[...]) * scale).astype(dk_ref.dtype)
    dv_ref[...] = jnp.transpose(dv_t[...]).astype(dv_ref.dtype)


def attend_back(q, k, v, o, do, p):
    length, width = q.shape
    keys = k.shape[0]
    pairs = width // (2 * HEAD)
    short = pl.BlockSpec((length, 2 * HEAD), lambda i: (0, i))
    long = pl.BlockSpec((keys, 2 * HEAD), lambda i: (0, i))
    return pl.pallas_call(
        attend_back_kernel,
        grid=(pairs,),
        out_shape=[
            jax.ShapeDtypeStruct((length, width), B16),
            jax.ShapeDtypeStruct((keys, width), F32),
            jax.ShapeDtypeStruct((keys, width), F32),
        ],
        in_specs=[
            short,
            long,
            long,
            short,
            short,
            pl.BlockSpec((2, length, keys), lambda i: (i, 0, 0)),
        ],
        out_specs=[short, long, long],
        scratch_shapes=[VMEM((2 * HEAD, keys), F32), VMEM((2 * HEAD, keys), F32)],
        compiler_params=pltpu.CompilerParams(vmem_limit_bytes=LIMIT),
        name="attend_back",
    )(q, k, v, o, do, p)


def normed(z, gain):
    centre = z - jnp.mean(z, -1, keepdims=True)
    inverse = lax.rsqrt(jnp.mean(centre * centre, -1, keepdims=True) + EPS)
    unit = centre * inverse
    return unit, inverse, (unit * gain).astype(B16)


def norm_back(grad, unit, inverse, gain):
    scaled = grad * gain
    return inverse * (
        scaled
        - jnp.mean(scaled, -1, keepdims=True)
        - unit * jnp.mean(scaled * unit, -1, keepdims=True)
    )


def gelu(u):
    return 0.5 * u * (1.0 + lax.erf(u * 0.5**0.5))


def gelu_slope(u):
    return 0.5 * (1.0 + lax.erf(u * 0.5**0.5)) + u * jnp.exp(-0.5 * u * u) * (
        0.5 / jnp.pi
    ) ** 0.5


def small_attend(triple, length):
    rows = triple.shape[0]
    q, k, v = (triple[:, i] for i in range(3))
    scores = jnp.einsum("qhd,khd->hqk", q, k, preferred_element_type=F32) * HEAD**-0.5
    scores = jnp.where(jnp.arange(rows)[None, None, :] < length, scores, NEG)
    p = jax.nn.softmax(scores, axis=-1)
    o = jnp.einsum("hqk,khd->qhd", p.astype(B16), v, preferred_element_type=F32)
    return p, o.reshape(rows, -1).astype(B16)


def small_attend_back(triple, p, do):
    q, k, v = (triple[:, i] for i in range(3))
    do = do.reshape(q.shape)
    dp = jnp.einsum("qhd,khd->hqk", do, v, preferred_element_type=F32)
    ds = (p * (dp - jnp.sum(p * dp, -1, keepdims=True))).astype(B16)
    scale = HEAD**-0.5
    dq = jnp.einsum("hqk,khd->qhd", ds, k, preferred_element_type=F32) * scale
    dk = jnp.einsum("hqk,qhd->khd", ds, q, preferred_element_type=F32) * scale
    dv = jnp.einsum("hqk,qhd->khd", p.astype(B16), do, preferred_element_type=F32)
    return jnp.stack([dq, dk, dv], 1).astype(B16).reshape(q.shape[0], -1)


def pack(grad, owners):
    rows, cols = grad.shape
    own = rows // owners
    fold = 1
    while own * fold % 16:
        fold *= 2
    grad = grad.astype(B16).reshape(owners, own, fold, cols // fold)
    return jnp.swapaxes(grad, 1, 2).reshape(owners, fold * own, cols // fold)


def unpack(piece, own):
    fold = piece.shape[0] // own
    return jnp.swapaxes(piece.reshape(fold, own, -1), 0, 1).reshape(own, -1)


def pick(pair, index):
    return lax.dynamic_index_in_dim(pair, index, 0, keepdims=False)


def per_device(
    tokens,
    clip_lengths,
    clip_cells,
    enc_qkv,
    enc_attn_out,
    enc_up,
    enc_down,
    enc_gain_one,
    enc_gain_two,
    bridge_weight,
    mask_token,
    position_embed,
    dec_qkv,
    dec_attn_out,
    dec_up,
    dec_down,
    dec_gain_one,
    dec_gain_two,
    cotangent,
):
    s, d, m = place_of()
    n = lax.axis_size("dp")
    owners = 2 * n
    stays = s == m
    cells_half, dec_wide = position_embed.shape
    slots = clip_cells.shape[2]
    half_slots = tokens.shape[2]
    enc_wide = tokens.shape[3]
    used = -(-LONGEST // 32) * 32

    swapped = swap(
        [
            pick(tokens[:, 0], s),
            dec_qkv.reshape(dec_wide, -1),
            dec_attn_out,
            dec_up,
            dec_down,
            pick(cotangent[:, 0], 1 - m),
            position_embed.astype(B16),
        ],
        "x",
        1,
    )
    tok_far, dqkv_far, dout_far, dup_far, ddown_far, cot_far, pos_far = swapped
    cot = jnp.where(stays, pick(cotangent[:, 0], m), cot_far)
    pos = jnp.where(stays, position_embed, pos_far.astype(F32))
    w_qkv = jnp.concatenate(
        [dec_qkv, dqkv_far.reshape(dec_qkv.shape)], 2
    ).reshape(dec_wide, -1)
    w_out = jnp.concatenate([dec_attn_out, dout_far], 0)
    w_up = jnp.concatenate([dec_up, dup_far], 1)
    w_down = jnp.concatenate([dec_down, ddown_far], 0)

    tok_near = pick(tokens[:, 0], s)
    x = jnp.concatenate(
        [jnp.where(m == 0, tok_near, tok_far), jnp.where(m == 0, tok_far, tok_near)], 0
    )[:used].astype(F32)
    length = pick(clip_lengths[:, 0], s)
    e_qkv = enc_qkv.reshape(enc_wide, -1)
    unit1, inv1, a = normed(x, enc_gain_one)
    triple = jnp.dot(a, e_qkv, preferred_element_type=F32).astype(B16)
    triple = triple.reshape(used, 3, -1, HEAD)
    ep, eo = small_attend(triple, length)
    part = jnp.dot(eo, enc_attn_out, preferred_element_type=F32)
    z2 = x + part + swap([part.astype(B16)], "x", 2)[0].astype(F32)
    unit2, inv2, b = normed(z2, enc_gain_two)
    u = jnp.dot(b, enc_up, preferred_element_type=F32)
    h = gelu(u).astype(B16)
    part = jnp.dot(h, enc_down, preferred_element_type=F32)
    enc = (z2 + part + swap([part.astype(B16)], "x", 3)[0].astype(F32)).astype(B16)
    vis = jnp.dot(enc, bridge_weight, preferred_element_type=F32).astype(B16)
    vis_far = swap([vis], "core", 4)[0]

    vis_used = jnp.where(stays, vis, vis_far)
    cell_ids = s * cells_half + jnp.arange(cells_half, dtype=jnp.int32)
    place = (pick(clip_cells[:, 0], m)[None, :used] == cell_ids[:, None]) & (
        jnp.arange(used)[None, :] < pick(clip_lengths[:, 0], m)
    )
    place = place.astype(B16)
    unseen = 1.0 - jnp.sum(place.astype(F32), 1, keepdims=True)
    filled = jnp.dot(place, vis_used, preferred_element_type=F32) + unseen * mask_token + pos
    dunit1, dinv1, da_in = normed(filled, dec_gain_one)
    dqkv = jnp.dot(da_in, w_qkv, preferred_element_type=F32).astype(B16)
    q, kv = dqkv[:, :dec_wide], dqkv[:, dec_wide:]
    kv_all = jnp.concatenate([kv, swap([kv], "core", 5)[0]], 0)
    k_all, v_all = kv_all[:, :dec_wide], kv_all[:, dec_wide:]
    do_out, dp_saved = attend(q, k_all, v_all)
    dz2 = filled + jnp.dot(do_out, w_out, preferred_element_type=F32)
    dunit2, dinv2, db_in = normed(dz2, dec_gain_two)
    du = jnp.dot(db_in, w_up, preferred_element_type=F32)
    dh = gelu(du).astype(B16)
    dec = dz2 + jnp.dot(dh, w_down, preferred_element_type=F32)

    def cut(value):
        return jnp.stack(jnp.split(value.astype(B16), 2, axis=1))

    decoded = route(cut(dec), 6)

    dy = cot.astype(F32)
    grad_h = dot_nt(cot, w_down)
    g_down = dot_tn(cot, dh)
    grad_u = (grad_h * gelu_slope(du)).astype(B16)
    g_up = dot_tn(db_in, grad_u)
    grad_b = dot_nt(grad_u, w_up)
    g_dtwo = jnp.sum(grad_b * dunit2, 0)
    grad_z2 = dy + norm_back(grad_b, dunit2, dinv2, dec_gain_two)
    grad_a = grad_z2.astype(B16)
    g_out = dot_tn(grad_a, do_out)
    grad_o = dot_nt(grad_a, w_out).astype(B16)
    grad_q, grad_k, grad_v = attend_back(q, k_all, v_all, do_out, grad_o, dp_saved)
    half = cells_half
    far_kv = jnp.concatenate([grad_k[half:], grad_v[half:]], 1).astype(B16)
    near_kv = jnp.concatenate([grad_k[:half], grad_v[:half]], 1)
    grad_kv = (near_kv + swap([far_kv], "core", 7)[0].astype(F32)).astype(B16)
    grad_qkv = jnp.concatenate([grad_q, grad_kv], 1)
    g_qkv = dot_tn(da_in, grad_qkv)
    grad_n = dot_nt(grad_qkv, w_qkv)
    g_done = jnp.sum(grad_n * dunit1, 0)
    grad_filled = grad_z2 + norm_back(grad_n, dunit1, dinv1, dec_gain_one)
    g_mask = jnp.sum(unseen * grad_filled, 0)
    position_parts = route(cut(grad_filled), 8)

    dvis = dot_tn(place, grad_filled.astype(B16)).astype(B16)
    dvis = dvis + swap([dvis], "core", 9)[0]
    dvis = jnp.where(stays, dvis, swap([dvis], "x", 10)[0])

    g_qkv = g_qkv.reshape(dec_wide, 3, 2, -1)
    g_out = g_out.reshape(dec_wide, 2, -1)
    g_up = g_up.reshape(dec_wide, 2, -1)
    g_down = g_down.reshape(dec_wide, 2, -1)
    packed = jnp.stack(
        [
            pack(
                jnp.concatenate(
                    [
                        g_qkv[:, :, side].reshape(dec_wide, -1),
                        g_out[:, side],
                        g_up[:, side],
                        g_down[:, side],
                    ],
                    1,
                ),
                owners,
            )
            for side in range(2)
        ]
    )
    own = dec_wide // owners
    dec_final = unpack(scatter(packed, 11), own)
    pos_sum = (position_parts[0].astype(F32) + position_parts[1].astype(F32))
    pos_t = jnp.transpose(pos_sum)

    grad_out = dot_nt(dvis, bridge_weight)
    dm = grad_out.astype(B16)
    enc_mine = lax.dynamic_slice_in_dim(enc, m * (enc_wide // 2), enc_wide // 2, 1)
    g_bridge = dot_tn(enc_mine, dvis)
    eg_h = dot_nt(dm, enc_down)
    eg_down = dot_tn(dm, h)
    eg_u = (eg_h * gelu_slope(u)).astype(B16)
    eg_up = dot_tn(b, eg_u)
    part = dot_nt(eg_u, enc_up)
    g_etwo = jnp.sum(part * unit2, 0)
    whole = part + swap([part.astype(B16)], "x", 12)[0].astype(F32)
    eg_z2 = grad_out + norm_back(whole, unit2, inv2, enc_gain_two)
    eg_a = eg_z2.astype(B16)
    eg_out = dot_tn(eg_a, eo)
    eg_o = dot_nt(eg_a, enc_attn_out).astype(B16)
    eg_triple = small_attend_back(triple, ep, eg_o)
    eg_qkv = dot_tn(a, eg_triple)
    part = dot_nt(eg_triple, e_qkv)
    g_eone = jnp.sum(part * unit1, 0)
    whole = part + swap([part.astype(B16)], "x", 13)[0].astype(F32)
    grad_x = eg_z2 + norm_back(whole, unit1, inv1, enc_gain_one)
    grad_x = jnp.pad(grad_x, ((0, slots - used), (0, 0)))
    grad_x = lax.dynamic_slice_in_dim(grad_x, m * half_slots, half_slots, 0)
    halves = jnp.stack(jnp.split(grad_x, 2, axis=1))
    other = swap([pick(halves, 1 - s)], "core", 14)[0]
    mine = pick(halves, s)
    tokens_grad = jnp.stack([jnp.where(s == 0, mine, other), jnp.where(s == 0, other, mine)])

    packed = pack(jnp.concatenate([eg_qkv, eg_up, eg_out, eg_down], 1), owners)
    enc_own = enc_wide // owners
    enc_final = unpack(scatter(packed[None], 15), enc_own)

    pos_rows = dec_wide // 2 // n
    pos_packed = pack(pos_t, n)
    zero = jnp.zeros_like(pos_packed)
    pos_two = jnp.concatenate(
        [jnp.where(s == 0, pos_packed, zero), jnp.where(s == 1, pos_packed, zero)], 0
    )
    pos_final = unpack(scatter(pos_two[None], 16), pos_rows)

    small = jnp.concatenate([g_eone, g_etwo, g_done, g_dtwo, g_mask])
    per = -(-small.shape[0] // owners)
    small = jnp.pad(small, (0, per * owners - small.shape[0])).reshape(owners, 1, per)
    small = jnp.pad(small, ((0, 0), (0, 0), (0, dec_wide - per)))
    bridge_own = enc_wide // 2 // owners
    rows = -(-(bridge_own + 1) // 16) * 16
    rep = jnp.concatenate(
        [
            g_bridge.reshape(owners, bridge_own, dec_wide),
            small,
            jnp.zeros((owners, rows - bridge_own - 1, dec_wide), F32),
        ],
        1,
    ).astype(B16)
    rep = scatter(rep[None], 17).astype(B16)
    everyone = gather(rep, n, 18).reshape(owners, 2, rows, dec_wide)
    bridge_grad = jnp.swapaxes(everyone[:, :, :bridge_own], 0, 1).reshape(enc_wide, dec_wide)
    small = everyone[:, 0, bridge_own, :per].astype(F32) + everyone[:, 1, bridge_own, :per].astype(F32)
    small = small.reshape(-1)
    cuts = [enc_wide, 2 * enc_wide, 2 * enc_wide + dec_wide, 2 * enc_wide + 2 * dec_wide]
    one_e, two_e, one_d, two_d, mask_grad = (
        part for part in jnp.split(small[: 2 * enc_wide + 3 * dec_wide], cuts)
    )

    enc_cols = enc_qkv.shape[2]
    sizes = [3 * enc_cols, enc_up.shape[1], enc_attn_out.shape[0]]
    e1, e2, e3, e4 = jnp.split(enc_final, [sizes[0], sizes[0] + sizes[1], sum(sizes)], 1)
    dec_cols = dec_qkv.shape[2]
    sizes = [3 * dec_cols, dec_attn_out.shape[0], dec_up.shape[1]]
    d1, d3, d2, d4 = jnp.split(dec_final, [sizes[0], sizes[0] + sizes[1], sum(sizes)], 1)
    return (
        decoded.astype(F32)[:, None],
        tokens_grad[:, None],
        e1.reshape(enc_own, 3, -1),
        e3.T,
        e2,
        e4.T,
        one_e,
        two_e,
        bridge_grad.astype(F32),
        mask_grad,
        pos_final.T,
        d1.reshape(own, 3, -1),
        d3.T,
        d2,
        d4.T,
        one_d,
        two_d,
    )


def solution(mesh):
    return jax.shard_map(
        per_device,
        mesh=mesh,
        in_specs=(
            P(None, "dp", "mp", None),
            P(None, "dp"),
            P(None, "dp", None),
            P(None, None, "mp"),
            P("mp", None),
            P(None, "mp"),
            P("mp", None),
            P(),
            P(),
            P(),
            P(),
            P("mp", None),
            P(None, None, "mp"),
            P("mp", None),
            P(None, "mp"),
            P("mp", None),
            P(),
            P(),
            P(None, "dp", "mp", None),
        ),
        out_specs=(
            P(None, "dp", "mp", "section"),
            P(None, "dp", "mp", "section"),
            P(("section", "dp"), None, "mp"),
            P("mp", ("section", "dp")),
            P(("section", "dp"), "mp"),
            P("mp", ("section", "dp")),
            P(),
            P(),
            P(),
            P(),
            P("mp", ("section", "dp")),
            P(("section", "dp"), None, "mp"),
            P("mp", ("section", "dp")),
            P(("section", "dp"), "mp"),
            P("mp", ("section", "dp")),
            P(),
            P(),
        ),
        check_vma=False,
    )
```

time: 2240 us -> 611 us (0.27)
  waiting for transfers between devices: 1310 us -> 0 us
  Pallas kernels: 0 us -> 370 us
  matrix products: 349 us -> 67.2 us
  other arithmetic: 286 us -> 50.3 us
  blocking collectives: 114 us -> 0 us
  local copies, waits for them, and re-layouts: 133 us -> 110 us
    reduce_scatter x32 -> x0, waiting for transfers between devices: 811 us -> none  [the longest x22 402 us: narrow(): lax.psum_scatter(only(active, lambda: contract(operand, weight, 1, along)...]
    pallas_call x0 -> x20, Pallas kernels: none -> 370 us  [the longest x4 154 us: scatter(): pl.pallas_call(body, out_shape=jax.ShapeDtypeStruct((rows, cols), F32), i...]
    dot_general x64 -> x34, matrix products: 343 us -> 64.7 us  [the longest x9 24.3 us: dot_nt(): lax.dot_general(a, b, (((1,), (1,)), ((), ())), preferred_element_type=F32)]
    all_gather x10 -> x0, waiting for transfers between devices: 190 us -> none  [widen(): return lax.all_gather(shard_rows, 'mp', axis=0, tiled=True)]
    unnamed x53 -> x0, waiting for transfers between devices: 162 us -> none
    psum x1 -> x0, waiting for transfers between devices: 137 us -> none  [per_device(): lax.psum((enc_gains[0], enc_gains[1], dec_gains[0], dec_gains[1], other_g...]
    convert_element_type x32 -> x6, other arithmetic: 140 us -> 6.45 us  [the longest x1 1.71 us: per_device(): grad_kv = (near_kv + swap([far_kv], 'core', 7)[0].astype(F32)).astype(B16)]
    all_gather x12 -> x0, blocking collectives: 74.1 us -> none  [the longest x10 65.9 us: widen(): return lax.all_gather(shard_rows, 'mp', axis=0, tiled=True)]
  transfers between devices with their start and end apart: 52 -> 0, of which waited for: 44 -> 0; matrix products, arithmetic and copies ran while one was open for 14% -> 0% of each run, Pallas kernels for 0% -> 0%
where the time goes in v1:
time: 611 us; the launch traced here: 600 us
  Pallas kernels  370 us (61%)
  local copies, waits for them, and re-layouts  110 us (18%)
  matrix products  67.2 us (11%)
  other arithmetic  50.3 us (8%)
    pallas_call x4, Pallas kernels, scatter(): pl.pallas_call(body, out_shape=jax.ShapeDtypeStruct((rows, cols), F32), i...  154 us
    pallas_call x11, Pallas kernels, swap(): pl.pallas_call(functools.partial(swap_kernel, kind, count), out_shape=[ja...  119 us
    pallas_call x1, Pallas kernels, attend(): pl.pallas_call(attend_kernel, grid=(pairs,), out_shape=[jax.ShapeDtypeStr...  27.9 us
    pallas_call x2, Pallas kernels, route(): pl.pallas_call(route_kernel, out_shape=jax.ShapeDtypeStruct(x.shape, x.dt...  25.2 us
    dot_general x9, matrix products, dot_nt(): lax.dot_general(a, b, (((1,), (1,)), ((), ())), preferred_element_type=F32)  24.3 us
    unnamed x210, local copies, waits for them, and re-layouts  23.7 us
    pallas_call x1, Pallas kernels, gather(): pl.pallas_call(functools.partial(gather_kernel, n), out_shape=jax.ShapeDt...  23.3 us
    pallas_call x1, Pallas kernels, attend_back(): pl.pallas_call(attend_back_kernel, grid=(pairs,), out_shape=[jax.ShapeDty...  20.7 us

profile of v1, /device:TPU:17, one launch (start us, length us, event | category | flops | bytes accessed | tf_op | source)
XLA Modules:
  0.0 599.7 jit_solution(18390329663422918337)
XLA Ops:
  7.5 2.0 copy.99.refs_1_
  9.5 2.0 dynamic-slice_bitcast_fusion.refs_5_
  13.1 71.0 %swap_x_1.1 = (bf16[128,768]{1,0:T(8,128)(2,1)}, bf16[384,576]{1,0:T(8,128)(2,1)}, bf16[192,384]{1,0:T(8,128)(2,1)}, bf16[384,768]{1,0:T(8,128)(2,1)}, bf16[768,...) custom-call(bf16[128,768]{1,0:T(8,128)(2,1)} %dynamic-slice_bitcast_fusion.1.refs_0_, ...), custom_call_target="tpu_custom_call" | custom-call | tf_op jit(solution)/shard_map/swap_x_1/pallas_call | solution.py:65
  87.2 2.0 copy.103
  89.2 2.1 pad_maximum_fusion.7
  91.3 2.0 bitcast_select_fusion
  93.3 3.9 copy.100
  97.1 2.2 convolution_convert_fusion.7
  100.4 2.5 fusion.88
  104.8 2.2 fusion.89
  106.9 6.7 %swap_x_2.1 = bf16[160,768]{1,0:T(8,128)(2,1)} custom-call(bf16[160,768]{1,0:T(8,128)(2,1)} %get-tuple-element.149.refs_0_), custom_call_target="tpu_custom_call" | custom-call | tf_op jit(solution)/shard_map/swap_x_2/pallas_call | solution.py:65
  118.1 5.8 swap_x_3.1
  126.1 4.2 swap_core_4.1
  137.0 3.2 swap_core_5.1
  140.3 3.0 pad_maximum_fusion.3
  143.3 27.9 %attend.1 = (bf16[784,384]{1,0:T(8,128)(2,1)}, bf16[6,784,1568]{2,1,0:T(8,128)(2,1)}) custom-call(bf16[784,384]{1,0:T(8,128)(2,1)} %slice.121.q_ref, bf16[1568,384]{1,0:T(8,128)(2,1)} %get-tuple-element.113.k_ref, bf16[1568,384]{1,0:T(8,128)(2,1)} %get-tuple-element.112.v_ref), custom_call_target="tpu_custom_call" | custom-call | tf_op jit(solution)/shard_map/attend/pallas_call | solution.py:292
  176.4 4.0 fusion.6
  180.3 2.3 fusion.14
  182.6 2.4 convolution_convert_fusion.4
  185.0 4.1 reshape.400
  189.1 5.6 multiply_reduce_fusion.1
  194.7 2.6 convolution_convert_fusion.5
  197.3 3.7 reshape.399
  201.0 2.4 multiply_add_fusion.1
  204.7 12.2 %route_6.1 = bf16[2,784,192]{2,1,0:T(8,128)(2,1)} custom-call(bf16[2,784,192]{2,1,0:T(8,128)(2,1)} %pad_maximum_fusion.8.x_ref), custom_call_target="tpu_custom_call" | custom-call | tf_op jit(solution)/shard_map/route_6/pallas_call | solution.py:109
  220.7 2.7 convolution_convert_fusion.8.do_ref
  223.4 20.7 %attend_back.1 = (bf16[784,384]{1,0:T(8,128)(2,1)}, f32[1568,384]{1,0:T(8,128)}, f32[1568,384]{1,0:T(8,128)}) custom-call(bf16[784,384]{1,0:T(8,128)(2,1)} %slice.121.q_ref, bf16[1568,384]{1,0:T(8,128)(2,1)} %get-tuple-element.113.k_ref, bf16[1568,384]{1,0:T(8,128)(2,1)} %get-tuple-element.112.v_ref, bf16[784,384]{1,0:T(8,128)(2,1)} %get-tuple-element.32.o_ref, ...), custom_call_target="tpu_custom_call" | custom-call | tf_op jit(solution)/shard_map/attend_back/pallas_call | solution.py:350
  248.8 5.0 swap_core_7.1
  255.9 2.9 multiply_reduce_fusion.2
  258.8 2.3 convolution_convert_fusion.6
  261.1 2.3 copy.119
  263.4 2.1 fusion.84
  265.6 3.5 multiply_reduce_fusion
  269.0 2.0 copy.128
  272.0 2.2 convolution_convert_fusion.15.refs_0_
  277.6 4.9 swap_x_10.1
  282.5 1.9 convolution_convert_fusion.11
  285.7 13.0 %route_8.1 = bf16[2,784,192]{2,1,0:T(8,128)(2,1)} custom-call(bf16[2,784,192]{2,1,0:T(8,128)(2,1)} %pad_maximum_fusion.9.x_ref), custom_call_target="tpu_custom_call" | custom-call | tf_op jit(solution)/shard_map/route_8/pallas_call | solution.py:109
  298.7 2.2 select_bitcast_fusion.1
  300.9 2.0 copy.114
  302.8 2.1 select_n.142
  309.0 3.5 fusion.8
  314.9 2.0 maximum_bitcast_fusion.g_ref
  316.8 17.3 %scatter_16.1 = f32[48,392]{1,0:T(8,128)} custom-call(bf16[1,16,48,392]{3,2,1,0:T(8,128)(2,1)} %maximum_bitcast_fusion.g_ref), custom_call_target="tpu_custom_call" | custom-call | tf_op jit(solution)/shard_map/scatter_16/pallas_call | solution.py:183
  335.9 2.6 fusion.93
  338.5 7.4 %swap_x_12.1 = bf16[160,768]{1,0:T(8,128)(2,1)} custom-call(bf16[160,768]{1,0:T(8,128)(2,1)} %get-tuple-element.161.refs_0_), custom_call_target="tpu_custom_call" | custom-call | tf_op jit(solution)/shard_map/swap_x_12/pallas_call | solution.py:65
  351.4 2.2 fusion.15
  361.4 6.5 %swap_x_13.1 = bf16[160,768]{1,0:T(8,128)(2,1)} custom-call(bf16[160,768]{1,0:T(8,128)(2,1)} %get-tuple-element.165.refs_0_), custom_call_target="tpu_custom_call" | custom-call | tf_op jit(solution)/shard_map/swap_x_13/pallas_call | solution.py:65
  370.4 2.3 fusion.76
  374.7 13.2 %scatter_17.1 = f32[32,384]{1,0:T(8,128)} custom-call(bf16[1,16,32,384]{3,2,1,0:T(8,128)(2,1)} %maximum_maximum_fusion.g_ref), custom_call_target="tpu_custom_call" | custom-call | tf_op jit(solution)/shard_map/scatter_17/pallas_call | solution.py:183
  392.0 2.6 swap_core_14.1
  396.4 23.3 %gather_18.1 = bf16[32,32,384]{2,1,0:T(8,128)(2,1)} custom-call(bf16[32,384]{1,0:T(8,128)(2,1)} %convert_element_type.252.x_ref), custom_call_target="tpu_custom_call" | custom-call | tf_op jit(solution)/shard_map/gather_18/pallas_call | solution.py:230
  424.6 2.0 fusion.7
  427.9 3.0 copy.131
  430.9 3.7 fusion.83
  439.0 3.9 concatenate.97
  442.8 4.6 convert_element_type.263
  447.4 3.0 copy.129
  450.4 3.8 concatenate.96
  454.1 4.6 convert_element_type.262
  460.7 2.1 pad_maximum_fusion.1.g_ref
  462.9 35.1 %scatter_11.1 = f32[48,1152]{1,0:T(8,128)} custom-call(bf16[2,16,48,1152]{3,2,1,0:T(8,128)(2,1)} %pad_maximum_fusion.1.g_ref), custom_call_target="tpu_custom_call" | custom-call | tf_op jit(solution)/shard_map/scatter_11/pallas_call | solution.py:183
  503.9 3.3 pad_maximum_fusion.g_ref
  507.2 88.1 %scatter_15.1 = f32[48,4608]{1,0:T(8,128)} custom-call(bf16[1,16,48,4608]{3,2,1,0:T(8,128)(2,1)} %pad_maximum_fusion.g_ref), custom_call_target="tpu_custom_call" | custom-call | tf_op jit(solution)/shard_map/scatter_15/pallas_call | solution.py:183
  (326 shorter events, 103.9 us)
Async XLA Ops:
  0.7 114.4 %copy-start = (bf16[768,1536]{1,0:T(8,128)(2,1)S(1)}, bf16[768,1536]{1,0:T(8,128)(2,1)}, u32[]{:S(2)}) copy-start(bf16[768,1536]{1,0:T(8,128)(2,1)} %param.24) | copy-start | bytes 7077892
  2.1 128.3 %copy-start.81 = (s32[1,1,160]{2,1,0:T(1,128)}, s32[1,1,160]{2,1,0:T(1,128)S(1)}, u32[]{:S(2)}) copy-start(s32[1,1,160]{2,1,0:T(1,128)S(1)} %constant_dynamic-slice_fusion.2) | copy-start | bytes 1924
  4.0 99.0 %copy-start.97 = (pred[160]{0:T(512)(128)(4,1)}, pred[160]{0:T(512)(128)(4,1)S(1)}, u32[]{:S(2)}) copy-start(pred[160]{0:T(512)(128)(4,1)S(1)} %iota_compare_fusion) | copy-start | bytes 484
  4.7 125.6 %copy-start.92 = (pred[160]{0:T(512)(128)(4,1)}, pred[160]{0:T(512)(128)(4,1)S(1)}, u32[]{:S(2)}) copy-start(pred[160]{0:T(512)(128)(4,1)S(1)} %iota_compare_fusion.1) | copy-start | bytes 484
  4.9 125.4 %copy-start.67 = (f32[784]{0:T(1024)}, f32[784]{0:T(1024)S(1)}, u32[]{:S(2)}) copy-start(f32[784]{0:T(1024)S(1)} %broadcast_subtract_fusion) | copy-start | bytes 9412
  9.5 2.0 copy-start.17
  85.5 3.6 copy-start.41
  86.9 10.2 %copy-start.74 = (f32[160]{0:T(256)}, f32[160]{0:T(256)S(1)}, u32[]{:S(2)}) copy-start(f32[160]{0:T(256)S(1)} %broadcast_multiply_fusion.11) | copy-start | bytes 1924
  87.2 10.0 %copy-start.76 = (f32[160]{0:T(256)}, f32[160]{0:T(256)S(1)}, u32[]{:S(2)}) copy-start(f32[160]{0:T(256)S(1)} %add_rsqrt_fusion.3) | copy-start | bytes 1924
  89.2 2.1 copy-start.48
  93.3 3.9 copy-start.66
  104.8 2.2 copy-start.55
  106.9 8.1 %copy-start.65 = (f32[768]{0:T(1024)S(1)}, f32[768]{0:T(1024)}, u32[]{:S(2)}) copy-start(f32[768]{0:T(1024)} %param.27) | copy-start | bytes 9220
  118.1 7.0 %copy-start.32 = (bf16[768,384]{1,0:T(8,128)(2,1)S(1)}, bf16[768,384]{1,0:T(8,128)(2,1)}, u32[]{:S(2)}) copy-start(bf16[768,384]{1,0:T(8,128)(2,1)} %param.28) | copy-start | bytes 1769476
  123.9 6.4 %copy-start.18 = (f32[784,384]{1,0:T(8,128)S(1)}, f32[784,384]{1,0:T(8,128)}, u32[]{:S(2)}) copy-start(f32[784,384]{1,0:T(8,128)} %param.30) | copy-start | bytes 3612676
  124.0 6.4 %copy-start.56 = (bf16[784,384]{1,0:T(8,128)(2,1)S(1)}, bf16[784,384]{1,0:T(8,128)(2,1)}, u32[]{:S(2)}) copy-start(bf16[784,384]{1,0:T(8,128)(2,1)} %get-tuple-element.30) | copy-start | bytes 1806340
  124.0 6.4 %copy-start.91 = (f32[384]{0:T(512)S(1)}, f32[384]{0:T(512)}, u32[]{:S(2)}) copy-start(f32[384]{0:T(512)} %param.29) | copy-start | bytes 4612
  125.1 7.0 %copy-start.45 = (bf16[160,768]{1,0:T(8,128)(2,1)}, bf16[160,768]{1,0:T(8,128)(2,1)S(1)}, u32[]{:S(2)}) copy-start(bf16[160,768]{1,0:T(8,128)(2,1)S(1)} %add_convert_fusion.1) | copy-start | bytes 737284
  132.1 39.1 %copy-start.3 = (f32[784,384]{1,0:T(8,128)}, f32[784,384]{1,0:T(8,128)S(1)}, u32[]{:S(2)}) copy-start(f32[784,384]{1,0:T(8,128)S(1)} %get-tuple-element.156) | copy-start | bytes 3612676
  132.1 2.9 copy-start.69
  137.0 3.3 copy-start.8
  173.0 7.4 %copy-start.1 = (f32[784,384]{1,0:T(8,128)}, f32[784,384]{1,0:T(8,128)S(1)}, u32[]{:S(2)}) copy-start(f32[784,384]{1,0:T(8,128)S(1)} %get-tuple-element.158) | copy-start | bytes 3612676
  189.1 5.7 copy-start.2
  189.1 5.7 copy-start.29
  201.0 2.4 copy-start.50
  203.4 13.5 %copy-start.6 = (f32[784,384]{1,0:T(8,128)}, f32[784,384]{1,0:T(8,128)S(1)}, u32[]{:S(2)}) copy-start(f32[784,384]{1,0:T(8,128)S(1)} %multiply_add_fusion.1) | copy-start | bytes 3612676
  204.6 12.2 %copy-start.13 = (bf16[784,384]{1,0:T(8,128)(2,1)S(1)}, bf16[784,384]{1,0:T(8,128)(2,1)}, u32[]{:S(2)}) copy-start(bf16[784,384]{1,0:T(8,128)(2,1)} %get-tuple-element.32.o_ref) | copy-start | bytes 1806340
  245.5 2.0 copy-start.47
  253.8 1.9 copy-start.54
  253.8 1.9 copy-start.70
  253.9 1.9 copy-start.79
  253.9 2.1 copy-start.96
  263.3 2.1 copy-start.87
  263.4 2.1 copy-start.86
  263.4 2.1 copy-start.5
  263.4 2.2 copy-start.68
  263.4 2.2 copy-start.71
  263.4 2.2 copy-start.80
  263.4 2.2 copy-start.90
  272.0 10.5 %copy-start.46 = (bf16[160,768]{1,0:T(8,128)(2,1)S(1)}, bf16[160,768]{1,0:T(8,128)(2,1)}, u32[]{:S(2)}) copy-start(bf16[160,768]{1,0:T(8,128)(2,1)} %copy-done.45) | copy-start | bytes 737284
  272.0 12.4 %copy-start.25 = (bf16[784,384]{1,0:T(8,128)(2,1)S(1)}, bf16[784,384]{1,0:T(8,128)(2,1)}, u32[]{:S(2)}) copy-start(bf16[784,384]{1,0:T(8,128)(2,1)} %get-tuple-element.105) | copy-start | bytes 1806340
  300.9 6.0 %copy-start.40 = (bf16[160,384]{1,0:T(8,128)(2,1)S(1)}, bf16[160,384]{1,0:T(8,128)(2,1)}, u32[]{:S(2)}) copy-start(bf16[160,384]{1,0:T(8,128)(2,1)} %add.172.refs_0_) | copy-start | bytes 368644
  300.9 6.0 %copy-start.49 = (bf16[160,384]{1,0:T(8,128)(2,1)S(1)}, bf16[160,384]{1,0:T(8,128)(2,1)}, u32[]{:S(2)}) copy-start(bf16[160,384]{1,0:T(8,128)(2,1)} %swap_x_10.1) | copy-start | bytes 368644
  304.9 4.1 copy-start.52
  309.0 3.5 copy-start.43
  335.9 10.1 %copy-start.73 = (f32[160]{0:T(256)S(1)}, f32[160]{0:T(256)}, u32[]{:S(2)}) copy-start(f32[160]{0:T(256)} %copy-done.72) | copy-start | bytes 1924
  338.5 8.8 %copy-start.22 = (f32[160,768]{1,0:T(8,128)S(1)}, f32[160,768]{1,0:T(8,128)}, u32[]{:S(2)}) copy-start(f32[160,768]{1,0:T(8,128)} %copy-done.21) | copy-start | bytes 1474564
  349.4 4.1 copy-start.83
  349.4 4.1 copy-start.98
  358.8 2.6 copy-start.15
  360.2 7.8 %copy-start.75 = (f32[160]{0:T(256)S(1)}, f32[160]{0:T(256)}, u32[]{:S(2)}) copy-start(f32[160]{0:T(256)} %copy-done.74) | copy-start | bytes 1924
  360.2 7.8 %copy-start.77 = (f32[160]{0:T(256)S(1)}, f32[160]{0:T(256)}, u32[]{:S(2)}) copy-start(f32[160]{0:T(256)} %copy-done.76) | copy-start | bytes 1924
  361.4 6.6 %copy-start.12 = (f32[160,768]{1,0:T(8,128)}, f32[160,768]{1,0:T(8,128)S(1)}, u32[]{:S(2)}) copy-start(f32[160,768]{1,0:T(8,128)S(1)} %get-tuple-element.166) | copy-start | bytes 1474564
  361.4 7.9 %copy-start.84 = (bf16[2688]{0:T(1024)(128)(2,1)S(1)}, bf16[2688]{0:T(1024)(128)(2,1)}, u32[]{:S(2)}) copy-start(bf16[2688]{0:T(1024)(128)(2,1)} %custom-call) | copy-start | bytes 16132
  361.4 8.4 %copy-start.94 = (bf16[384]{0:T(512)(128)(2,1)S(1)}, bf16[384]{0:T(512)(128)(2,1)}, u32[]{:S(2)}) copy-start(bf16[384]{0:T(512)(128)(2,1)} %get-tuple-element.94) | copy-start | bytes 2308
  361.4 8.6 %copy-start.93 = (bf16[384]{0:T(512)(128)(2,1)S(1)}, bf16[384]{0:T(512)(128)(2,1)}, u32[]{:S(2)}) copy-start(bf16[384]{0:T(512)(128)(2,1)} %get-tuple-element.92) | copy-start | bytes 2308
  361.4 8.8 %copy-start.85 = (bf16[384]{0:T(512)(128)(2,1)S(1)}, bf16[384]{0:T(512)(128)(2,1)}, u32[]{:S(2)}) copy-start(bf16[384]{0:T(512)(128)(2,1)} %get-tuple-element.104) | copy-start | bytes 2308
  368.0 2.4 copy-start.37
  369.3 3.6 copy-start.95
  372.7 18.6 %copy-start.39 = (f32[160,768]{1,0:T(8,128)S(1)}, f32[160,768]{1,0:T(8,128)}, u32[]{:S(2)}) copy-start(f32[160,768]{1,0:T(8,128)} %get-tuple-element.137) | copy-start | bytes 1474564
  424.6 2.0 copy-start.26
  458.7 2.0 copy-start.10
  498.0 3.1 copy-start.38
  595.3 3.5 slice-start
  (36 other events, 53.2 us)

commit v2 on v1

--- a/solution.py
+++ b/solution.py
@@ -368,6 +368,426 @@
         compiler_params=pltpu.CompilerParams(vmem_limit_bytes=LIMIT),
         name="attend_back",
     )(q, k, v, o, do, p)
+
+
+class Wire:
+    def __init__(self, send_sem, recv_sem):
+        self.send_sem, self.recv_sem, self.used = send_sem, recv_sem, 0
+
+    def copy(self, src, dst, partner):
+        index = self.used
+        self.used += 1
+        return send(src, dst, self.send_sem.at[index], self.recv_sem.at[index], partner)
+
+
+def norm_of(z):
+    centre = z - jnp.mean(z, -1, keepdims=True)
+    inverse = lax.rsqrt(jnp.mean(centre * centre, -1, keepdims=True) + EPS)
+    return centre * inverse, inverse
+
+
+def each(count, body):
+    def step(i, carry):
+        body(i)
+        return carry
+
+    lax.fori_loop(0, count, step, 0)
+
+
+def softmax_fwd(q, k, v):
+    scores = dot_nt(q, k)
+    raised = jnp.exp(scores - jnp.max(scores, -1, keepdims=True))
+    scale = 1.0 / jnp.sum(raised, -1, keepdims=True)
+    raised = raised.astype(B16)
+    return raised, scale, dot_nn(raised, v) * scale
+
+
+def dec_kernel(*refs):
+    (
+        vis_ref, cells_row, cells_col, pos_own, pos_far, mask_ref, gain1_ref, gain2_ref,
+        qkv_own, qkv_far, out_own, out_far, up_hbm, down_hbm, cot_hbm,
+        dec_out, pos_out, dvis_out, grad_out, small_out,
+        w_up, w_down, cot, z1, unit1, a_ref, q_ref, keys, values, probs, stats,
+        o_ref, unit2, b_ref, h_ref, slope, z2, do_ref, flip, dkt, dvt, got_kv,
+        dvis_mine, dvis_near, dvis_far, local_sem, send_sem, recv_sem,
+    ) = refs
+    s, d, m = place_of()
+    sibling, facing = (1 - s, d, m), (s, d, 1 - m)
+    stays = s == m
+    length, wide = z1.shape
+    third = wide // 2
+    heads = third // HEAD
+    wire = Wire(send_sem, recv_sem)
+    scale = HEAD**-0.5
+
+    greet([sibling, facing])
+
+    loads = [
+        pltpu.make_async_copy(up_hbm, w_up.at[0], local_sem.at[0]),
+        pltpu.make_async_copy(down_hbm, w_down.at[0], local_sem.at[1]),
+    ]
+    pos_load = pltpu.make_async_copy(pos_own, z1, local_sem.at[3])
+    pos_load.start()
+    cot_load = pltpu.make_async_copy(cot_hbm.at[m], cot, local_sem.at[2])
+    for load in loads:
+        load.start()
+    over, share = [], []
+    for hbm, held in ((up_hbm, w_up), (down_hbm, w_down)):
+        half = hbm.shape[0] // 2
+        mine = pl.ds(s * half, half)
+        over.append(wire.copy(hbm.at[mine], held.at[1, mine], facing))
+        share.append(wire.copy(held.at[1, mine], held.at[1, mine], sibling))
+        over[-1].start()
+    cot_over = wire.copy(cot_hbm.at[1 - m], cot, facing)
+
+    @pl.when(stays)
+    def _():
+        cot_load.start()
+        cot_over.start()
+
+    lane = lax.broadcasted_iota(jnp.int32, (1, 128), 1)
+
+    def keep(plane, rows, column, value):
+        stats[plane, rows] = jnp.where(lane == column, value, stats[plane, rows])
+
+    def kept(plane, rows, column):
+        return stats[plane, rows][:, column : column + 1]
+
+    pos_load.wait()
+    rows_at = 112
+    base = s * length
+
+    def fill(i):
+        rows = pl.ds(pl.multiple_of(i * rows_at, 16), rows_at)
+        ids = lax.broadcasted_iota(jnp.int32, (rows_at, 1), 0) + (base + i * rows_at)
+        place = jnp.where(cells_row[...] == ids, 1.0, 0.0)
+        unseen = 1.0 - jnp.sum(place, -1, keepdims=True)
+        pos = jnp.where(stays, z1[rows], pos_far[rows].astype(F32))
+        z = dot_nn(place.astype(B16), vis_ref[...]) + unseen * mask_ref[...] + pos
+        unit, inverse = norm_of(z)
+        z1[rows] = z
+        unit1[rows] = unit
+        keep(0, rows, heads, inverse)
+        a_ref[rows] = (unit * gain1_ref[...]).astype(B16)
+
+    each(length // rows_at, fill)
+
+    a = a_ref[...]
+    mine_rows = pl.ds(0, length)
+    kv_copies = []
+    for side, weight in enumerate((qkv_own, qkv_far)):
+        keys[side, mine_rows] = dot_nn(a, weight[1]).astype(B16)
+        values[side, mine_rows] = dot_nn(a, weight[2]).astype(B16)
+        for held in (keys, values):
+            copy = wire.copy(
+                held.at[side, mine_rows], held.at[side, pl.ds(length, length)], sibling
+            )
+            copy.start()
+            kv_copies.append(copy)
+    for side, weight in enumerate((qkv_own, qkv_far)):
+        q_ref[side] = (dot_nn(a, weight[0]).astype(B16).astype(F32) * scale).astype(B16)
+    for copy in kv_copies:
+        copy.wait()
+
+    masks = head_masks()
+    pair = pl.ds(0, 2 * HEAD)
+    lone = pl.ds(2 * HEAD, HEAD)
+
+    def attend_side(side):
+        for start, size in chunks_of(length, 400):
+            rows = pl.ds(start, size)
+            halves = []
+            for head in range(2):
+                q = jnp.where(masks[head], q_ref[side, rows, pair], 0)
+                raised, over_sum, o = softmax_fwd(q, keys[side, :, pair], values[side, :, pair])
+                probs[side, head, rows] = raised
+                keep(side, rows, head, over_sum)
+                halves.append(o)
+            o_ref[side, rows, pair] = jnp.where(masks[0], halves[0], halves[1]).astype(B16)
+            raised, over_sum, o = softmax_fwd(
+                q_ref[side, rows, lone], keys[side, :, lone], values[side, :, lone]
+            )
+            probs[side, 2, rows] = raised
+            keep(side, rows, 2, over_sum)
+            o_ref[side, rows, lone] = o.astype(B16)
+
+    each(2, attend_side)
+
+    for copy, other in zip(over, share):
+        copy.wait()
+        other.start()
+
+    z2[...] = z1[...] + dot_nn(o_ref[0], out_own[...]) + dot_nn(o_ref[1], out_far[...])
+
+    def second(i):
+        rows = pl.ds(pl.multiple_of(i * rows_at, 16), rows_at)
+        unit, inverse = norm_of(z2[rows])
+        unit2[rows] = unit
+        keep(1, rows, heads, inverse)
+        b_ref[rows] = (unit * gain2_ref[...]).astype(B16)
+
+    each(length // rows_at, second)
+    for load in loads:
+        load.wait()
+    for copy in share:
+        copy.wait()
+
+    step = 256
+    steps = w_up.shape[2] // step
+
+    def hidden_at(i):
+        return i // steps, pl.ds(pl.multiple_of((i % steps) * step, step), step)
+
+    def up(i):
+        side, cols = hidden_at(i)
+        u = dot_nn(b_ref[...], w_up[side, :, cols])
+        phi = 0.5 + 0.5 * lax.erf(u * 0.5**0.5)
+        h_ref[side, :, cols] = (u * phi).astype(B16)
+        bell = jnp.exp(u * u * -0.5) * (0.5 / jnp.pi) ** 0.5
+        slope[side, :, cols] = (phi + u * bell).astype(B16)
+
+    each(2 * steps, up)
+
+    def cut(value, out):
+        out[0] = value[:, :third].astype(B16)
+        out[1] = value[:, third:].astype(B16)
+
+    cut(z2[...] + dot_nn(h_ref[0], w_down[0]) + dot_nn(h_ref[1], w_down[1]), dec_out)
+
+    @pl.when(stays)
+    def _():
+        cot_load.wait()
+        cot_over.wait_send()
+
+    @pl.when(jnp.logical_not(stays))
+    def _():
+        cot_over.wait_recv()
+
+    def transposed(value):
+        return jnp.transpose(value.astype(F32)).astype(B16)
+
+    cot_flip = flip.at[0]
+    b_flip = flip.at[1]
+    cot_flip[...] = transposed(cot[...])
+    b_flip[...] = transposed(b_ref[...])
+
+    def down(i):
+        side, cols = hidden_at(i)
+        grad_out[side, 2, :, cols] = dot_nn(cot_flip[...], h_ref[side, :, cols]).astype(B16)
+        grad_u = dot_nt(cot[...], w_down[side, cols, :]) * slope[side, :, cols].astype(F32)
+        grad_u = grad_u.astype(B16)
+        slope[side, :, cols] = grad_u
+        grad_out[side, 1, :, cols] = dot_nn(b_flip[...], grad_u).astype(B16)
+
+    each(2 * steps, down)
+    z1[...] = dot_nt(slope[0], w_up[0]) + dot_nt(slope[1], w_up[1])
+
+    def back_norm(grad, unit, inverse, gain):
+        scaled = grad * gain
+        mean = jnp.mean(scaled, -1, keepdims=True)
+        tilt = jnp.mean(scaled * unit, -1, keepdims=True)
+        return inverse * (scaled - mean - unit * tilt)
+
+    def add_rows(total, value):
+        return total + jnp.sum(value, 0, keepdims=True)
+
+    def second_back(i, total):
+        rows = pl.ds(pl.multiple_of(i * rows_at, 16), rows_at)
+        grad = z1[rows]
+        unit = unit2[rows]
+        z = cot[rows].astype(F32) + back_norm(grad, unit, kept(1, rows, heads), gain2_ref[...])
+        z2[rows] = z
+        b_ref[rows] = z.astype(B16)
+        return add_rows(total, grad * unit)
+
+    zero = jnp.zeros((1, wide), F32)
+    gain2_grad = lax.fori_loop(0, length // rows_at, second_back, zero)
+
+    grad_a = b_ref[...]
+    flip[0] = transposed(grad_a)
+    for side, weight in enumerate((out_own, out_far)):
+        grad_out[side, 0, :, pl.ds(3 * third, third)] = dot_nn(flip[0], o_ref[side]).astype(B16)
+        do_ref[side] = dot_nt(grad_a, weight[...]).astype(B16)
+
+    def attend_back_side(side):
+        for index, (start, size) in enumerate(chunks_of(length, 256)):
+            rows = pl.ds(start, size)
+            for feats, heads in ((pair, (0, 1)), (lone, (2,))):
+                q = q_ref[side, rows, feats]
+                do = do_ref[side, rows, feats].astype(F32)
+                both = do * o_ref[side, rows, feats].astype(F32)
+                k = keys[side, :, feats]
+                v = values[side, :, feats]
+                dq = []
+                for head in heads:
+                    over_sum = kept(side, rows, head)
+                    if len(heads) == 2:
+                        lanes = slice(head * HEAD, (head + 1) * HEAD)
+                        mine = jnp.where(masks[head], both, 0.0)
+                        do_head = jnp.where(masks[head], do, 0.0)
+                    else:
+                        lanes = slice(0, HEAD)
+                        mine, do_head = both, do
+                    delta = jnp.sum(mine, -1, keepdims=True) * over_sum
+                    do_head = (do_head * over_sum).astype(B16)
+                    raised = probs[side, head, rows]
+                    ds = (raised.astype(F32) * (dot_nt(do_head, v) - delta)).astype(B16)
+                    dq.append(dot_nn(ds, k))
+                    dv_part = dot_tn(do_head[:, lanes], raised)
+                    dk_part = dot_tn(q[:, lanes], ds)
+                    at = pl.ds(head * HEAD, HEAD)
+                    if index:
+                        dv_part = dv_part + dvt[at]
+                        dk_part = dk_part + dkt[at]
+                    dvt[at] = dv_part
+                    dkt[at] = dk_part
+                dq = jnp.where(masks[0], dq[0], dq[1]) if len(heads) == 2 else dq[0]
+                q_ref[side, rows, feats] = (dq * scale).astype(B16)
+        for held, out in ((dkt, keys), (dvt, values)):
+            for feats, at in ((pair, pl.ds(0, 2 * HEAD)), (lone, pl.ds(2 * HEAD, HEAD))):
+                out[side, :, feats] = jnp.transpose(held[at]).astype(B16)
+
+    each(2, attend_back_side)
+    far_rows = pl.ds(length, length)
+    kv_back = [
+        [
+            wire.copy(held.at[side, far_rows], got_kv.at[slot, side], sibling)
+            for side in range(2)
+        ]
+        for slot, held in enumerate((keys, values))
+    ]
+    for copies in kv_back:
+        for copy in copies:
+            copy.start()
+
+    a_flip = flip.at[0]
+    a_flip[...] = transposed(a_ref[...])
+    total = None
+    for slot in range(3):
+        for side, weight in enumerate((qkv_own, qkv_far)):
+            if slot:
+                kv_back[slot - 1][side].wait()
+                own = (keys, values)[slot - 1][side, mine_rows].astype(F32)
+                grad = (own + got_kv[slot - 1, side].astype(F32)).astype(B16)
+            else:
+                grad = q_ref[side]
+            grad_out[side, 0, :, pl.ds(slot * third, third)] = dot_nn(a_flip[...], grad).astype(B16)
+            part = dot_nt(grad, weight[slot])
+            total = part if total is None else total + part
+    z1[...] = total
+
+    def first_back(i, totals):
+        rows = pl.ds(pl.multiple_of(i * rows_at, 16), rows_at)
+        grad = z1[rows]
+        unit = unit1[rows]
+        z = z2[rows] + back_norm(grad, unit, kept(0, rows, heads), gain1_ref[...])
+        b_ref[rows] = z.astype(B16)
+        pos_out[0, rows] = z[:, :third].astype(B16)
+        pos_out[1, rows] = z[:, third:].astype(B16)
+        ids = lax.broadcasted_iota(jnp.int32, (rows_at, 1), 0) + (base + i * rows_at)
+        seen = jnp.sum(jnp.where(cells_row[...] == ids, 1.0, 0.0), -1, keepdims=True)
+        return add_rows(totals[0], grad * unit), add_rows(totals[1], (1.0 - seen) * z)
+
+    gain1_grad, mask_grad = lax.fori_loop(0, length // rows_at, first_back, (zero, zero))
+    small_out[0:1] = gain1_grad
+    small_out[1:2] = gain2_grad
+    small_out[2:3] = mask_grad
+
+    used = vis_ref.shape[0]
+    ids = lax.broadcasted_iota(jnp.int32, (used, length), 1) + base
+    place = jnp.where(cells_col[...] == ids, 1.0, 0.0).astype(B16)
+    dvis_mine[...] = dot_nn(place, b_ref[...]).astype(B16)
+    near = wire.copy(dvis_mine, dvis_near, sibling)
+    near.start()
+    near.wait()
+    dvis_mine[...] = (dvis_mine[...].astype(F32) + dvis_near[...].astype(F32)).astype(B16)
+    beyond = wire.copy(dvis_mine, dvis_far, facing)
+
+    @pl.when(stays)
+    def _():
+        beyond.start()
+        dvis_out[...] = dvis_mine[...]
+        beyond.wait_send()
+
+    @pl.when(jnp.logical_not(stays))
+    def _():
+        beyond.wait_recv()
+        dvis_out[...] = dvis_far[...]
+
+
+def decoder(vis, cells, pos_own, pos_far, mask, gains, weights, cot, ident):
+    qkv_own, qkv_far, out_own, out_far, up, down = weights
+    length, wide = pos_own.shape
+    used = vis.shape[0]
+    third = wide // 2
+    hidden = up.shape[1]
+    keys = 2 * length
+    heads = third // HEAD
+    assert heads == 3 and length % 112 == 0
+    whole = pl.BlockSpec(memory_space=VMEM)
+    there = pl.BlockSpec(memory_space=pl.ANY)
+    return pl.pallas_call(
+        dec_kernel,
+        out_shape=[
+            jax.ShapeDtypeStruct((2, length, third), B16),
+            jax.ShapeDtypeStruct((2, length, third), B16),
+            jax.ShapeDtypeStruct((used, wide), B16),
+            jax.ShapeDtypeStruct((2, 3, wide, hidden), B16),
+            jax.ShapeDtypeStruct((8, wide), F32),
+        ],
+        in_specs=[whole] * 3 + [there] + [whole] * 8 + [there] * 3,
+        out_specs=[whole] * 5,
+        scratch_shapes=[
+            VMEM((2, wide, hidden), B16),
+            VMEM((2, hidden, wide), B16),
+            VMEM((length, wide), B16),
+            VMEM((length, wide), F32),
+            VMEM((length, wide), F32),
+            VMEM((length, wide), B16),
+            VMEM((2, length, third), B16),
+            VMEM((2, keys, third), B16),
+            VMEM((2, keys, third), B16),
+            VMEM((2, heads, length, keys), B16),
+            VMEM((2, length, 128), F32),
+            VMEM((2, length, third), B16),
+            VMEM((length, wide), F32),
+            VMEM((length, wide), B16),
+            VMEM((2, length, hidden), B16),
+            VMEM((2, length, hidden), B16),
+            VMEM((length, wide), F32),
+            VMEM((2, length, third), B16),
+            VMEM((2, wide, length), B16),
+            VMEM((third, keys), F32),
+            VMEM((third, keys), F32),
+            VMEM((2, 2, length, third), B16),
+            VMEM((used, wide), B16),
+            VMEM((used, wide), B16),
+            VMEM((used, wide), B16),
+            pltpu.SemaphoreType.DMA((4,)),
+            pltpu.SemaphoreType.DMA((16,)),
+            pltpu.SemaphoreType.DMA((16,)),
+        ],
+        compiler_params=pltpu.CompilerParams(
+            collective_id=ident, has_side_effects=True, vmem_limit_bytes=63 * 1024 * 1024
+        ),
+        name="decoder",
+    )(
+        vis,
+        cells[None, :],
+        cells[:, None],
+        pos_own,
+        pos_far,
+        mask[None, :],
+        gains[0][None, :],
+        gains[1][None, :],
+        qkv_own,
+        qkv_far,
+        out_own,
+        out_far,
+        up,
+        down,
+        cot,
+    )
 
 
 def normed(z, gain):
@@ -468,28 +888,18 @@
     enc_wide = tokens.shape[3]
     used = -(-LONGEST // 32) * 32
 
+    qkv_own = jnp.swapaxes(dec_qkv, 0, 1)
     swapped = swap(
         [
             pick(tokens[:, 0], s),
-            dec_qkv.reshape(dec_wide, -1),
+            qkv_own,
             dec_attn_out,
-            dec_up,
-            dec_down,
-            pick(cotangent[:, 0], 1 - m),
             position_embed.astype(B16),
         ],
         "x",
         1,
     )
-    tok_far, dqkv_far, dout_far, dup_far, ddown_far, cot_far, pos_far = swapped
-    cot = jnp.where(stays, pick(cotangent[:, 0], m), cot_far)
-    pos = jnp.where(stays, position_embed, pos_far.astype(F32))
-    w_qkv = jnp.concatenate(
-        [dec_qkv, dqkv_far.reshape(dec_qkv.shape)], 2
-    ).reshape(dec_wide, -1)
-    w_out = jnp.concatenate([dec_attn_out, dout_far], 0)
-    w_up = jnp.concatenate([dec_up, dup_far], 1)
-    w_down = jnp.concatenate([dec_down, ddown_far], 0)
+    tok_far, qkv_far, out_far, pos_far = swapped
 
     tok_near = pick(tokens[:, 0], s)
     x = jnp.concatenate(
@@ -512,76 +922,24 @@
     vis_far = swap([vis], "core", 4)[0]
 
     vis_used = jnp.where(stays, vis, vis_far)
-    cell_ids = s * cells_half + jnp.arange(cells_half, dtype=jnp.int32)
-    place = (pick(clip_cells[:, 0], m)[None, :used] == cell_ids[:, None]) & (
-        jnp.arange(used)[None, :] < pick(clip_lengths[:, 0], m)
+    cells = jnp.where(jnp.arange(used) < pick(clip_lengths[:, 0], m), pick(clip_cells[:, 0], m)[:used], -1)
+    dec, pos_parts, dvis, dec_grads, dec_small = decoder(
+        vis_used,
+        cells,
+        position_embed,
+        pos_far,
+        mask_token,
+        (dec_gain_one, dec_gain_two),
+        (qkv_own, qkv_far, dec_attn_out, out_far, dec_up, dec_down),
+        cotangent[:, 0],
+        5,
     )
-    place = place.astype(B16)
-    unseen = 1.0 - jnp.sum(place.astype(F32), 1, keepdims=True)
-    filled = jnp.dot(place, vis_used, preferred_element_type=F32) + unseen * mask_token + pos
-    dunit1, dinv1, da_in = normed(filled, dec_gain_one)
-    dqkv = jnp.dot(da_in, w_qkv, preferred_element_type=F32).astype(B16)
-    q, kv = dqkv[:, :dec_wide], dqkv[:, dec_wide:]
-    kv_all = jnp.concatenate([kv, swap([kv], "core", 5)[0]], 0)
-    k_all, v_all = kv_all[:, :dec_wide], kv_all[:, dec_wide:]
-    do_out, dp_saved = attend(q, k_all, v_all)
-    dz2 = filled + jnp.dot(do_out, w_out, preferred_element_type=F32)
-    dunit2, dinv2, db_in = normed(dz2, dec_gain_two)
-    du = jnp.dot(db_in, w_up, preferred_element_type=F32)
-    dh = gelu(du).astype(B16)
-    dec = dz2 + jnp.dot(dh, w_down, preferred_element_type=F32)
-
-    def cut(value):
-        return jnp.stack(jnp.split(value.astype(B16), 2, axis=1))
-
-    decoded = route(cut(dec), 6)
-
-    dy = cot.astype(F32)
-    grad_h = dot_nt(cot, w_down)
-    g_down = dot_tn(cot, dh)
-    grad_u = (grad_h * gelu_slope(du)).astype(B16)
-    g_up = dot_tn(db_in, grad_u)
-    grad_b = dot_nt(grad_u, w_up)
-    g_dtwo = jnp.sum(grad_b * dunit2, 0)
-    grad_z2 = dy + norm_back(grad_b, dunit2, dinv2, dec_gain_two)
-    grad_a = grad_z2.astype(B16)
-    g_out = dot_tn(grad_a, do_out)
-    grad_o = dot_nt(grad_a, w_out).astype(B16)
-    grad_q, grad_k, grad_v = attend_back(q, k_all, v_all, do_out, grad_o, dp_saved)
-    half = cells_half
-    far_kv = jnp.concatenate([grad_k[half:], grad_v[half:]], 1).astype(B16)
-    near_kv = jnp.concatenate([grad_k[:half], grad_v[:half]], 1)
-    grad_kv = (near_kv + swap([far_kv], "core", 7)[0].astype(F32)).astype(B16)
-    grad_qkv = jnp.concatenate([grad_q, grad_kv], 1)
-    g_qkv = dot_tn(da_in, grad_qkv)
-    grad_n = dot_nt(grad_qkv, w_qkv)
-    g_done = jnp.sum(grad_n * dunit1, 0)
-    grad_filled = grad_z2 + norm_back(grad_n, dunit1, dinv1, dec_gain_one)
-    g_mask = jnp.sum(unseen * grad_filled, 0)
-    position_parts = route(cut(grad_filled), 8)
-
-    dvis = dot_tn(place, grad_filled.astype(B16)).astype(B16)
-    dvis = dvis + swap([dvis], "core", 9)[0]
-    dvis = jnp.where(stays, dvis, swap([dvis], "x", 10)[0])
-
-    g_qkv = g_qkv.reshape(dec_wide, 3, 2, -1)
-    g_out = g_out.reshape(dec_wide, 2, -1)
-    g_up = g_up.reshape(dec_wide, 2, -1)
-    g_down = g_down.reshape(dec_wide, 2, -1)
+    g_done, g_dtwo, g_mask = dec_small[0], dec_small[1], dec_small[2]
+    decoded = route(dec, 6)
+    position_parts = route(pos_parts, 8)
     packed = jnp.stack(
         [
-            pack(
-                jnp.concatenate(
-                    [
-                        g_qkv[:, :, side].reshape(dec_wide, -1),
-                        g_out[:, side],
-                        g_up[:, side],
-                        g_down[:, side],
-                    ],
-                    1,
-                ),
-                owners,
-            )
+            pack(jnp.concatenate([dec_grads[side, 0], dec_grads[side, 1], dec_grads[side, 2]], 1), owners)
             for side in range(2)
         ]
     )

time: 611 us -> 467 us (0.76)
  local copies, waits for them, and re-layouts: 110 us -> 43.1 us
  matrix products: 67.2 us -> 28.5 us
  Pallas kernels: 370 us -> 349 us
  other arithmetic: 50.3 us -> 35.3 us
    pallas_call x11 -> x7, Pallas kernels: 119 us -> 67.2 us  [swap(): pl.pallas_call(functools.partial(swap_kernel, kind, count), out_shape=[ja...]
    pallas_call x2 -> x1, Pallas kernels: 48.6 us -> 79.9 us  [decoder(): pl.pallas_call(dec_kernel, out_shape=[jax.ShapeDtypeStruct((2, length, th...]
    dot_general x9 -> x5, matrix products: 24.3 us -> 7.27 us  [dot_nt(): lax.dot_general(a, b, (((1,), (1,)), ((), ())), preferred_element_type=F32)]
    unnamed x210 -> x100, local copies, waits for them, and re-layouts: 23.7 us -> 8.34 us
    slice x11 -> x3, local copies, waits for them, and re-layouts: 13.8 us -> 0.15 us  [the longest x2 0.11 us: per_device(): pick(clip_cells[:, 0], m)[:used]]
    another operation x7 -> x0, local copies, waits for them, and re-layouts: 13.4 us -> none
    dot_general x10 -> x5, matrix products: 17.8 us -> 7.52 us  [dot_tn(): lax.dot_general(a, b, (((0,), (0,)), ((), ())), preferred_element_type=F32)]
    reshape x1 -> x4, local copies, waits for them, and re-layouts: 2 us -> 11.4 us  [pack(): grad = grad.astype(B16).reshape(owners, own, fold, cols // fold)]
where the time goes in v2:
time: 467 us; the launch traced here: 458 us
  Pallas kernels  349 us (75%)
  local copies, waits for them, and re-layouts  43.1 us (9%)
  other arithmetic  35.3 us (8%)
  matrix products  28.5 us (6%)
    pallas_call x4, Pallas kernels, scatter(): pl.pallas_call(body, out_shape=jax.ShapeDtypeStruct((rows, cols), F32), i...  154 us
    pallas_call x1, Pallas kernels, decoder(): pl.pallas_call(dec_kernel, out_shape=[jax.ShapeDtypeStruct((2, length, th...  79.9 us
    pallas_call x7, Pallas kernels, swap(): pl.pallas_call(functools.partial(swap_kernel, kind, count), out_shape=[ja...  67.2 us
    pallas_call x2, Pallas kernels, route(): pl.pallas_call(route_kernel, out_shape=jax.ShapeDtypeStruct(x.shape, x.dt...  24.5 us
    pallas_call x1, Pallas kernels, gather(): pl.pallas_call(functools.partial(gather_kernel, n), out_shape=jax.ShapeDt...  23.1 us
    reshape x4, local copies, waits for them, and re-layouts, pack(): grad = grad.astype(B16).reshape(owners, own, fold, cols // fold)  11.4 us

profile of v2, /device:TPU:17, one launch (start us, length us, event | category | flops | bytes accessed | tf_op | source)
XLA Modules:
  0.0 457.7 jit_solution(5646924835839873204)
XLA Ops:
  0.7 1.7 dynamic-slice_bitcast_fusion.refs_0_
  2.4 2.1 copy.60
  4.5 2.2 convert_element_type.150.refs_3_
  6.6 34.9 %swap_x_1.1 = (bf16[128,768]{1,0:T(8,128)(2,1)}, bf16[3,384,192]{2,1,0:T(8,128)(2,1)}, bf16[192,384]{1,0:T(8,128)(2,1)}, bf16[784,384]{1,0:T(8,128)(2,1)}) custom-call(bf16[128,768]{1,0:T(8,128)(2,1)} %dynamic-slice_bitcast_fusion.refs_0_, bf16[3,384,192]{2,1,0:T(8,128)(2,1)} %bitcast.205, bf16[192,384]{1,0:T(8,128)(2,1)} %refs_10_.1, ...), custom_call_target="tpu_custom_call" | custom-call | tf_op jit(solution)/shard_map/swap_x_1/pallas_call | solution.py:65
  42.9 2.6 copy.61
  45.5 1.5 convolution_convert_fusion.3
  47.0 1.2 copy.62
  49.6 1.4 fusion.60
  51.8 1.0 fusion.61
  52.8 6.2 %swap_x_2.1 = bf16[160,768]{1,0:T(8,128)(2,1)} custom-call(bf16[160,768]{1,0:T(8,128)(2,1)} %get-tuple-element.113.refs_0_), custom_call_target="tpu_custom_call" | custom-call | tf_op jit(solution)/shard_map/swap_x_2/pallas_call | solution.py:65
  59.0 1.1 fusion.56
  60.4 1.6 multiply_convert_fusion.1
  62.0 1.2 fusion.62
  63.3 5.4 %swap_x_3.1 = bf16[160,768]{1,0:T(8,128)(2,1)} custom-call(bf16[160,768]{1,0:T(8,128)(2,1)} %get-tuple-element.117.refs_0_), custom_call_target="tpu_custom_call" | custom-call | tf_op jit(solution)/shard_map/swap_x_3/pallas_call | solution.py:65
  68.7 1.0 add_convert_fusion.1
  70.7 5.0 %swap_core_4.1 = bf16[160,384]{1,0:T(8,128)(2,1)} custom-call(bf16[160,384]{1,0:T(8,128)(2,1)} %convolution_convert_fusion.9.refs_0_), custom_call_target="tpu_custom_call" | custom-call | tf_op jit(solution)/shard_map/swap_core_4/pallas_call | solution.py:65
  75.7 1.6 broadcast_select_fusion.2.refs_0_
  77.4 1.3 fusion.45.refs_2_
  78.7 1.2 compare_select_fusion.refs_1_
  81.6 79.9 %decoder.1 = (bf16[2,784,192]{2,1,0:T(8,128)(2,1)}, bf16[2,784,192]{2,1,0:T(8,128)(2,1)}, bf16[160,384]{1,0:T(8,128)(2,1)}, bf16[2,3,384,768]{3,2,1,0:T(8,128)(2,1)}, f32[8,384]{1,0:T(8,128)}) custom-call(bf16[160,384]{1,0:T(8,128)(2,1)} %broadcast_select_fusion.2.refs_0_, s32[1,160]{1,0:T(1,128)} %compare_select_fusion.refs_1_, s32[160,1]{1,0:T(8,128)} %fusion.45.refs_2_, ...), custom_call_target="tpu_custom_call" | custom-call | tf_op jit(solution)/shard_map/decoder/pallas_call | solution.py:729
  161.6 2.2 slice_bitcast_fusion.5
  163.7 1.4 pad_maximum_fusion.2
  165.1 4.6 %reshape.330 = bf16[16,24,2,1152]{3,2,1,0:T(2,128)(2,1)} reshape(bf16[384,2304]{1,0:T(8,128)(2,1)} %get-tuple-element.127) | data formatting | bytes 3538944 | tf_op jit(solution)/shard_map/reshape | solution.py:847
  169.8 2.9 copy.80
  172.7 2.0 reshape.331
  174.7 1.8 copy.81
  176.7 2.2 pad_maximum_fusion.1.g_ref
  178.9 34.1 %scatter_11.1 = f32[48,1152]{1,0:T(8,128)} custom-call(bf16[2,16,48,1152]{3,2,1,0:T(8,128)(2,1)} %pad_maximum_fusion.1.g_ref), custom_call_target="tpu_custom_call" | custom-call | tf_op jit(solution)/shard_map/scatter_11/pallas_call | solution.py:183
  216.5 3.1 fusion.2
  219.6 1.6 fusion.63
  221.2 7.4 %swap_x_12.1 = bf16[160,768]{1,0:T(8,128)(2,1)} custom-call(bf16[160,768]{1,0:T(8,128)(2,1)} %get-tuple-element.119.refs_0_), custom_call_target="tpu_custom_call" | custom-call | tf_op jit(solution)/shard_map/swap_x_12/pallas_call | solution.py:65
  228.6 1.9 multiply_reduce_fusion.1
  230.5 1.9 convert_bitcast_fusion.1
  232.4 1.0 convolution_convert_fusion.8
  233.4 1.1 copy.65
  234.6 1.6 multiply_reduce_fusion
  238.3 1.9 fusion.11
  240.4 1.2 fusion.64
  241.6 6.5 %swap_x_13.1 = bf16[160,768]{1,0:T(8,128)(2,1)} custom-call(bf16[160,768]{1,0:T(8,128)(2,1)} %get-tuple-element.123.refs_0_), custom_call_target="tpu_custom_call" | custom-call | tf_op jit(solution)/shard_map/swap_x_13/pallas_call | solution.py:65
  248.1 1.2 fusion.40
  251.9 13.6 %scatter_17.1 = f32[32,384]{1,0:T(8,128)} custom-call(bf16[1,16,32,384]{3,2,1,0:T(8,128)(2,1)} %maximum_maximum_fusion.g_ref), custom_call_target="tpu_custom_call" | custom-call | tf_op jit(solution)/shard_map/scatter_17/pallas_call | solution.py:183
  265.5 1.4 convert_element_type.176.x_ref
  266.9 23.1 %gather_18.1 = bf16[32,32,384]{2,1,0:T(8,128)(2,1)} custom-call(bf16[32,384]{1,0:T(8,128)(2,1)} %convert_element_type.176.x_ref), custom_call_target="tpu_custom_call" | custom-call | tf_op jit(solution)/shard_map/gather_18/pallas_call | solution.py:230
  290.0 1.2 convert_bitcast_fusion
  291.2 1.1 copy.74
  294.5 2.1 fusion.53
  296.8 2.0 fusion.1
  298.7 2.0 convolution_convert_fusion.1
  300.7 1.1 copy.71
  301.8 1.4 fusion.6
  303.3 1.8 convolution_convert_fusion
  305.2 3.4 pad_maximum_fusion.g_ref
  308.6 88.4 %scatter_15.1 = f32[48,4608]{1,0:T(8,128)} custom-call(bf16[1,16,48,4608]{3,2,1,0:T(8,128)(2,1)} %pad_maximum_fusion.g_ref), custom_call_target="tpu_custom_call" | custom-call | tf_op jit(solution)/shard_map/scatter_15/pallas_call | solution.py:183
  397.0 1.9 slice_bitcast_fusion.6
  400.5 1.5 slice_bitcast_fusion.17
  402.0 12.3 %route_8.1 = bf16[2,784,192]{2,1,0:T(8,128)(2,1)} custom-call(bf16[2,784,192]{2,1,0:T(8,128)(2,1)} %get-tuple-element.33.x_ref), custom_call_target="tpu_custom_call" | custom-call | tf_op jit(solution)/shard_map/route_8/pallas_call | solution.py:109
  414.3 1.3 select_bitcast_fusion.1
  417.9 18.3 %scatter_16.1 = f32[48,392]{1,0:T(8,128)} custom-call(bf16[1,16,48,392]{3,2,1,0:T(8,128)(2,1)} %maximum_bitcast_fusion.g_ref), custom_call_target="tpu_custom_call" | custom-call | tf_op jit(solution)/shard_map/scatter_16/pallas_call | solution.py:183
  436.2 1.0 copy.79
  438.8 1.9 swap_core_14.1
  440.7 1.0 select_bitcast_fusion.3
  442.4 12.2 %route_6.1 = bf16[2,784,192]{2,1,0:T(8,128)(2,1)} custom-call(bf16[2,784,192]{2,1,0:T(8,128)(2,1)} %get-tuple-element.30.x_ref), custom_call_target="tpu_custom_call" | custom-call | tf_op jit(solution)/shard_map/route_6/pallas_call | solution.py:109
  454.6 1.3 bitcast_convert_fusion
  455.9 1.6 copy.83
  (156 shorter events, 23.4 us)
Async XLA Ops:
  0.7 51.1 %copy-start = (bf16[384,768]{1,0:T(8,128)(2,1)S(1)}, bf16[384,768]{1,0:T(8,128)(2,1)}, u32[]{:S(2)}) copy-start(bf16[384,768]{1,0:T(8,128)(2,1)} %param.23) | copy-start | bytes 1769476
  0.7 40.8 %copy-start.31 = (bf16[2,1,128,768]{3,2,1,0:T(8,128)(2,1)S(1)}, bf16[2,1,128,768]{3,2,1,0:T(8,128)(2,1)}, u32[]{:S(2)}) copy-start(bf16[2,1,128,768]{3,2,1,0:T(8,128)(2,1)} %param.19) | copy-start | bytes 1179652
  42.5 3.0 copy-start.34
  45.5 5.6 %copy-start.4 = (bf16[768,3,384]{0,2,1:T(8,128)(2,1)}, bf16[768,3,384]{0,2,1:T(8,128)(2,1)S(1)}, u32[]{:S(2)}) copy-start(bf16[768,3,384]{0,2,1:T(8,128)(2,1)S(1)} %copy.61) | copy-start | bytes 5308420
  45.5 2.7 copy-start.39
  48.2 3.5 copy-start.22
  49.6 2.1 copy-start.44
  51.1 0.7 copy-start.36
  51.7 10.2 %copy-start.27 = (bf16[6,64,160]{2,1,0:T(8,128)(2,1)}, bf16[6,64,160]{2,1,0:T(8,128)(2,1)S(1)}, u32[]{:S(2)}) copy-start(bf16[6,64,160]{2,1,0:T(8,128)(2,1)S(1)} %convolution_convert_fusion.7) | copy-start | bytes 368644
  51.8 8.6 %copy-start.6 = (bf16[768,1536]{1,0:T(8,128)(2,1)S(1)}, bf16[768,1536]{1,0:T(8,128)(2,1)}, u32[]{:S(2)}) copy-start(bf16[768,1536]{1,0:T(8,128)(2,1)} %param.24) | copy-start | bytes 7077892
  51.8 8.6 %copy-start.33 = (f32[768]{0:T(1024)S(1)}, f32[768]{0:T(1024)}, u32[]{:S(2)}) copy-start(f32[768]{0:T(1024)} %param.27) | copy-start | bytes 9220
  60.2 8.6 %copy-start.2 = (f32[160,768]{1,0:T(8,128)}, f32[160,768]{1,0:T(8,128)S(1)}, u32[]{:S(2)}) copy-start(f32[160,768]{1,0:T(8,128)S(1)} %get-tuple-element.81) | copy-start | bytes 1474564
  60.2 1.9 copy-start.16
  62.0 7.8 %copy-start.12 = (bf16[160,1536]{1,0:T(8,128)(2,1)}, bf16[160,1536]{1,0:T(8,128)(2,1)S(1)}, u32[]{:S(2)}) copy-start(bf16[160,1536]{1,0:T(8,128)(2,1)S(1)} %get-tuple-element.115) | copy-start | bytes 1474564
  62.0 7.7 %copy-start.17 = (bf16[768,384]{1,0:T(8,128)(2,1)S(1)}, bf16[768,384]{1,0:T(8,128)(2,1)}, u32[]{:S(2)}) copy-start(bf16[768,384]{1,0:T(8,128)(2,1)} %param.28) | copy-start | bytes 1769476
  63.3 14.0 %copy-start.40 = (s32[2,1,256]{2,1,0:T(1,128)S(1)}, s32[2,1,256]{2,1,0:T(1,128)}, u32[]{:S(2)}) copy-start(s32[2,1,256]{2,1,0:T(1,128)} %param.21) | copy-start | bytes 6148
  63.3 16.6 %copy-start.41 = (f32[384]{0:T(512)S(1)}, f32[384]{0:T(512)}, u32[]{:S(2)}) copy-start(f32[384]{0:T(512)} %param.29) | copy-start | bytes 4612
  63.3 17.2 %copy-start.42 = (f32[384]{0:T(512)S(1)}, f32[384]{0:T(512)}, u32[]{:S(2)}) copy-start(f32[384]{0:T(512)} %param.35) | copy-start | bytes 4612
  63.3 17.8 %copy-start.43 = (f32[384]{0:T(512)S(1)}, f32[384]{0:T(512)}, u32[]{:S(2)}) copy-start(f32[384]{0:T(512)} %param.36) | copy-start | bytes 4612
  69.8 1.0 copy-start.24
  174.7 2.0 copy-start.8
  178.9 37.2 %copy-start.18 = (bf16[768,384]{1,0:T(8,128)(2,1)S(1)}, bf16[768,384]{1,0:T(8,128)(2,1)}, u32[]{:S(2)}) copy-start(bf16[768,384]{1,0:T(8,128)(2,1)} %param.28) | copy-start | bytes 1769476
  178.9 37.2 %copy-start.30 = (bf16[160,384]{1,0:T(8,128)(2,1)S(1)}, bf16[160,384]{1,0:T(8,128)(2,1)}, u32[]{:S(2)}) copy-start(bf16[160,384]{1,0:T(8,128)(2,1)} %get-tuple-element.31) | copy-start | bytes 368644
  216.4 14.1 %copy-start.14 = (f32[160,768]{1,0:T(8,128)}, f32[160,768]{1,0:T(8,128)S(1)}, u32[]{:S(2)}) copy-start(f32[160,768]{1,0:T(8,128)S(1)} %fusion.65) | copy-start | bytes 1474564
  216.4 3.1 copy-start.7
  219.6 11.0 %copy-start.20 = (bf16[160,1536]{1,0:T(8,128)(2,1)}, bf16[160,1536]{1,0:T(8,128)(2,1)S(1)}, u32[]{:S(2)}) copy-start(bf16[160,1536]{1,0:T(8,128)(2,1)S(1)} %fusion.2) | copy-start | bytes 1474564
  219.6 9.0 %copy-start.3 = (f32[160,768]{1,0:T(8,128)S(1)}, f32[160,768]{1,0:T(8,128)}, u32[]{:S(2)}) copy-start(f32[160,768]{1,0:T(8,128)} %copy-done.2) | copy-start | bytes 1474564
  228.6 6.0 %copy-start.23 = (bf16[160,1152]{0,1:T(8,128)(2,1)S(1)}, bf16[160,1152]{0,1:T(8,128)(2,1)}, u32[]{:S(2)}) copy-start(bf16[160,1152]{0,1:T(8,128)(2,1)} %copy-done.22) | copy-start | bytes 1105924
  228.6 6.0 %copy-start.37 = (f32[6,160]{1,0:T(8,128)S(1)}, f32[6,160]{1,0:T(8,128)}, u32[]{:S(2)}) copy-start(f32[6,160]{1,0:T(8,128)} %copy-done.36) | copy-start | bytes 11524
  232.4 3.8 copy-start.15
  233.4 2.8 copy-start.26
  234.5 1.7 copy-start.32
  236.2 2.1 copy-start.45
  238.3 1.9 copy-start.28
  238.3 1.9 copy-start.29
  238.3 2.1 copy-start.5
  240.4 1.3 copy-start.10
  240.4 9.2 %copy-start.38 = (bf16[768]{0:T(1024)(128)(2,1)S(1)}, bf16[768]{0:T(1024)(128)(2,1)}, u32[]{:S(2)}) copy-start(bf16[768]{0:T(1024)(128)(2,1)} %get-tuple-element.69) | copy-start | bytes 4612
  240.4 9.4 %copy-start.35 = (f32[8,384]{1,0:T(8,128)S(1)}, f32[8,384]{1,0:T(8,128)}, u32[]{:S(2)}) copy-start(f32[8,384]{1,0:T(8,128)} %get-tuple-element.32) | copy-start | bytes 36868
  240.4 10.2 %copy-start.25 = (bf16[160,768]{1,0:T(8,128)(2,1)S(1)}, bf16[160,768]{1,0:T(8,128)(2,1)}, u32[]{:S(2)}) copy-start(bf16[160,768]{1,0:T(8,128)(2,1)} %copy-done.24) | copy-start | bytes 737284
  266.9 27.6 %copy-start.19 = (bf16[160,768]{1,0:T(8,128)(2,1)S(1)}, bf16[160,768]{1,0:T(8,128)(2,1)}, u32[]{:S(2)}) copy-start(bf16[160,768]{1,0:T(8,128)(2,1)} %swap_x_13.1) | copy-start | bytes 737284
  291.2 5.6 %copy-start.11 = (bf16[160,3,6,64]{0,3,2,1:T(8,128)(2,1)S(1)}, bf16[160,3,6,64]{0,3,2,1:T(8,128)(2,1)}, u32[]{:S(2)}) copy-start(bf16[160,3,6,64]{0,3,2,1:T(8,128)(2,1)} %copy-done.10) | copy-start | bytes 1105924
  298.7 4.6 %copy-start.13 = (bf16[160,1536]{1,0:T(8,128)(2,1)S(1)}, bf16[160,1536]{1,0:T(8,128)(2,1)}, u32[]{:S(2)}) copy-start(bf16[160,1536]{1,0:T(8,128)(2,1)} %copy-done.12) | copy-start | bytes 1474564
  301.8 3.3 copy-start.9
  416.5 21.5 %copy-start.21 = (f32[160,768]{1,0:T(8,128)S(1)}, f32[160,768]{1,0:T(8,128)}, u32[]{:S(2)}) copy-start(f32[160,768]{1,0:T(8,128)} %get-tuple-element.101) | copy-start | bytes 1474564
  442.4 15.1 %copy-start.1 = (bf16[384,768]{1,0:T(8,128)(2,1)S(1)}, bf16[384,768]{1,0:T(8,128)(2,1)}, u32[]{:S(2)}) copy-start(bf16[384,768]{1,0:T(8,128)(2,1)} %param.23) | copy-start | bytes 1769476

commit v3 on v2

--- a/solution.py
+++ b/solution.py
@@ -1,4 +1,5 @@
 import functools
+import itertools
 
 import jax
 import jax.numpy as jnp
@@ -44,33 +45,6 @@
     return pltpu.CompilerParams(
         collective_id=ident, has_side_effects=True, vmem_limit_bytes=LIMIT
     )
-
-
-def swap_kernel(kind, count, *refs):
-    ins, outs, (send_sem, recv_sem) = refs[:count], refs[count : 2 * count], refs[2 * count :]
-    s, d, m = place_of()
-    partner = (1 - s, d, m) if kind == "core" else (s, d, 1 - m)
-    greet([partner])
-    copies = [
-        send(ins[i], outs[i], send_sem.at[i], recv_sem.at[i], partner) for i in range(count)
-    ]
-    for copy in copies:
-        copy.start()
-    for copy in copies:
-        copy.wait()
-
-
-def swap(arrays, kind, ident):
-    count = len(arrays)
-    return pl.pallas_call(
-        functools.partial(swap_kernel, kind, count),
-        out_shape=[jax.ShapeDtypeStruct(a.shape, a.dtype) for a in arrays],
-        in_specs=[pl.BlockSpec(memory_space=pl.ANY)] * count,
-        out_specs=[pl.BlockSpec(memory_space=pl.ANY)] * count,
-        scratch_shapes=[pltpu.SemaphoreType.DMA((count,)), pltpu.SemaphoreType.DMA((count,))],
-        compiler_params=remote_params(ident),
-        name=f"swap_{kind}_{ident}",
-    )(*arrays)
 
 
 def route_kernel(x_ref, out_ref, send_sem, recv_sem, local_sem):
@@ -266,110 +240,6 @@
     return (lanes < HEAD, lanes >= HEAD)
 
 
-def attend_kernel(q_ref, k_ref, v_ref, o_ref, p_ref):
-    masks = head_masks()
-    k = k_ref[...]
-    v = v_ref[...]
-    for start, size in chunks_of(q_ref.shape[0], 128):
-        rows = pl.ds(start, size)
-        q = q_ref[rows] * jnp.asarray(HEAD**-0.5, B16)
-        halves = []
-        for head in range(2):
-            scores = dot_nt(jnp.where(masks[head], q, 0), k)
-            top = jnp.max(scores, -1, keepdims=True)
-            raised = jnp.exp(scores - top)
-            whole = jnp.sum(raised, -1, keepdims=True)
-            p = (raised * (1.0 / whole)).astype(B16)
-            p_ref[head, rows] = p
-            halves.append(dot_nn(p, v))
-        o_ref[rows] = jnp.where(masks[0], halves[0], halves[1]).astype(B16)
-
-
-def attend(q, k, v):
-    length, width = q.shape
-    keys = k.shape[0]
-    pairs = width // (2 * HEAD)
-    return pl.pallas_call(
-        attend_kernel,
-        grid=(pairs,),
-        out_shape=[
-            jax.ShapeDtypeStruct((length, width), B16),
-            jax.ShapeDtypeStruct((2 * pairs, length, keys), B16),
-        ],
-        in_specs=[
-            pl.BlockSpec((length, 2 * HEAD), lambda i: (0, i)),
-            pl.BlockSpec((keys, 2 * HEAD), lambda i: (0, i)),
-            pl.BlockSpec((keys, 2 * HEAD), lambda i: (0, i)),
-        ],
-        out_specs=[
-            pl.BlockSpec((length, 2 * HEAD), lambda i: (0, i)),
-            pl.BlockSpec((2, length, keys), lambda i: (i, 0, 0)),
-        ],
-        compiler_params=pltpu.CompilerParams(vmem_limit_bytes=LIMIT),
-        name="attend",
-    )(q, k, v)
-
-
-def attend_back_kernel(q_ref, k_ref, v_ref, o_ref, do_ref, p_ref, dq_ref, dk_ref, dv_ref, dk_t, dv_t):
-    masks = head_masks()
-    k = k_ref[...]
-    v = v_ref[...]
-    scale = HEAD**-0.5
-    for index, (start, size) in enumerate(chunks_of(q_ref.shape[0], 256)):
-        rows = pl.ds(start, size)
-        q = q_ref[rows]
-        do = do_ref[rows]
-        both = do.astype(F32) * o_ref[rows].astype(F32)
-        dq = []
-        for head in range(2):
-            do_head = jnp.where(masks[head], do, 0)
-            delta = jnp.sum(jnp.where(masks[head], both, 0.0), -1, keepdims=True)
-            p = p_ref[head, rows]
-            dp = dot_nt(do_head, v)
-            ds = (p.astype(F32) * (dp - delta)).astype(B16)
-            dq.append(dot_nn(ds, k))
-            feats = pl.ds(head * HEAD, HEAD)
-            dv_part = dot_tn(do[:, head * HEAD : (head + 1) * HEAD], p)
-            dk_part = dot_tn(q[:, head * HEAD : (head + 1) * HEAD], ds)
-            if index:
-                dv_part = dv_part + dv_t[feats]
-                dk_part = dk_part + dk_t[feats]
-            dv_t[feats] = dv_part
-            dk_t[feats] = dk_part
-        dq_ref[rows] = (jnp.where(masks[0], dq[0], dq[1]) * scale).astype(B16)
-    dk_ref[...] = (jnp.transpose(dk_t[...]) * scale).astype(dk_ref.dtype)
-    dv_ref[...] = jnp.transpose(dv_t[...]).astype(dv_ref.dtype)
-
-
-def attend_back(q, k, v, o, do, p):
-    length, width = q.shape
-    keys = k.shape[0]
-    pairs = width // (2 * HEAD)
-    short = pl.BlockSpec((length, 2 * HEAD), lambda i: (0, i))
-    long = pl.BlockSpec((keys, 2 * HEAD), lambda i: (0, i))
-    return pl.pallas_call(
-        attend_back_kernel,
-        grid=(pairs,),
-        out_shape=[
-            jax.ShapeDtypeStruct((length, width), B16),
-            jax.ShapeDtypeStruct((keys, width), F32),
-            jax.ShapeDtypeStruct((keys, width), F32),
-        ],
-        in_specs=[
-            short,
-            long,
-            long,
-            short,
-            short,
-            pl.BlockSpec((2, length, keys), lambda i: (i, 0, 0)),
-        ],
-        out_specs=[short, long, long],
-        scratch_shapes=[VMEM((2 * HEAD, keys), F32), VMEM((2 * HEAD, keys), F32)],
-        compiler_params=pltpu.CompilerParams(vmem_limit_bytes=LIMIT),
-        name="attend_back",
-    )(q, k, v, o, do, p)
-
-
 class Wire:
     def __init__(self, send_sem, recv_sem):
         self.send_sem, self.recv_sem, self.used = send_sem, recv_sem, 0
@@ -402,14 +272,14 @@
     return raised, scale, dot_nn(raised, v) * scale
 
 
-def dec_kernel(*refs):
+def dec_kernel(early, *refs):
     (
         vis_ref, cells_row, cells_col, pos_own, pos_far, mask_ref, gain1_ref, gain2_ref,
         qkv_own, qkv_far, out_own, out_far, up_hbm, down_hbm, cot_hbm,
-        dec_out, pos_out, dvis_out, grad_out, small_out,
-        w_up, w_down, cot, z1, unit1, a_ref, q_ref, keys, values, probs, stats,
+        routed, pos_out, dvis_out, grad_out, small_out,
+        dec_out, w_up, w_down, cot, z1, unit1, a_ref, q_ref, keys, values, probs, stats,
         o_ref, unit2, b_ref, h_ref, slope, z2, do_ref, flip, dkt, dvt, got_kv,
-        dvis_mine, dvis_near, dvis_far, local_sem, send_sem, recv_sem,
+        dvis_mine, dvis_near, dvis_far, free_sem, local_sem, send_sem, recv_sem,
     ) = refs
     s, d, m = place_of()
     sibling, facing = (1 - s, d, m), (s, d, 1 - m)
@@ -420,7 +290,8 @@
     wire = Wire(send_sem, recv_sem)
     scale = HEAD**-0.5
 
-    greet([sibling, facing])
+    beyond = (1 - s, d, 1 - m)
+    greet([sibling, facing, beyond])
 
     loads = [
         pltpu.make_async_copy(up_hbm, w_up.at[0], local_sem.at[0]),
@@ -554,6 +425,21 @@
 
     cut(z2[...] + dot_nn(h_ref[0], w_down[0]) + dot_nn(h_ref[1], w_down[1]), dec_out)
 
+    route_local = pltpu.make_async_copy(dec_out.at[s], routed.at[m], local_sem.at[4])
+    route_near = wire.copy(dec_out.at[1 - s], routed.at[m], sibling)
+    route_over = wire.copy(dec_out.at[s], routed.at[m], facing)
+    route_far = wire.copy(dec_out.at[1 - s], routed.at[m], beyond)
+
+    @pl.when(stays)
+    def _():
+        route_local.start()
+        route_near.start()
+
+    @pl.when(jnp.logical_not(stays))
+    def _():
+        route_over.start()
+        route_far.start()
+
     @pl.when(stays)
     def _():
         cot_load.wait()
@@ -580,6 +466,18 @@
         grad_out[side, 1, :, cols] = dot_nn(b_flip[...], grad_u).astype(B16)
 
     each(2 * steps, down)
+    if early:
+        rows = wide // 2
+        mine_grads = pl.ds(pl.multiple_of(s * rows, 16), rows)
+        away_grads = pl.ds(pl.multiple_of((1 - s) * rows, 16), rows)
+        for partner in (sibling, facing):
+            pl.semaphore_signal(free_sem, inc=1, device_id=partner, device_id_type=MESH)
+        pl.semaphore_wait(free_sem, 2)
+        near = {}
+        for side, t in ((1, 1), (1, 2), (0, 1), (0, 2)):
+            held = h_ref.at[0, pl.ds((side * 2 + t - 1) * rows, rows)]
+            near[side, t] = (held, wire.copy(grad_out.at[side, t, away_grads], held, sibling))
+            near[side, t][1].start()
     z1[...] = dot_nt(slope[0], w_up[0]) + dot_nt(slope[1], w_up[1])
 
     def back_norm(grad, unit, inverse, gain):
@@ -608,6 +506,16 @@
     for side, weight in enumerate((out_own, out_far)):
         grad_out[side, 0, :, pl.ds(3 * third, third)] = dot_nn(flip[0], o_ref[side]).astype(B16)
         do_ref[side] = dot_nt(grad_a, weight[...]).astype(B16)
+
+    if early:
+        across = {}
+        for t in (1, 2):
+            held, copy = near[1, t]
+            copy.wait()
+            held[...] = (held[...].astype(F32) + grad_out[1, t, mine_grads].astype(F32)).astype(B16)
+            got = h_ref.at[1, pl.ds((t - 1) * rows, rows)]
+            across[t] = (got, wire.copy(held, got, facing))
+            across[t][1].start()
 
     def attend_back_side(side):
         for index, (start, size) in enumerate(chunks_of(length, 256)):
@@ -660,6 +568,17 @@
         for copy in copies:
             copy.start()
 
+    if early:
+        for t in (1, 2):
+            held, copy = near[0, t]
+            copy.wait()
+            across[t][1].wait()
+            grad_out[0, t, mine_grads] = (
+                held[...].astype(F32)
+                + grad_out[0, t, mine_grads].astype(F32)
+                + across[t][0][...].astype(F32)
+            ).astype(B16)
+
     a_flip = flip.at[0]
     a_flip[...] = transposed(a_ref[...])
     total = None
@@ -701,21 +620,28 @@
     near.start()
     near.wait()
     dvis_mine[...] = (dvis_mine[...].astype(F32) + dvis_near[...].astype(F32)).astype(B16)
-    beyond = wire.copy(dvis_mine, dvis_far, facing)
+    dvis_over = wire.copy(dvis_mine, dvis_far, facing)
 
     @pl.when(stays)
     def _():
-        beyond.start()
+        dvis_over.start()
         dvis_out[...] = dvis_mine[...]
-        beyond.wait_send()
+        dvis_over.wait_send()
+        route_local.wait()
+        route_near.wait_send()
+        route_over.wait_recv()
 
     @pl.when(jnp.logical_not(stays))
     def _():
-        beyond.wait_recv()
+        dvis_over.wait_recv()
         dvis_out[...] = dvis_far[...]
-
-
-def decoder(vis, cells, pos_own, pos_far, mask, gains, weights, cot, ident):
+        route_over.wait_send()
+        route_far.wait_send()
+        route_near.wait_recv()
+        route_far.wait_recv()
+
+
+def decoder(early, vis, cells, pos_own, pos_far, mask, gains, weights, cot, ident):
     qkv_own, qkv_far, out_own, out_far, up, down = weights
     length, wide = pos_own.shape
     used = vis.shape[0]
@@ -727,7 +653,7 @@
     whole = pl.BlockSpec(memory_space=VMEM)
     there = pl.BlockSpec(memory_space=pl.ANY)
     return pl.pallas_call(
-        dec_kernel,
+        functools.partial(dec_kernel, early),
         out_shape=[
             jax.ShapeDtypeStruct((2, length, third), B16),
             jax.ShapeDtypeStruct((2, length, third), B16),
@@ -736,8 +662,9 @@
             jax.ShapeDtypeStruct((8, wide), F32),
         ],
         in_specs=[whole] * 3 + [there] + [whole] * 8 + [there] * 3,
-        out_specs=[whole] * 5,
+        out_specs=[there] + [whole] * 4,
         scratch_shapes=[
+            VMEM((2, length, third), B16),
             VMEM((2, wide, hidden), B16),
             VMEM((2, hidden, wide), B16),
             VMEM((length, wide), B16),
@@ -763,9 +690,10 @@
             VMEM((used, wide), B16),
             VMEM((used, wide), B16),
             VMEM((used, wide), B16),
-            pltpu.SemaphoreType.DMA((4,)),
-            pltpu.SemaphoreType.DMA((16,)),
-            pltpu.SemaphoreType.DMA((16,)),
+            pltpu.SemaphoreType.REGULAR,
+            pltpu.SemaphoreType.DMA((5,)),
+            pltpu.SemaphoreType.DMA((32,)),
+            pltpu.SemaphoreType.DMA((32,)),
         ],
         compiler_params=pltpu.CompilerParams(
             collective_id=ident, has_side_effects=True, vmem_limit_bytes=63 * 1024 * 1024
@@ -790,54 +718,6 @@
     )
 
 
-def normed(z, gain):
-    centre = z - jnp.mean(z, -1, keepdims=True)
-    inverse = lax.rsqrt(jnp.mean(centre * centre, -1, keepdims=True) + EPS)
-    unit = centre * inverse
-    return unit, inverse, (unit * gain).astype(B16)
-
-
-def norm_back(grad, unit, inverse, gain):
-    scaled = grad * gain
-    return inverse * (
-        scaled
-        - jnp.mean(scaled, -1, keepdims=True)
-        - unit * jnp.mean(scaled * unit, -1, keepdims=True)
-    )
-
-
-def gelu(u):
-    return 0.5 * u * (1.0 + lax.erf(u * 0.5**0.5))
-
-
-def gelu_slope(u):
-    return 0.5 * (1.0 + lax.erf(u * 0.5**0.5)) + u * jnp.exp(-0.5 * u * u) * (
-        0.5 / jnp.pi
-    ) ** 0.5
-
-
-def small_attend(triple, length):
-    rows = triple.shape[0]
-    q, k, v = (triple[:, i] for i in range(3))
-    scores = jnp.einsum("qhd,khd->hqk", q, k, preferred_element_type=F32) * HEAD**-0.5
-    scores = jnp.where(jnp.arange(rows)[None, None, :] < length, scores, NEG)
-    p = jax.nn.softmax(scores, axis=-1)
-    o = jnp.einsum("hqk,khd->qhd", p.astype(B16), v, preferred_element_type=F32)
-    return p, o.reshape(rows, -1).astype(B16)
-
-
-def small_attend_back(triple, p, do):
-    q, k, v = (triple[:, i] for i in range(3))
-    do = do.reshape(q.shape)
-    dp = jnp.einsum("qhd,khd->hqk", do, v, preferred_element_type=F32)
-    ds = (p * (dp - jnp.sum(p * dp, -1, keepdims=True))).astype(B16)
-    scale = HEAD**-0.5
-    dq = jnp.einsum("hqk,khd->qhd", ds, k, preferred_element_type=F32) * scale
-    dk = jnp.einsum("hqk,qhd->khd", ds, q, preferred_element_type=F32) * scale
-    dv = jnp.einsum("hqk,qhd->khd", p.astype(B16), do, preferred_element_type=F32)
-    return jnp.stack([dq, dk, dv], 1).astype(B16).reshape(q.shape[0], -1)
-
-
 def pack(grad, owners):
     rows, cols = grad.shape
     own = rows // owners
@@ -855,6 +735,762 @@
 
 def pick(pair, index):
     return lax.dynamic_index_in_dim(pair, index, 0, keepdims=False)
+
+
+def load(src, dst, sem):
+    copy = pltpu.make_async_copy(src, dst, sem)
+    copy.start()
+    return copy
+
+
+def enc_kernel(*refs):
+    (
+        length_ref, tok_hbm, qkv_hbm, out_hbm, up_hbm, down_hbm, bridge_ref, gain1_ref, gain2_ref,
+        pos_hbm, dqkv_hbm, dout_hbm,
+        vis_out, dqkv_far, dout_far, pos_far, unit1, unit2, stats, a_ref, triple, probs, o_ref, b_ref,
+        slope, h_ref, enc_half,
+        x_ref, qkv, w_out, w_up, w_down, z2, part_ref, part_far, enc_ref, pos_full, pos_half,
+        local_sem, send_sem, recv_sem,
+    ) = refs
+    s, d, m = place_of()
+    sibling, facing = (1 - s, d, m), (s, d, 1 - m)
+    stays = s == m
+    used, wide = x_ref.shape
+    half = tok_hbm.shape[1]
+    rest = used - half
+    wire = Wire(send_sem, recv_sem)
+
+    greet([sibling, facing])
+    first, last = pl.ds(0, half), pl.ds(half, rest)
+    tok_first = wire.copy(tok_hbm.at[s], x_ref.at[first], facing)
+    tok_last = wire.copy(tok_hbm.at[s, pl.ds(0, rest)], x_ref.at[last], facing)
+    own_first = pltpu.make_async_copy(tok_hbm.at[s], x_ref.at[first], local_sem.at[0])
+    own_last = pltpu.make_async_copy(
+        tok_hbm.at[s, pl.ds(0, rest)], x_ref.at[last], local_sem.at[0]
+    )
+
+    @pl.when(m == 0)
+    def _():
+        tok_first.start()
+        own_first.start()
+
+    @pl.when(m == 1)
+    def _():
+        tok_last.start()
+        own_last.start()
+
+    loads = [
+        load(hbm, held, local_sem.at[i + 1])
+        for i, (hbm, held) in enumerate(
+            ((qkv_hbm, qkv), (out_hbm, w_out), (up_hbm, w_up), (down_hbm, w_down))
+        )
+    ]
+    pos_load = load(pos_hbm, pos_full, local_sem.at[5])
+    over, share = [], []
+    for hbm, held in ((dqkv_hbm, dqkv_far), (dout_hbm, dout_far)):
+        at = (slice(None),) * (len(hbm.shape) - 2)
+        size = hbm.shape[-2] // 2
+        mine = at + (pl.ds(s * size, size),)
+        over.append(wire.copy(hbm.at[mine], held.at[mine], facing))
+        share.append(wire.copy(held.at[mine], held.at[mine], sibling))
+
+    @pl.when(m == 0)
+    def _():
+        own_first.wait()
+        tok_first.wait_send()
+        tok_last.wait_recv()
+
+    @pl.when(m == 1)
+    def _():
+        own_last.wait()
+        tok_last.wait_send()
+        tok_first.wait_recv()
+
+    for copy in over:
+        copy.start()
+
+    lane = lax.broadcasted_iota(jnp.int32, (1, 128), 1)
+
+    unit, inverse = norm_of(x_ref[...].astype(F32))
+    unit1[...] = unit
+    stats[...] = jnp.where(lane == 0, inverse, 0.0)
+    a = (unit * gain1_ref[...]).astype(B16)
+    a_ref[...] = a
+    loads[0].wait()
+    for slot in range(3):
+        triple[slot] = dot_nn(a, qkv[slot]).astype(B16)
+
+    valid = lax.broadcasted_iota(jnp.int32, (1, used), 1) < length_ref[s]
+    masks = head_masks()
+    for pair in range(triple.shape[2] // (2 * HEAD)):
+        feats = pl.ds(pair * 2 * HEAD, 2 * HEAD)
+        q, k, v = (triple[slot, :, feats] for slot in range(3))
+        halves = []
+        for head in range(2):
+            scores = dot_nt(jnp.where(masks[head], q, 0), k) * HEAD**-0.5
+            scores = jnp.where(valid, scores, NEG)
+            raised = jnp.exp(scores - jnp.max(scores, -1, keepdims=True))
+            p = (raised / jnp.sum(raised, -1, keepdims=True)).astype(B16)
+            probs[2 * pair + head] = p
+            halves.append(dot_nn(p, v))
+        o_ref[:, feats] = jnp.where(masks[0], halves[0], halves[1]).astype(B16)
+
+    loads[1].wait()
+    part = dot_nn(o_ref[...], w_out[...])
+    part_ref[0] = part.astype(B16)
+    attn = wire.copy(part_ref.at[0], part_far.at[0], facing)
+    attn.start()
+    z2[...] = x_ref[...].astype(F32) + part
+
+    pos_load.wait()
+    pos_over = wire.copy(pos_half, pos_far, facing)
+
+    @pl.when(stays)
+    def _():
+        pos_half[...] = pos_full[...].astype(B16)
+        pos_over.start()
+
+    attn.wait()
+    z = z2[...] + part_far[0].astype(F32)
+    z2[...] = z
+    unit, inverse = norm_of(z)
+    unit2[...] = unit
+    stats[...] = jnp.where(lane == 1, inverse, stats[...])
+    b = (unit * gain2_ref[...]).astype(B16)
+    b_ref[...] = b
+    loads[2].wait()
+    step = 512
+
+    def up(i):
+        cols = pl.ds(pl.multiple_of(i * step, step), step)
+        u = dot_nn(b_ref[...], w_up[:, cols])
+        phi = 0.5 + 0.5 * lax.erf(u * 0.5**0.5)
+        h_ref[:, cols] = (u * phi).astype(B16)
+        bell = jnp.exp(u * u * -0.5) * (0.5 / jnp.pi) ** 0.5
+        slope[:, cols] = (phi + u * bell).astype(B16)
+
+    each(w_up.shape[1] // step, up)
+    loads[3].wait()
+    part = dot_nn(h_ref[...], w_down[...])
+    z2[...] = z2[...] + part
+    part_ref[1] = part.astype(B16)
+    mlp = wire.copy(part_ref.at[1], part_far.at[1], facing)
+    vis_near = wire.copy(vis_out, vis_out, sibling)
+    mid = wide // 2
+    enc_over = wire.copy(
+        enc_ref.at[:, pl.ds(pl.multiple_of((1 - m) * mid, 128), mid)], enc_half, facing
+    )
+
+    @pl.when(stays)
+    def _():
+        mlp.wait_recv()
+        enc = (z2[...] + part_far[1].astype(F32)).astype(B16)
+        enc_ref[...] = enc
+        enc_over.start()
+        vis_out[...] = dot_nn(enc, bridge_ref[...]).astype(B16)
+        vis_near.start()
+        enc_half[...] = enc_ref[:, pl.ds(pl.multiple_of(m * mid, 128), mid)]
+
+    @pl.when(jnp.logical_not(stays))
+    def _():
+        mlp.start()
+
+    for copy, other in zip(over, share):
+        copy.wait()
+        other.start()
+
+    @pl.when(stays)
+    def _():
+        vis_near.wait_send()
+        enc_over.wait_send()
+        pos_over.wait_send()
+
+    @pl.when(jnp.logical_not(stays))
+    def _():
+        mlp.wait_send()
+        vis_near.wait_recv()
+        enc_over.wait_recv()
+        pos_over.wait_recv()
+
+    for copy in share:
+        copy.wait()
+
+
+def encoder(lengths, tokens, weights, bridge, gains, pos, dqkv, dout, used, ident):
+    qkv, out, up, down = weights
+    wide = tokens.shape[2]
+    feats = qkv.shape[2]
+    hidden = up.shape[1]
+    whole = pl.BlockSpec(memory_space=VMEM)
+    there = pl.BlockSpec(memory_space=pl.ANY)
+    shape = jax.ShapeDtypeStruct
+    outs = [
+        (shape((used, dout.shape[1]), B16), whole),
+        (shape(dqkv.shape, B16), there),
+        (shape(dout.shape, B16), there),
+        (shape(pos.shape, B16), there),
+        (shape((used, wide), F32), whole),
+        (shape((used, wide), F32), whole),
+        (shape((used, 128), F32), whole),
+        (shape((used, wide), B16), whole),
+        (shape((3, used, feats), B16), whole),
+        (shape((feats // HEAD, used, used), B16), whole),
+        (shape((used, feats), B16), whole),
+        (shape((used, wide), B16), whole),
+        (shape((used, hidden), B16), whole),
+        (shape((used, hidden), B16), whole),
+        (shape((used, wide // 2), B16), whole),
+    ]
+    return pl.pallas_call(
+        enc_kernel,
+        out_shape=[item for item, _ in outs],
+        in_specs=[pl.BlockSpec(memory_space=pltpu.SMEM)]
+        + [there] * 5
+        + [whole] * 3
+        + [there] * 3,
+        out_specs=[spec for _, spec in outs],
+        scratch_shapes=[
+            VMEM((used, wide), B16),
+            VMEM(qkv.shape, B16),
+            VMEM(out.shape, B16),
+            VMEM(up.shape, B16),
+            VMEM(down.shape, B16),
+            VMEM((used, wide), F32),
+            VMEM((2, used, wide), B16),
+            VMEM((2, used, wide), B16),
+            VMEM((used, wide), B16),
+            VMEM(pos.shape, F32),
+            VMEM(pos.shape, B16),
+            pltpu.SemaphoreType.DMA((6,)),
+            pltpu.SemaphoreType.DMA((16,)),
+            pltpu.SemaphoreType.DMA((16,)),
+        ],
+        compiler_params=remote_params(ident),
+        name="encoder",
+    )(
+        lengths, tokens, qkv, out, up, down, bridge, gains[0][None, :], gains[1][None, :],
+        pos, dqkv, dout,
+    )
+
+
+class Fold:
+    def __init__(self, wire, me, held, inbox, lanes, order, rows_of, device_of, last):
+        self.held, self.inbox, self.lanes = held, inbox, lanes
+        self.rounds = []
+        slot = 0
+        for k, axis in enumerate(order):
+            rest = order[k + 1 :]
+            other = dict(me)
+            other[axis] = 1 - me[axis]
+            copies = []
+            for bits in itertools.product((0, 1), repeat=len(rest)):
+                mine, theirs = dict(me, **dict(zip(rest, bits))), dict(other, **dict(zip(rest, bits)))
+                copy = wire.copy(
+                    held.at[rows_of(theirs), lanes], inbox.at[slot, :, lanes], device_of(other)
+                )
+                copies.append((copy, rows_of(mine), slot))
+                slot += 1
+            self.rounds.append(copies)
+        self.mine = rows_of(me)
+        if last:
+            other = dict(me, y=1 - me["y"])
+            copy = wire.copy(held.at[self.mine, lanes], inbox.at[slot, :, lanes], device_of(other))
+            self.rounds.append([(copy, self.mine, slot)])
+
+    def start(self, k):
+        for copy, _, _ in self.rounds[k]:
+            copy.start()
+
+    def total(self, rows, slot):
+        return self.held[rows, self.lanes].astype(F32) + self.inbox[slot, :, self.lanes].astype(F32)
+
+    def step(self, k):
+        for copy, rows, slot in self.rounds[k]:
+            copy.wait()
+            self.held[rows, self.lanes] = self.total(rows, slot).astype(B16)
+        self.start(k + 1)
+
+    def end(self):
+        ((copy, rows, slot),) = self.rounds[-1]
+        copy.wait()
+        return self.total(rows, slot)
+
+
+def back_kernel(cube, *refs):
+    (
+        dvis_ref, bridge_ref, gain1_ref, gain2_ref, unit1, unit2, stats, a_ref, triple, probs, o_ref,
+        b_ref, slope, h_ref, enc_half, small_dec, qkv_hbm, out_hbm, up_hbm, down_hbm, *refs,
+    ) = refs
+    if cube:
+        (
+            dec_hbm, pos_hbm,
+            tok_out, small_out, enc_out, dec_out, pos_out, bridge_all,
+            near, inbox, dec_raw, dec_near, dec_over, dec_held, dec_box, pos_got, pos_held, pos_box,
+            bridge_near, bridge_box, small_box, grads, bridge_grad, *refs,
+        ) = refs
+    else:
+        tok_out, small_out, grads, bridge_grad, *refs = refs
+    (
+        qkv, w_out, w_up, w_down, gu, dy, part, part_far, dz, da_ref, do_ref, dqkv, flip, tok_part,
+        local_sem, send_sem, recv_sem,
+    ) = refs
+    s, d, m = place_of()
+    sibling, facing = (1 - s, d, m), (s, d, 1 - m)
+    stays = s == m
+    used, wide = unit1.shape
+    feats = o_ref.shape[1]
+    hidden = h_ref.shape[1]
+    half = tok_part.shape[1]
+    rest = used - half
+    wire = Wire(send_sem, recv_sem)
+    section = wide // 2
+
+    if cube:
+        z = d // 2
+        me = {"y": lax.rem(d, 2), "b": z // 2, "a": lax.rem(z + z // 2, 2)}
+
+        def z_of(c):
+            return lax.rem(c["a"] + c["b"], 2) + 2 * c["b"]
+
+        def device_of(c):
+            return (s, 2 * z_of(c) + c["y"], m)
+
+        def rows_eight(c):
+            return pl.ds(pl.multiple_of((2 * z_of(c) + c["y"]) * 48, 16), 48)
+
+        def rows_four(c):
+            return pl.ds(pl.multiple_of(z_of(c) * 48, 16), 48)
+
+        near_chips = [device_of(dict(me, **{axis: 1 - me[axis]})) for axis in "yab"]
+        across = lax.rem(z_of(me) + 2, 4)
+        more = [(s, 2 * across + me["y"], m)] + [
+            (s, 2 * lax.rem(z + k, 4) + me["y"], 1 - m) for k in (1, 2, 3)
+        ]
+        greet([sibling, facing, (1 - s, d, 1 - m)] + near_chips + more)
+    else:
+        greet([sibling, facing])
+
+    loads = [
+        load(hbm, held, local_sem.at[i])
+        for i, (hbm, held) in enumerate(
+            ((down_hbm, w_down), (up_hbm, w_up), (out_hbm, w_out), (qkv_hbm, qkv))
+        )
+    ]
+
+    if cube:
+        route_local = pltpu.make_async_copy(pos_hbm.at[s], pos_got.at[m], local_sem.at[4])
+        route_near = wire.copy(pos_hbm.at[1 - s], pos_got.at[m], sibling)
+        route_over = wire.copy(pos_hbm.at[s], pos_got.at[m], facing)
+        route_far = wire.copy(pos_hbm.at[1 - s], pos_got.at[m], (1 - s, d, 1 - m))
+
+        @pl.when(stays)
+        def _():
+            route_local.start()
+            route_near.start()
+
+        @pl.when(jnp.logical_not(stays))
+        def _():
+            route_over.start()
+            route_far.start()
+
+        dec_rows = dec_raw.shape[1] // 2
+        mine = pl.ds(pl.multiple_of(s * dec_rows, 16), dec_rows)
+        away = pl.ds(pl.multiple_of((1 - s) * dec_rows, 16), dec_rows)
+        raw_load = load(dec_hbm.at[:, 0], dec_raw, local_sem.at[5])
+        span = dec_raw.shape[2]
+        sum_loads = [
+            load(dec_hbm.at[0, t, mine], dec_held.at[:, pl.ds(t * span, span)], local_sem.at[5 + t])
+            for t in (1, 2)
+        ]
+        raw_load.wait()
+        dec_pair = [
+            wire.copy(dec_raw.at[side, away], dec_near.at[side], sibling) for side in range(2)
+        ]
+        for copy in reversed(dec_pair):
+            copy.start()
+
+    def transposed(value):
+        return jnp.transpose(value.astype(F32)).astype(B16)
+
+    dvis = dvis_ref[...]
+    grad = dot_nt(dvis, bridge_ref[...])
+    dy[...] = grad
+    dm = grad.astype(B16)
+    da_ref[...] = dm
+    flip[0] = transposed(dm)
+    flip[1] = transposed(b_ref[...])
+    bridge_grad[...] = dot_tn(enc_half[...], dvis).astype(B16)
+    if cube:
+        bridge_rows = bridge_near.shape[0]
+        bridge_pair = wire.copy(
+            bridge_grad.at[pl.ds(pl.multiple_of((1 - s) * bridge_rows, 16), bridge_rows)],
+            bridge_near,
+            sibling,
+        )
+        bridge_pair.start()
+        dec_pair[1].wait()
+        dec_near[1] = (dec_near[1].astype(F32) + dec_raw[1, mine].astype(F32)).astype(B16)
+        dec_across = wire.copy(dec_near.at[1], dec_over, facing)
+        dec_across.start()
+
+    loads[0].wait()
+    step = 512
+    first_up, first_down = 3 * feats + feats, 3 * feats + feats + hidden
+
+    def down(i):
+        cols = pl.ds(pl.multiple_of(i * step, step), step)
+        grads[:, pl.ds(pl.multiple_of(first_down + i * step, 128), step)] = dot_nn(
+            flip[0], h_ref[:, cols]
+        ).astype(B16)
+        grad_u = dot_nt(da_ref[...], w_down[cols, :]) * slope[:, cols].astype(F32)
+        grad_u = grad_u.astype(B16)
+        gu[:, cols] = grad_u
+        grads[:, pl.ds(pl.multiple_of(first_up + i * step, 128), step)] = dot_nn(
+            flip[1], grad_u
+        ).astype(B16)
+
+    each(hidden // step, down)
+
+    if cube:
+        attn_lanes, mlp_lanes = pl.ds(0, first_up), pl.ds(first_up, 2 * hidden)
+        theirs = pl.ds(pl.multiple_of((1 - s) * section, 16), section)
+        mlp_pair = wire.copy(grads.at[theirs, mlp_lanes], near.at[:, mlp_lanes], sibling)
+        mlp_pair.start()
+
+    loads[1].wait()
+    grad = dot_nt(gu[...], w_up[...])
+    part[...] = grad.astype(B16)
+    over = wire.copy(part, part_far.at[0], facing)
+    over.start()
+    dz[...] = grad
+    gain2_grad = jnp.sum(grad * unit2[...], 0, keepdims=True)
+
+    if cube:
+        def pair_sum(lanes):
+            def body(i):
+                rows = pl.ds(pl.multiple_of(i * 48, 16), 48)
+                from_rows = pl.ds(pl.multiple_of(s * section + i * 48, 16), 48)
+                near[rows, lanes] = (
+                    near[rows, lanes].astype(F32) + grads[from_rows, lanes].astype(F32)
+                ).astype(B16)
+
+            each(section // 48, body)
+
+        orders = (("y", "a", "b"), ("a", "b", "y"), ("b", "y", "a"))
+
+        def folds_of(first, size):
+            third = size // 3
+            return [
+                Fold(
+                    wire, me, near, inbox, pl.ds(first + i * third, third), orders[i], rows_eight,
+                    device_of, False,
+                )
+                for i in range(3)
+            ]
+
+        mlp_folds = folds_of(first_up, 2 * hidden)
+        mlp_pair.wait()
+        pair_sum(mlp_lanes)
+        for fold in mlp_folds:
+            fold.start(0)
+
+        dec_pair[0].wait()
+        dec_across.wait()
+        dec_held[:, pl.ds(0, span)] = (
+            dec_near[0].astype(F32) + dec_raw[0, mine].astype(F32) + dec_over[...].astype(F32)
+        ).astype(B16)
+        for copy in sum_loads:
+            copy.wait()
+        side_folds = [
+            Fold(
+                wire, me, dec_held, dec_box, pl.ds(i * (3 * span // 2), 3 * span // 2), order,
+                rows_four, device_of, True,
+            )
+            for i, order in enumerate((("a", "b"), ("b", "a")))
+        ]
+        bridge_pair.wait()
+        bridge_near[...] = (
+            bridge_near[...].astype(F32)
+            + bridge_grad[
+                pl.ds(pl.multiple_of(s * bridge_rows, 16), bridge_rows)
+            ].astype(F32)
+        ).astype(B16)
+        side_folds.append(
+            Fold(
+                wire, me, bridge_near, bridge_box, pl.ds(0, bridge_near.shape[1]), ("a", "b"),
+                rows_four, device_of, True,
+            )
+        )
+
+        @pl.when(stays)
+        def _():
+            route_local.wait()
+            route_near.wait_send()
+            route_over.wait_recv()
+
+        @pl.when(jnp.logical_not(stays))
+        def _():
+            route_over.wait_send()
+            route_far.wait_send()
+            route_near.wait_recv()
+            route_far.wait_recv()
+
+        pos_held[...] = transposed(pos_got[0].astype(F32) + pos_got[1].astype(F32))
+        side_folds.append(
+            Fold(
+                wire, me, pos_held, pos_box, pl.ds(0, pos_held.shape[1]), ("b", "a"), rows_four,
+                device_of, True,
+            )
+        )
+        for fold in side_folds:
+            fold.start(0)
+
+    def back_norm(grad, unit, inverse, gain):
+        scaled = grad * gain
+        mean = jnp.mean(scaled, -1, keepdims=True)
+        tilt = jnp.mean(scaled * unit, -1, keepdims=True)
+        return inverse * (scaled - mean - unit * tilt)
+
+    over.wait()
+    whole = dz[...] + part_far[0].astype(F32)
+    dz2 = dy[...] + back_norm(whole, unit2[...], stats[:, 1:2], gain2_ref[...])
+    dy[...] = dz2
+    grad_a = dz2.astype(B16)
+    da_ref[...] = grad_a
+    flip[0] = transposed(grad_a)
+    loads[2].wait()
+    grads[:, pl.ds(3 * feats, feats)] = dot_nn(flip[0], o_ref[...]).astype(B16)
+    do_ref[...] = dot_nt(grad_a, w_out[...]).astype(B16)
+
+    if cube:
+        for fold in side_folds:
+            fold.step(0)
+
+    masks = head_masks()
+    scale = HEAD**-0.5
+    for pair in range(feats // (2 * HEAD)):
+        at = pl.ds(pair * 2 * HEAD, 2 * HEAD)
+        q, k, v = (triple[slot, :, at] for slot in range(3))
+        do = do_ref[:, at]
+        both = do.astype(F32) * o_ref[:, at].astype(F32)
+        parts = []
+        for head in range(2):
+            delta = jnp.sum(jnp.where(masks[head], both, 0.0), -1, keepdims=True)
+            do_head = jnp.where(masks[head], do, 0)
+            p = probs[2 * pair + head]
+            ds = (p.astype(F32) * (dot_nt(do_head, v) - delta)).astype(B16)
+            parts.append((dot_nn(ds, k) * scale, dot_tn(ds, q) * scale, dot_tn(p, do)))
+        for slot in range(3):
+            dqkv[slot, :, at] = jnp.where(masks[0], parts[0][slot], parts[1][slot]).astype(B16)
+
+    flip[1] = transposed(a_ref[...])
+    loads[3].wait()
+    total = None
+    for slot in range(3):
+        grads[:, pl.ds(slot * feats, feats)] = dot_nn(flip[1], dqkv[slot]).astype(B16)
+        term = dot_nt(dqkv[slot], qkv[slot])
+        total = term if total is None else total + term
+    part[...] = total.astype(B16)
+    dz[...] = total
+    gain1_grad = jnp.sum(total * unit1[...], 0, keepdims=True)
+    first, last = pl.ds(0, half), pl.ds(half, rest)
+    over_first = wire.copy(part.at[first], part_far.at[1, first], facing)
+    over_last = wire.copy(part.at[last], part_far.at[1, last], facing)
+
+    @pl.when(m == 0)
+    def _():
+        over_last.start()
+
+    @pl.when(m == 1)
+    def _():
+        over_first.start()
+
+    small_out[...] = jnp.zeros(small_out.shape, F32)
+    row = 0
+    for value in (
+        gain1_grad, gain2_grad, small_dec[0:1], small_dec[1:2], small_dec[2:3],
+    ):
+        for i in range(value.shape[1] // 128):
+            small_out[row : row + 1] = value[:, i * 128 : (i + 1) * 128]
+            row += 1
+
+    if cube:
+        attn_pair = wire.copy(grads.at[theirs, attn_lanes], near.at[:, attn_lanes], sibling)
+        attn_pair.start()
+
+        small_steps = [sibling, facing] + near_chips
+        small_copies = [
+            wire.copy(small_out, small_box.at[i], partner) for i, partner in enumerate(small_steps)
+        ]
+
+        def small_step(i):
+            small_copies[i].wait()
+            small_out[...] = small_out[...] + small_box[i]
+            if i + 1 < len(small_copies):
+                small_copies[i + 1].start()
+
+        small_copies[0].start()
+        for fold in mlp_folds:
+            fold.step(0)
+        for fold in side_folds:
+            fold.step(1)
+        small_step(0)
+
+    def finish(rows, size):
+        whole = dz[rows] + part_far[1, rows].astype(F32)
+        unit = unit1[rows]
+        grad = dy[rows] + back_norm(whole, unit, stats[rows][:, 0:1], gain1_ref[...])
+        for side in range(2):
+            tok_part[side, pl.ds(0, size)] = grad[:, side * section : (side + 1) * section]
+
+    @pl.when(m == 0)
+    def _():
+        over_last.wait_send()
+        over_first.wait_recv()
+        finish(first, half)
+
+    @pl.when(m == 1)
+    def _():
+        over_first.wait_send()
+        over_last.wait_recv()
+        tok_part[...] = jnp.zeros(tok_part.shape, F32)
+        finish(last, rest)
+
+    tok_pair = wire.copy(tok_part.at[1 - s], tok_out.at[s], sibling)
+    tok_pair.start()
+    tok_out[s] = tok_part[s]
+
+    if cube:
+        attn_folds = folds_of(0, first_up)
+        attn_pair.wait()
+        pair_sum(attn_lanes)
+        for fold in attn_folds:
+            fold.start(0)
+        small_step(1)
+
+        def own_rows(value, out):
+            @pl.when(me["y"] == 0)
+            def _():
+                out[...] = value[:24]
+
+            @pl.when(me["y"] == 1)
+            def _():
+                out[...] = value[24:]
+
+        slot = (s * 4 + z) * 2 + m
+        bridge_all[slot] = side_folds[2].end().astype(B16)
+        spread = [
+            wire.copy(bridge_all.at[slot], bridge_all.at[slot], partner)
+            for partner in [facing]
+            + [
+                (s, 2 * lax.rem(z + k, 4) + me["y"], lax.rem(m + side, 2))
+                for k in (1, 2, 3)
+                for side in range(2)
+            ]
+        ]
+        for copy in spread:
+            copy.start()
+        for i in range(2):
+            own = pl.ds(i * (3 * span // 2), 3 * span // 2)
+            own_rows(side_folds[i].end(), dec_out.at[:, own])
+        own_rows(side_folds[3].end(), pos_out)
+        for fold in mlp_folds:
+            fold.step(1)
+        for fold in attn_folds:
+            fold.step(0)
+        small_step(2)
+        for copy in spread:
+            copy.wait()
+        ours = pl.ds(s * 8, 8)
+        bridge_pair_all = wire.copy(bridge_all.at[ours], bridge_all.at[ours], sibling)
+        bridge_pair_all.start()
+        for fold in mlp_folds:
+            enc_out[:, fold.lanes] = fold.end()
+        for fold in attn_folds:
+            fold.step(1)
+        small_step(3)
+        for fold in attn_folds:
+            enc_out[:, fold.lanes] = fold.end()
+        small_step(4)
+        bridge_pair_all.wait()
+
+    tok_pair.wait()
+
+
+def back(cube, dvis, bridge, gains, saved, small_dec, weights, dec_grads, pos_parts, half, ident):
+    unit1, unit2, stats, a, triple, probs, o, b, slope, h, enc_half = saved
+    qkv, out, up, down = weights
+    used, wide = unit1.shape
+    feats, hidden = o.shape[1], h.shape[1]
+    cols = 4 * feats + 2 * hidden
+    narrow = bridge.shape[1]
+    whole = pl.BlockSpec(memory_space=VMEM)
+    there = pl.BlockSpec(memory_space=pl.ANY)
+    shape = jax.ShapeDtypeStruct
+    args = [dvis, bridge, gains[0][None, :], gains[1][None, :], *saved, small_dec, qkv, out, up, down]
+    in_specs = [whole] * 16 + [there] * 4
+    outs = [shape((2, half, wide // 2), F32), shape((24, 128), F32)]
+    assert 2 * wide + 3 * narrow <= 24 * 128
+    grads, bridge_grad = (wide, cols), (wide // 2, narrow)
+    scratch = []
+    if cube:
+        span = dec_grads.shape[3]
+        cells = pos_parts.shape[1]
+        args += [dec_grads, pos_parts]
+        in_specs += [there] * 2
+        outs += [
+            shape((48, cols), F32),
+            shape((24, 3 * span), F32),
+            shape((24, cells), F32),
+            shape((16, 48, narrow), B16),
+        ]
+        scratch = [
+            VMEM((wide // 2, cols), B16),
+            VMEM((7, 48, cols), B16),
+            VMEM((2, narrow, span), B16),
+            VMEM((2, narrow // 2, span), B16),
+            VMEM((narrow // 2, span), B16),
+            VMEM((narrow // 2, 3 * span), B16),
+            VMEM((4, 48, 3 * span), B16),
+            VMEM(pos_parts.shape, B16),
+            VMEM((pos_parts.shape[2], cells), B16),
+            VMEM((4, 48, cells), B16),
+            VMEM((narrow // 2, narrow), B16),
+            VMEM((4, 48, narrow), B16),
+            VMEM((5, 24, 128), F32),
+            VMEM(grads, B16),
+            VMEM(bridge_grad, B16),
+        ]
+    else:
+        outs += [shape(grads, B16), shape(bridge_grad, B16)]
+    scratch += [
+        VMEM(qkv.shape, B16),
+        VMEM(out.shape, B16),
+        VMEM(up.shape, B16),
+        VMEM(down.shape, B16),
+        VMEM((used, hidden), B16),
+        VMEM((used, wide), F32),
+        VMEM((used, wide), B16),
+        VMEM((2, used, wide), B16),
+        VMEM((used, wide), F32),
+        VMEM((used, wide), B16),
+        VMEM((used, feats), B16),
+        VMEM((3, used, feats), B16),
+        VMEM((2, wide, used), B16),
+        VMEM((2, half, wide // 2), F32),
+        pltpu.SemaphoreType.DMA((8,)),
+        pltpu.SemaphoreType.DMA((96,)),
+        pltpu.SemaphoreType.DMA((96,)),
+    ]
+    return pl.pallas_call(
+        functools.partial(back_kernel, cube),
+        out_shape=outs,
+        in_specs=in_specs,
+        out_specs=[whole] * len(outs),
+        scratch_shapes=scratch,
+        compiler_params=remote_params(ident),
+        name="encoder_back",
+    )(*args)
 
 
 def per_device(
@@ -881,159 +1517,115 @@
     s, d, m = place_of()
     n = lax.axis_size("dp")
     owners = 2 * n
-    stays = s == m
-    cells_half, dec_wide = position_embed.shape
-    slots = clip_cells.shape[2]
-    half_slots = tokens.shape[2]
-    enc_wide = tokens.shape[3]
+    cube = n == 8
+    dec_wide = position_embed.shape[1]
+    half_slots, enc_wide = tokens.shape[2:]
     used = -(-LONGEST // 32) * 32
 
-    qkv_own = jnp.swapaxes(dec_qkv, 0, 1)
-    swapped = swap(
-        [
-            pick(tokens[:, 0], s),
-            qkv_own,
-            dec_attn_out,
-            position_embed.astype(B16),
-        ],
-        "x",
+    e_weights = (jnp.swapaxes(enc_qkv, 0, 1), enc_attn_out, enc_up, enc_down)
+    d_qkv = jnp.swapaxes(dec_qkv, 0, 1)
+    vis, d_qkv_far, d_out_far, pos_far, *saved = encoder(
+        clip_lengths[:, 0],
+        tokens[:, 0],
+        e_weights,
+        bridge_weight,
+        (enc_gain_one, enc_gain_two),
+        position_embed,
+        d_qkv,
+        dec_attn_out,
+        used,
         1,
     )
-    tok_far, qkv_far, out_far, pos_far = swapped
-
-    tok_near = pick(tokens[:, 0], s)
-    x = jnp.concatenate(
-        [jnp.where(m == 0, tok_near, tok_far), jnp.where(m == 0, tok_far, tok_near)], 0
-    )[:used].astype(F32)
-    length = pick(clip_lengths[:, 0], s)
-    e_qkv = enc_qkv.reshape(enc_wide, -1)
-    unit1, inv1, a = normed(x, enc_gain_one)
-    triple = jnp.dot(a, e_qkv, preferred_element_type=F32).astype(B16)
-    triple = triple.reshape(used, 3, -1, HEAD)
-    ep, eo = small_attend(triple, length)
-    part = jnp.dot(eo, enc_attn_out, preferred_element_type=F32)
-    z2 = x + part + swap([part.astype(B16)], "x", 2)[0].astype(F32)
-    unit2, inv2, b = normed(z2, enc_gain_two)
-    u = jnp.dot(b, enc_up, preferred_element_type=F32)
-    h = gelu(u).astype(B16)
-    part = jnp.dot(h, enc_down, preferred_element_type=F32)
-    enc = (z2 + part + swap([part.astype(B16)], "x", 3)[0].astype(F32)).astype(B16)
-    vis = jnp.dot(enc, bridge_weight, preferred_element_type=F32).astype(B16)
-    vis_far = swap([vis], "core", 4)[0]
-
-    vis_used = jnp.where(stays, vis, vis_far)
-    cells = jnp.where(jnp.arange(used) < pick(clip_lengths[:, 0], m), pick(clip_cells[:, 0], m)[:used], -1)
-    dec, pos_parts, dvis, dec_grads, dec_small = decoder(
-        vis_used,
+    cells = jnp.where(
+        jnp.arange(used) < pick(clip_lengths[:, 0], m), pick(clip_cells[:, 0], m)[:used], -1
+    )
+    decoded, pos_parts, dvis, dec_grads, dec_small = decoder(
+        cube,
+        vis,
         cells,
         position_embed,
         pos_far,
         mask_token,
         (dec_gain_one, dec_gain_two),
-        (qkv_own, qkv_far, dec_attn_out, out_far, dec_up, dec_down),
+        (d_qkv, d_qkv_far, dec_attn_out, d_out_far, dec_up, dec_down),
         cotangent[:, 0],
-        5,
+        2,
     )
-    g_done, g_dtwo, g_mask = dec_small[0], dec_small[1], dec_small[2]
-    decoded = route(dec, 6)
-    position_parts = route(pos_parts, 8)
-    packed = jnp.stack(
-        [
-            pack(jnp.concatenate([dec_grads[side, 0], dec_grads[side, 1], dec_grads[side, 2]], 1), owners)
+    tokens_grad, small, *rest = back(
+        cube,
+        dvis,
+        bridge_weight,
+        (enc_gain_one, enc_gain_two),
+        saved,
+        dec_small,
+        e_weights,
+        dec_grads,
+        pos_parts,
+        half_slots,
+        3,
+    )
+    if cube:
+        enc_final, dec_final, pos_final, bridge_all = rest
+        pieces = bridge_all.reshape(8, 2, -1, dec_wide)
+        bridge_grad = jnp.swapaxes(pieces, 0, 1).reshape(enc_wide, dec_wide)
+    else:
+        grads, bridge = rest
+        enc_final = unpack(scatter(pack(grads, owners)[None], 11), enc_wide // owners)
+        packed = [
+            pack(jnp.concatenate([dec_grads[side, t] for t in range(3)], 1), owners)
             for side in range(2)
         ]
-    )
-    own = dec_wide // owners
-    dec_final = unpack(scatter(packed, 11), own)
-    pos_sum = (position_parts[0].astype(F32) + position_parts[1].astype(F32))
-    pos_t = jnp.transpose(pos_sum)
-
-    grad_out = dot_nt(dvis, bridge_weight)
-    dm = grad_out.astype(B16)
-    enc_mine = lax.dynamic_slice_in_dim(enc, m * (enc_wide // 2), enc_wide // 2, 1)
-    g_bridge = dot_tn(enc_mine, dvis)
-    eg_h = dot_nt(dm, enc_down)
-    eg_down = dot_tn(dm, h)
-    eg_u = (eg_h * gelu_slope(u)).astype(B16)
-    eg_up = dot_tn(b, eg_u)
-    part = dot_nt(eg_u, enc_up)
-    g_etwo = jnp.sum(part * unit2, 0)
-    whole = part + swap([part.astype(B16)], "x", 12)[0].astype(F32)
-    eg_z2 = grad_out + norm_back(whole, unit2, inv2, enc_gain_two)
-    eg_a = eg_z2.astype(B16)
-    eg_out = dot_tn(eg_a, eo)
-    eg_o = dot_nt(eg_a, enc_attn_out).astype(B16)
-    eg_triple = small_attend_back(triple, ep, eg_o)
-    eg_qkv = dot_tn(a, eg_triple)
-    part = dot_nt(eg_triple, e_qkv)
-    g_eone = jnp.sum(part * unit1, 0)
-    whole = part + swap([part.astype(B16)], "x", 13)[0].astype(F32)
-    grad_x = eg_z2 + norm_back(whole, unit1, inv1, enc_gain_one)
-    grad_x = jnp.pad(grad_x, ((0, slots - used), (0, 0)))
-    grad_x = lax.dynamic_slice_in_dim(grad_x, m * half_slots, half_slots, 0)
-    halves = jnp.stack(jnp.split(grad_x, 2, axis=1))
-    other = swap([pick(halves, 1 - s)], "core", 14)[0]
-    mine = pick(halves, s)
-    tokens_grad = jnp.stack([jnp.where(s == 0, mine, other), jnp.where(s == 0, other, mine)])
-
-    packed = pack(jnp.concatenate([eg_qkv, eg_up, eg_out, eg_down], 1), owners)
-    enc_own = enc_wide // owners
-    enc_final = unpack(scatter(packed[None], 15), enc_own)
-
-    pos_rows = dec_wide // 2 // n
-    pos_packed = pack(pos_t, n)
-    zero = jnp.zeros_like(pos_packed)
-    pos_two = jnp.concatenate(
-        [jnp.where(s == 0, pos_packed, zero), jnp.where(s == 1, pos_packed, zero)], 0
-    )
-    pos_final = unpack(scatter(pos_two[None], 16), pos_rows)
-
-    small = jnp.concatenate([g_eone, g_etwo, g_done, g_dtwo, g_mask])
-    per = -(-small.shape[0] // owners)
-    small = jnp.pad(small, (0, per * owners - small.shape[0])).reshape(owners, 1, per)
-    small = jnp.pad(small, ((0, 0), (0, 0), (0, dec_wide - per)))
-    bridge_own = enc_wide // 2 // owners
-    rows = -(-(bridge_own + 1) // 16) * 16
-    rep = jnp.concatenate(
-        [
-            g_bridge.reshape(owners, bridge_own, dec_wide),
-            small,
-            jnp.zeros((owners, rows - bridge_own - 1, dec_wide), F32),
-        ],
-        1,
-    ).astype(B16)
-    rep = scatter(rep[None], 17).astype(B16)
-    everyone = gather(rep, n, 18).reshape(owners, 2, rows, dec_wide)
-    bridge_grad = jnp.swapaxes(everyone[:, :, :bridge_own], 0, 1).reshape(enc_wide, dec_wide)
-    small = everyone[:, 0, bridge_own, :per].astype(F32) + everyone[:, 1, bridge_own, :per].astype(F32)
-    small = small.reshape(-1)
+        dec_final = unpack(scatter(jnp.stack(packed), 12), dec_wide // owners)
+        parts = route(pos_parts, 13).astype(F32)
+        packed = pack(jnp.transpose(parts[0] + parts[1]), n)
+        zero = jnp.zeros_like(packed)
+        packed = jnp.concatenate(
+            [jnp.where(s == 0, packed, zero), jnp.where(s == 1, packed, zero)], 0
+        )
+        pos_final = unpack(scatter(packed[None], 14), dec_wide // owners)
+        bridge_own = enc_wide // 2 // owners
+        per = -(-small.size // owners)
+        small = jnp.pad(small.reshape(-1), (0, per * owners - small.size)).reshape(owners, 1, per)
+        rows = -(-(bridge_own + 1) // 16) * 16
+        rep = jnp.concatenate(
+            [
+                bridge.astype(F32).reshape(owners, bridge_own, dec_wide),
+                jnp.pad(small, ((0, 0), (0, 0), (0, dec_wide - per))),
+                jnp.zeros((owners, rows - bridge_own - 1, dec_wide), F32),
+            ],
+            1,
+        ).astype(B16)
+        rep = scatter(rep[None], 15).astype(B16)
+        everyone = gather(rep, n, 16).reshape(owners, 2, rows, dec_wide)
+        bridge_grad = jnp.swapaxes(everyone[:, :, :bridge_own], 0, 1).reshape(enc_wide, dec_wide)
+        small = everyone[:, 0, bridge_own, :per].astype(F32) + everyone[
+            :, 1, bridge_own, :per
+        ].astype(F32)
     cuts = [enc_wide, 2 * enc_wide, 2 * enc_wide + dec_wide, 2 * enc_wide + 2 * dec_wide]
-    one_e, two_e, one_d, two_d, mask_grad = (
-        part for part in jnp.split(small[: 2 * enc_wide + 3 * dec_wide], cuts)
-    )
-
-    enc_cols = enc_qkv.shape[2]
-    sizes = [3 * enc_cols, enc_up.shape[1], enc_attn_out.shape[0]]
-    e1, e2, e3, e4 = jnp.split(enc_final, [sizes[0], sizes[0] + sizes[1], sum(sizes)], 1)
-    dec_cols = dec_qkv.shape[2]
-    sizes = [3 * dec_cols, dec_attn_out.shape[0], dec_up.shape[1]]
-    d1, d3, d2, d4 = jnp.split(dec_final, [sizes[0], sizes[0] + sizes[1], sum(sizes)], 1)
+    small = small.reshape(-1)[: 2 * enc_wide + 3 * dec_wide]
+    one_e, two_e, one_d, two_d, mask_grad = jnp.split(small, cuts)
+
+    def split(final, qkv, out, up):
+        cols = qkv.shape[2]
+        first = 3 * cols + out.shape[0]
+        second = first + up.shape[1]
+        return (
+            final[:, : 3 * cols].reshape(-1, 3, cols),
+            final[:, 3 * cols : first].T,
+            final[:, first:second],
+            final[:, second:].T,
+        )
+
     return (
         decoded.astype(F32)[:, None],
         tokens_grad[:, None],
-        e1.reshape(enc_own, 3, -1),
-        e3.T,
-        e2,
-        e4.T,
+        *split(enc_final, enc_qkv, enc_attn_out, enc_up),
         one_e,
         two_e,
         bridge_grad.astype(F32),
         mask_grad,
         pos_final.T,
-        d1.reshape(own, 3, -1),
-        d3.T,
-        d2,
-        d4.T,
+        *split(dec_final, dec_qkv, dec_attn_out, dec_up),
         one_d,
         two_d,
     )

time: 467 us -> 246 us (0.53)
  the two profiles are of different devices: /device:TPU:17 before, /device:TPU:0 now
where the time goes in v3:
time: 246 us; the launch traced here: 242 us
  Pallas kernels  211 us (86%)
  local copies, waits for them, and re-layouts  26.2 us (11%)
  other arithmetic  3.39 us (1%)
    pallas_call x1, Pallas kernels, back(): pl.pallas_call(functools.partial(back_kernel, cube), out_shape=outs, in_s...  102 us
    pallas_call x1, Pallas kernels, decoder(): pl.pallas_call(functools.partial(dec_kernel, early), out_shape=[jax.Shape...  71.5 us
    pallas_call x1, Pallas kernels, encoder(): pl.pallas_call(enc_kernel, out_shape=[item for item, _ in outs], in_specs...  38 us
    unnamed x15, local copies, waits for them, and re-layouts  6.08 us

profile of v3, /device:TPU:0, one launch (start us, length us, event | category | flops | bytes accessed | tf_op | source)
XLA Modules:
  0.0 242.1 jit_solution(15355215129405017298)
XLA Ops:
  0.7 1.2 constant_dynamic-slice_fusion.1
  1.9 1.9 compare_select_fusion.refs_1_
  3.8 0.7 fusion.1
  4.5 1.2 broadcast_in_dim.38.refs_5_
  5.7 1.2 broadcast_in_dim.39.refs_6_
  7.0 1.2 broadcast_in_dim.40.refs_7_
  8.2 1.3 broadcast_in_dim.34.refs_7_.refs_2_
  9.5 1.3 broadcast_in_dim.35.refs_8_.refs_3_
  10.7 0.1 copy.43
  10.9 1.3 fusion.refs_2_
  12.2 2.1 copy.42
  14.2 38.0 %encoder.1 = (bf16[160,384]{1,0:T(8,128)(2,1)}, bf16[3,384,192]{2,1,0:T(8,128)(2,1)}, bf16[192,384]{1,0:T(8,128)(2,1)}, bf16[784,384]{1,0:T(8,128)(2,1)}, f32[16...) custom-call(s32[2]{0:T(128)} %bitcast.56, ...), custom_call_target="tpu_custom_call" | custom-call | tf_op jit(solution)/shard_map/encoder/pallas_call | solution.py:944
  52.3 71.5 %decoder.1 = (bf16[2,784,192]{2,1,0:T(8,128)(2,1)}, bf16[2,784,192]{2,1,0:T(8,128)(2,1)}, bf16[160,384]{1,0:T(8,128)(2,1)}, bf16[2,3,384,768]{3,2,1,0:T(8,128)(2,1)}, f32[8,384]{1,0:T(8,128)}) custom-call(bf16[160,384]{1,0:T(8,128)(2,1)} %get-tuple-element.43.refs_0_, s32[1,160]{1,0:T(1,128)} %compare_select_fusion.refs_1_, s32[160,1]{1,0:T(8,128)} %fusion.refs_2_, ...), custom_call_target="tpu_custom_call" | custom-call | tf_op jit(solution)/shard_map/decoder/pallas_call | solution.py:655
  123.8 101.9 %encoder_back.1 = (f32[2,128,384]{2,1,0:T(8,128)}, f32[24,128]{1,0:T(8,128)}, f32[48,4608]{1,0:T(8,128)}, f32[24,2304]{1,0:T(8,128)}, f32[24,784]{1,0:T(8,128)}, /*index=5*/bf16[16,48,384]{2,1,0:T(8,128)(2,1)}) custom-call(bf16[160,384]{1,0:T(8,128)(2,1)} %get-tuple-element.48.refs_0_, bf16[768,384]{1,0:T(8,128)(2,1)} %refs_1_.1, ...), custom_call_target="tpu_custom_call" | custom-call | tf_op jit(solution)/shard_map/encoder_back/pallas_call | solution.py:1485
  225.7 0.0 copy-start
  225.7 0.0 copy-start.2
  225.7 1.4 slice_bitcast_fusion.6
  227.1 1.4 slice_bitcast_fusion.4
  228.5 1.4 slice_bitcast_fusion.3
  229.9 0.8 slice.51
  230.8 1.6 slice_bitcast_fusion.1
  232.4 0.1 reshape.93
  232.5 0.6 copy.48
  233.1 1.5 slice_bitcast_fusion.2
  234.6 0.9 slice.47
  235.6 0.0 copy-done
  235.6 0.8 slice_bitcast_fusion
  236.4 0.7 copy.51
  237.1 0.0 copy-done.2
  237.1 0.1 convert_bitcast_fusion
  237.2 0.0 copy-start.1
  237.2 1.1 copy.44
  238.3 0.4 copy-done.1
  238.7 0.1 bitcast_convert_fusion
  238.8 0.0 copy-start.3
  238.8 0.0 copy-start.4
  238.8 1.6 copy.45
  240.4 0.0 copy-done.3
  240.4 0.7 copy.54
  241.2 0.0 copy-done.4
  241.2 0.6 copy.55
Async XLA Ops:
  225.7 9.9 %copy-start = (f32[48,4608]{1,0:T(8,128)S(1)}, f32[48,4608]{1,0:T(8,128)}, u32[]{:S(2)}) copy-start(f32[48,4608]{1,0:T(8,128)} %get-tuple-element.64) | copy-start | bytes 2654212
  225.7 11.4 %copy-start.2 = (bf16[16,48,384]{2,1,0:T(8,128)(2,1)S(1)}, bf16[16,48,384]{2,1,0:T(8,128)(2,1)}, u32[]{:S(2)}) copy-start(bf16[16,48,384]{2,1,0:T(8,128)(2,1)} %get-tuple-element.66) | copy-start | bytes 1769476
  237.2 1.5 copy-start.1
  238.8 1.6 copy-start.3
  238.8 2.4 copy-start.4

commit v4 on v3

--- a/solution.py
+++ b/solution.py
@@ -240,6 +240,12 @@
     return (lanes < HEAD, lanes >= HEAD)
 
 
+def fetch(src, dst, sem):
+    copy = pltpu.make_async_copy(src, dst, sem)
+    copy.start()
+    return copy
+
+
 class Wire:
     def __init__(self, send_sem, recv_sem):
         self.send_sem, self.recv_sem, self.used = send_sem, recv_sem, 0
@@ -247,7 +253,71 @@
     def copy(self, src, dst, partner):
         index = self.used
         self.used += 1
+        assert index < self.send_sem.shape[0]
         return send(src, dst, self.send_sem.at[index], self.recv_sem.at[index], partner)
+
+
+class Chip:
+    def __init__(self, s, d, m):
+        self.s, self.m = s, m
+        z = d // 2
+        self.z = z
+        self.me = {"y": lax.rem(d, 2), "a": lax.rem(z + z // 2, 2), "b": z // 2}
+        self.near = [self.beside(axis) for axis in "yab"]
+
+    @staticmethod
+    def z_of(a, b):
+        return lax.rem(a + b, 2) + 2 * b
+
+    @staticmethod
+    def place(z):
+        return (z + z // 2) % 2, z // 2
+
+    def beside(self, axis):
+        at = dict(self.me, **{axis: 1 - self.me[axis]})
+        return (self.s, 2 * self.z_of(at["a"], at["b"]) + at["y"], self.m)
+
+    def own_rows(self, value, out):
+        for y in range(2):
+
+            @pl.when(self.me["y"] == y)
+            def _(y=y):
+                out[...] = value[24 * y : 24 * y + 24]
+
+
+class Fold:
+    def __init__(self, wire, chip, held, boxes, lanes, axes, order, last):
+        self.rounds = []
+        kept = {}
+        for k, axis in enumerate(order):
+
+            def part(value):
+                chosen = dict(kept, **{axis: value})
+                index = tuple(chosen.get(name, slice(None)) for name in axes)
+                return held.at[index + (slice(None), lanes)]
+
+            box = boxes[k].at[(slice(None),) * (len(axes) - k) + (lanes,)]
+            copy = wire.copy(part(1 - chip.me[axis]), box, chip.beside(axis))
+            self.rounds.append((copy, part(chip.me[axis]), box))
+            kept[axis] = chip.me[axis]
+        if last:
+            mine = held.at[tuple(kept[name] for name in axes) + (slice(None), lanes)]
+            box = boxes[-1].at[:, lanes]
+            self.rounds.append((wire.copy(mine, box, chip.beside("y")), mine, box))
+
+    def start(self):
+        self.rounds[0][0].start()
+
+    def step(self, k):
+        copy, mine, box = self.rounds[k]
+        copy.wait()
+        mine[...] = mine[...] + box[...]
+        self.rounds[k + 1][0].start()
+
+    def end(self):
+        copy, mine, box = self.rounds[-1]
+        copy.wait()
+        return mine[...].astype(F32) + box[...].astype(F32)
 
 
 def norm_of(z):
@@ -274,9 +344,15 @@
 
 def dec_kernel(early, *refs):
     (
-        vis_ref, cells_row, cells_col, pos_own, pos_far, mask_ref, gain1_ref, gain2_ref,
+        vis_ref, lengths, cells_ref, pos_own, pos_far, mask_ref, gain1_ref, gain2_ref,
         qkv_own, qkv_far, out_own, out_far, up_hbm, down_hbm, cot_hbm,
-        routed, pos_out, dvis_out, grad_out, small_out,
+        routed, dvis_out, small_out, *refs,
+    ) = refs
+    if early:
+        pos_out, attn_out, mlp_out, grad_out, *refs = refs
+    else:
+        pos_out, grad_out, *refs = refs
+    (
         dec_out, w_up, w_down, cot, z1, unit1, a_ref, q_ref, keys, values, probs, stats,
         o_ref, unit2, b_ref, h_ref, slope, z2, do_ref, flip, dkt, dvt, got_kv,
         dvis_mine, dvis_near, dvis_far, free_sem, local_sem, send_sem, recv_sem,
@@ -297,8 +373,7 @@
         pltpu.make_async_copy(up_hbm, w_up.at[0], local_sem.at[0]),
         pltpu.make_async_copy(down_hbm, w_down.at[0], local_sem.at[1]),
     ]
-    pos_load = pltpu.make_async_copy(pos_own, z1, local_sem.at[3])
-    pos_load.start()
+    pos_loads = [fetch(pos_own, z1, local_sem.at[3]), fetch(pos_far, b_ref, local_sem.at[5])]
     cot_load = pltpu.make_async_copy(cot_hbm.at[m], cot, local_sem.at[2])
     for load in loads:
         load.start()
@@ -324,22 +399,28 @@
     def kept(plane, rows, column):
         return stats[plane, rows][:, column : column + 1]
 
-    pos_load.wait()
+    for copy in pos_loads:
+        copy.wait()
     rows_at = 112
     base = s * length
+
+    used = vis_ref.shape[0]
+    slots = lax.broadcasted_iota(jnp.int32, (1, used), 1)
+    cells_row = jnp.where(m == 0, cells_ref[0:1, :used], cells_ref[1:2, :used])
+    cells_row = jnp.where(slots < lengths[m], cells_row, -1)
 
     def fill(i):
         rows = pl.ds(pl.multiple_of(i * rows_at, 16), rows_at)
         ids = lax.broadcasted_iota(jnp.int32, (rows_at, 1), 0) + (base + i * rows_at)
-        place = jnp.where(cells_row[...] == ids, 1.0, 0.0)
+        place = jnp.where(cells_row == ids, 1.0, 0.0)
         unseen = 1.0 - jnp.sum(place, -1, keepdims=True)
-        pos = jnp.where(stays, z1[rows], pos_far[rows].astype(F32))
-        z = dot_nn(place.astype(B16), vis_ref[...]) + unseen * mask_ref[...] + pos
+        pos = jnp.where(stays, z1[rows], b_ref[rows].astype(F32))
+        z = dot_nn(place.astype(B16), vis_ref[...]) + unseen * mask_ref[...][None, :] + pos
         unit, inverse = norm_of(z)
         z1[rows] = z
-        unit1[rows] = unit
+        unit1[rows] = unit.astype(B16)
         keep(0, rows, heads, inverse)
-        a_ref[rows] = (unit * gain1_ref[...]).astype(B16)
+        a_ref[rows] = (unit * gain1_ref[...][None, :]).astype(B16)
 
     each(length // rows_at, fill)
 
@@ -347,8 +428,8 @@
     mine_rows = pl.ds(0, length)
     kv_copies = []
     for side, weight in enumerate((qkv_own, qkv_far)):
-        keys[side, mine_rows] = dot_nn(a, weight[1]).astype(B16)
-        values[side, mine_rows] = dot_nn(a, weight[2]).astype(B16)
+        keys[side, mine_rows] = dot_nt(a, weight[1]).astype(B16)
+        values[side, mine_rows] = dot_nt(a, weight[2]).astype(B16)
         for held in (keys, values):
             copy = wire.copy(
                 held.at[side, mine_rows], held.at[side, pl.ds(length, length)], sibling
@@ -356,7 +437,7 @@
             copy.start()
             kv_copies.append(copy)
     for side, weight in enumerate((qkv_own, qkv_far)):
-        q_ref[side] = (dot_nn(a, weight[0]).astype(B16).astype(F32) * scale).astype(B16)
+        q_ref[side] = (dot_nt(a, weight[0]).astype(B16).astype(F32) * scale).astype(B16)
     for copy in kv_copies:
         copy.wait()
 
@@ -393,9 +474,9 @@
     def second(i):
         rows = pl.ds(pl.multiple_of(i * rows_at, 16), rows_at)
         unit, inverse = norm_of(z2[rows])
-        unit2[rows] = unit
+        unit2[rows] = unit.astype(B16)
         keep(1, rows, heads, inverse)
-        b_ref[rows] = (unit * gain2_ref[...]).astype(B16)
+        b_ref[rows] = (unit * gain2_ref[...][None, :]).astype(B16)
 
     each(length // rows_at, second)
     for load in loads:
@@ -492,8 +573,8 @@
     def second_back(i, total):
         rows = pl.ds(pl.multiple_of(i * rows_at, 16), rows_at)
         grad = z1[rows]
-        unit = unit2[rows]
-        z = cot[rows].astype(F32) + back_norm(grad, unit, kept(1, rows, heads), gain2_ref[...])
+        unit = unit2[rows].astype(F32)
+        z = cot[rows].astype(F32) + back_norm(grad, unit, kept(1, rows, heads), gain2_ref[...][None, :])
         z2[rows] = z
         b_ref[rows] = z.astype(B16)
         return add_rows(total, grad * unit)
@@ -567,17 +648,28 @@
     for copies in kv_back:
         for copy in copies:
             copy.start()
-
     if early:
+        def stage(slot, halves, out, sem):
+            lanes = pl.ds(0, out.shape[1])
+            for owner in range(8):
+                a, b = Chip.place(owner // 2)
+                rows = pl.ds(48 * (4 * (owner % 2) + 2 * a + b), 48)
+                piece = jnp.concatenate([half[24 * owner : 24 * owner + 24] for half in halves], 0)
+                piece = jnp.pad(piece, ((0, 0), (0, out.shape[1] - piece.shape[1])))
+                probs[0, slot, rows, lanes] = piece.astype(B16)
+            return fetch(probs.at[0, slot, pl.ds(0, wide), lanes], out, sem)
+
+        totals = []
         for t in (1, 2):
             held, copy = near[0, t]
             copy.wait()
             across[t][1].wait()
-            grad_out[0, t, mine_grads] = (
+            totals.append(
                 held[...].astype(F32)
                 + grad_out[0, t, mine_grads].astype(F32)
                 + across[t][0][...].astype(F32)
-            ).astype(B16)
+            )
+        stores = [stage(2, totals, mlp_out, local_sem.at[1])]
 
     a_flip = flip.at[0]
     a_flip[...] = transposed(a_ref[...])
@@ -591,57 +683,88 @@
             else:
                 grad = q_ref[side]
             grad_out[side, 0, :, pl.ds(slot * third, third)] = dot_nn(a_flip[...], grad).astype(B16)
-            part = dot_nt(grad, weight[slot])
+            part = dot_nn(grad, weight[slot])
             total = part if total is None else total + part
     z1[...] = total
-
-    def first_back(i, totals):
-        rows = pl.ds(pl.multiple_of(i * rows_at, 16), rows_at)
-        grad = z1[rows]
-        unit = unit1[rows]
-        z = z2[rows] + back_norm(grad, unit, kept(0, rows, heads), gain1_ref[...])
-        b_ref[rows] = z.astype(B16)
-        pos_out[0, rows] = z[:, :third].astype(B16)
-        pos_out[1, rows] = z[:, third:].astype(B16)
-        ids = lax.broadcasted_iota(jnp.int32, (rows_at, 1), 0) + (base + i * rows_at)
-        seen = jnp.sum(jnp.where(cells_row[...] == ids, 1.0, 0.0), -1, keepdims=True)
-        return add_rows(totals[0], grad * unit), add_rows(totals[1], (1.0 - seen) * z)
-
-    gain1_grad, mask_grad = lax.fori_loop(0, length // rows_at, first_back, (zero, zero))
-    small_out[0:1] = gain1_grad
-    small_out[1:2] = gain2_grad
-    small_out[2:3] = mask_grad
-
-    used = vis_ref.shape[0]
-    ids = lax.broadcasted_iota(jnp.int32, (used, length), 1) + base
-    place = jnp.where(cells_col[...] == ids, 1.0, 0.0).astype(B16)
-    dvis_mine[...] = dot_nn(place, b_ref[...]).astype(B16)
-    near = wire.copy(dvis_mine, dvis_near, sibling)
-    near.start()
-    near.wait()
-    dvis_mine[...] = (dvis_mine[...].astype(F32) + dvis_near[...].astype(F32)).astype(B16)
-    dvis_over = wire.copy(dvis_mine, dvis_far, facing)
-
+    if early:
+        attn_pairs = []
+        for side in (1, 0):
+            held = h_ref.at[1, pl.ds((2 + side) * rows, rows)]
+            copy = wire.copy(grad_out.at[side, 0, away_grads], held, sibling)
+            copy.start()
+            attn_pairs.append((held, copy))
     @pl.when(stays)
     def _():
-        dvis_over.start()
-        dvis_out[...] = dvis_mine[...]
-        dvis_over.wait_send()
         route_local.wait()
         route_near.wait_send()
         route_over.wait_recv()
 
     @pl.when(jnp.logical_not(stays))
     def _():
-        dvis_over.wait_recv()
-        dvis_out[...] = dvis_far[...]
         route_over.wait_send()
         route_far.wait_send()
         route_near.wait_recv()
         route_far.wait_recv()
 
-
-def decoder(early, vis, cells, pos_own, pos_far, mask, gains, weights, cot, ident):
+    def first_back(i, totals):
+        rows = pl.ds(pl.multiple_of(i * rows_at, 16), rows_at)
+        grad = z1[rows]
+        unit = unit1[rows].astype(F32)
+        z = z2[rows] + back_norm(grad, unit, kept(0, rows, heads), gain1_ref[...][None, :])
+        b_ref[rows] = z.astype(B16)
+        dec_out[0, rows] = z[:, :third].astype(B16)
+        dec_out[1, rows] = z[:, third:].astype(B16)
+        ids = lax.broadcasted_iota(jnp.int32, (rows_at, 1), 0) + (base + i * rows_at)
+        seen = jnp.sum(jnp.where(cells_row == ids, 1.0, 0.0), -1, keepdims=True)
+        return add_rows(totals[0], grad * unit), add_rows(totals[1], (1.0 - seen) * z)
+
+    gain1_grad, mask_grad = lax.fori_loop(0, length // rows_at, first_back, (zero, zero))
+    if not early:
+        stores = [fetch(dec_out, pos_out, local_sem.at[0])]
+    small_out[0:1] = gain1_grad
+    small_out[1:2] = gain2_grad
+    small_out[2:3] = mask_grad
+
+    ids = (lax.broadcasted_iota(jnp.int32, (used, length), 1) + base).astype(F32)
+    cells_col = jnp.transpose(jnp.broadcast_to(cells_row.astype(F32), (8, used)))[:, 0:1]
+    place = jnp.where(cells_col == ids, 1.0, 0.0).astype(B16)
+    dvis_mine[...] = dot_nn(place, b_ref[...]).astype(B16)
+    dvis_pair = wire.copy(dvis_mine, dvis_near, sibling)
+    dvis_pair.start()
+
+    if early:
+        halves = [jnp.transpose(dec_out[half].astype(F32)) for half in range(2)]
+        stores.append(stage(0, halves, pos_out, local_sem.at[0]))
+    dvis_pair.wait()
+    dvis_mine[...] = (dvis_mine[...].astype(F32) + dvis_near[...].astype(F32)).astype(B16)
+    dvis_over = wire.copy(dvis_mine, dvis_far, facing)
+
+    @pl.when(stays)
+    def _():
+        dvis_over.start()
+        dvis_out[...] = dvis_mine[...]
+
+    @pl.when(stays)
+    def _():
+        dvis_over.wait_send()
+
+    @pl.when(jnp.logical_not(stays))
+    def _():
+        dvis_over.wait_recv()
+        dvis_out[...] = dvis_far[...]
+
+    if early:
+        halves = []
+        for side, (held, copy) in zip((1, 0), attn_pairs):
+            copy.wait()
+            halves.insert(0, held[...].astype(F32) + grad_out[side, 0, mine_grads].astype(F32))
+        stores.append(stage(1, halves, attn_out, local_sem.at[2]))
+
+    for copy in stores:
+        copy.wait()
+
+
+def decoder(early, vis, lengths, cells, pos_own, pos_far, mask, gains, weights, cot, ident):
     qkv_own, qkv_far, out_own, out_far, up, down = weights
     length, wide = pos_own.shape
     used = vis.shape[0]
@@ -652,24 +775,40 @@
     assert heads == 3 and length % 112 == 0
     whole = pl.BlockSpec(memory_space=VMEM)
     there = pl.BlockSpec(memory_space=pl.ANY)
+    grads = (2, 3, wide, hidden)
+    outs = [
+        (jax.ShapeDtypeStruct((2, length, third), B16), there),
+        (jax.ShapeDtypeStruct((used, wide), B16), whole),
+        (jax.ShapeDtypeStruct((8, wide), F32), whole),
+    ]
+    if early:
+        lanes = -(-length // 128) * 128
+        outs += [
+            (jax.ShapeDtypeStruct((wide, lanes), B16), there),
+            (jax.ShapeDtypeStruct((wide, hidden), B16), there),
+            (jax.ShapeDtypeStruct((wide, hidden), B16), there),
+        ]
+    else:
+        outs += [
+            (jax.ShapeDtypeStruct((2, length, third), B16), there),
+            (jax.ShapeDtypeStruct(grads, B16), whole),
+        ]
     return pl.pallas_call(
         functools.partial(dec_kernel, early),
-        out_shape=[
-            jax.ShapeDtypeStruct((2, length, third), B16),
-            jax.ShapeDtypeStruct((2, length, third), B16),
-            jax.ShapeDtypeStruct((used, wide), B16),
-            jax.ShapeDtypeStruct((2, 3, wide, hidden), B16),
-            jax.ShapeDtypeStruct((8, wide), F32),
-        ],
-        in_specs=[whole] * 3 + [there] + [whole] * 8 + [there] * 3,
-        out_specs=[there] + [whole] * 4,
-        scratch_shapes=[
+        out_shape=[item for item, _ in outs],
+        in_specs=[whole, pl.BlockSpec(memory_space=pltpu.SMEM), whole]
+        + [there] * 2
+        + [whole] * 7
+        + [there] * 3,
+        out_specs=[spec for _, spec in outs],
+        scratch_shapes=[VMEM(grads, B16)] * early
+        + [
             VMEM((2, length, third), B16),
             VMEM((2, wide, hidden), B16),
             VMEM((2, hidden, wide), B16),
             VMEM((length, wide), B16),
             VMEM((length, wide), F32),
-            VMEM((length, wide), F32),
+            VMEM((length, wide), B16),
             VMEM((length, wide), B16),
             VMEM((2, length, third), B16),
             VMEM((2, keys, third), B16),
@@ -677,7 +816,7 @@
             VMEM((2, heads, length, keys), B16),
             VMEM((2, length, 128), F32),
             VMEM((2, length, third), B16),
-            VMEM((length, wide), F32),
+            VMEM((length, wide), B16),
             VMEM((length, wide), B16),
             VMEM((2, length, hidden), B16),
             VMEM((2, length, hidden), B16),
@@ -691,23 +830,23 @@
             VMEM((used, wide), B16),
             VMEM((used, wide), B16),
             pltpu.SemaphoreType.REGULAR,
-            pltpu.SemaphoreType.DMA((5,)),
+            pltpu.SemaphoreType.DMA((6,)),
             pltpu.SemaphoreType.DMA((32,)),
             pltpu.SemaphoreType.DMA((32,)),
         ],
         compiler_params=pltpu.CompilerParams(
-            collective_id=ident, has_side_effects=True, vmem_limit_bytes=63 * 1024 * 1024
+            collective_id=ident, has_side_effects=True, vmem_limit_bytes=int(63.9 * 1024) * 1024
         ),
         name="decoder",
     )(
         vis,
-        cells[None, :],
-        cells[:, None],
+        lengths,
+        cells,
         pos_own,
         pos_far,
-        mask[None, :],
-        gains[0][None, :],
-        gains[1][None, :],
+        mask,
+        gains[0],
+        gains[1],
         qkv_own,
         qkv_far,
         out_own,
@@ -735,12 +874,6 @@
 
 def pick(pair, index):
     return lax.dynamic_index_in_dim(pair, index, 0, keepdims=False)
-
-
-def load(src, dst, sem):
-    copy = pltpu.make_async_copy(src, dst, sem)
-    copy.start()
-    return copy
 
 
 def enc_kernel(*refs):
@@ -780,12 +913,12 @@
         own_last.start()
 
     loads = [
-        load(hbm, held, local_sem.at[i + 1])
+        fetch(hbm, held, local_sem.at[i + 1])
         for i, (hbm, held) in enumerate(
             ((qkv_hbm, qkv), (out_hbm, w_out), (up_hbm, w_up), (down_hbm, w_down))
         )
     ]
-    pos_load = load(pos_hbm, pos_full, local_sem.at[5])
+    pos_load = fetch(pos_hbm, pos_full, local_sem.at[5])
     over, share = [], []
     for hbm, held in ((dqkv_hbm, dqkv_far), (dout_hbm, dout_far)):
         at = (slice(None),) * (len(hbm.shape) - 2)
@@ -814,7 +947,7 @@
     unit, inverse = norm_of(x_ref[...].astype(F32))
     unit1[...] = unit
     stats[...] = jnp.where(lane == 0, inverse, 0.0)
-    a = (unit * gain1_ref[...]).astype(B16)
+    a = (unit * gain1_ref[...][None, :]).astype(B16)
     a_ref[...] = a
     loads[0].wait()
     for slot in range(3):
@@ -856,7 +989,7 @@
     unit, inverse = norm_of(z)
     unit2[...] = unit
     stats[...] = jnp.where(lane == 1, inverse, stats[...])
-    b = (unit * gain2_ref[...]).astype(B16)
+    b = (unit * gain2_ref[...][None, :]).astype(B16)
     b_ref[...] = b
     loads[2].wait()
     step = 512
@@ -968,52 +1101,9 @@
         compiler_params=remote_params(ident),
         name="encoder",
     )(
-        lengths, tokens, qkv, out, up, down, bridge, gains[0][None, :], gains[1][None, :],
+        lengths, tokens, qkv, out, up, down, bridge, gains[0], gains[1],
         pos, dqkv, dout,
     )
-
-
-class Fold:
-    def __init__(self, wire, me, held, inbox, lanes, order, rows_of, device_of, last):
-        self.held, self.inbox, self.lanes = held, inbox, lanes
-        self.rounds = []
-        slot = 0
-        for k, axis in enumerate(order):
-            rest = order[k + 1 :]
-            other = dict(me)
-            other[axis] = 1 - me[axis]
-            copies = []
-            for bits in itertools.product((0, 1), repeat=len(rest)):
-                mine, theirs = dict(me, **dict(zip(rest, bits))), dict(other, **dict(zip(rest, bits)))
-                copy = wire.copy(
-                    held.at[rows_of(theirs), lanes], inbox.at[slot, :, lanes], device_of(other)
-                )
-                copies.append((copy, rows_of(mine), slot))
-                slot += 1
-            self.rounds.append(copies)
-        self.mine = rows_of(me)
-        if last:
-            other = dict(me, y=1 - me["y"])
-            copy = wire.copy(held.at[self.mine, lanes], inbox.at[slot, :, lanes], device_of(other))
-            self.rounds.append([(copy, self.mine, slot)])
-
-    def start(self, k):
-        for copy, _, _ in self.rounds[k]:
-            copy.start()
-
-    def total(self, rows, slot):
-        return self.held[rows, self.lanes].astype(F32) + self.inbox[slot, :, self.lanes].astype(F32)
-
-    def step(self, k):
-        for copy, rows, slot in self.rounds[k]:
-            copy.wait()
-            self.held[rows, self.lanes] = self.total(rows, slot).astype(B16)
-        self.start(k + 1)
-
-    def end(self):
-        ((copy, rows, slot),) = self.rounds[-1]
-        copy.wait()
-        return self.total(rows, slot)
 
 
 def back_kernel(cube, *refs):
@@ -1023,10 +1113,11 @@
     ) = refs
     if cube:
         (
-            dec_hbm, pos_hbm,
-            tok_out, small_out, enc_out, dec_out, pos_out, bridge_all,
-            near, inbox, dec_raw, dec_near, dec_over, dec_held, dec_box, pos_got, pos_held, pos_box,
-            bridge_near, bridge_box, small_box, grads, bridge_grad, *refs,
+            pos_hbm, attn_hbm, mlp_hbm,
+            tok_out, small_out, enc_out, mlp_out, attn_out, pos_out, bridge_all,
+            near, held, box0, box1, box2,
+            dec_held, dec_box0, dec_box1, dec_box2, side_held, side_box0, side_box1, side_box2,
+            pos_sum, pos_got, attn_sum, attn_got, bridge_near, small_box, grads, bridge_grad, *refs,
         ) = refs
     else:
         tok_out, small_out, grads, bridge_grad, *refs = refs
@@ -1046,68 +1137,45 @@
     section = wide // 2
 
     if cube:
-        z = d // 2
-        me = {"y": lax.rem(d, 2), "b": z // 2, "a": lax.rem(z + z // 2, 2)}
-
-        def z_of(c):
-            return lax.rem(c["a"] + c["b"], 2) + 2 * c["b"]
-
-        def device_of(c):
-            return (s, 2 * z_of(c) + c["y"], m)
-
-        def rows_eight(c):
-            return pl.ds(pl.multiple_of((2 * z_of(c) + c["y"]) * 48, 16), 48)
-
-        def rows_four(c):
-            return pl.ds(pl.multiple_of(z_of(c) * 48, 16), 48)
-
-        near_chips = [device_of(dict(me, **{axis: 1 - me[axis]})) for axis in "yab"]
-        across = lax.rem(z_of(me) + 2, 4)
-        more = [(s, 2 * across + me["y"], m)] + [
-            (s, 2 * lax.rem(z + k, 4) + me["y"], 1 - m) for k in (1, 2, 3)
-        ]
-        greet([sibling, facing, (1 - s, d, 1 - m)] + near_chips + more)
+        chip = Chip(s, d, m)
+        z, y = chip.z, chip.me["y"]
+        others = [(s, 2 * lax.rem(z + k, 4) + y, lax.rem(m + side, 2)) for k in (1, 2, 3) for side in (0, 1)]
+        greet([sibling, facing, (1 - s, d, 1 - m), chip.near[0]] + others)
     else:
         greet([sibling, facing])
 
     loads = [
-        load(hbm, held, local_sem.at[i])
+        fetch(hbm, held, local_sem.at[i])
         for i, (hbm, held) in enumerate(
             ((down_hbm, w_down), (up_hbm, w_up), (out_hbm, w_out), (qkv_hbm, qkv))
         )
     ]
 
     if cube:
-        route_local = pltpu.make_async_copy(pos_hbm.at[s], pos_got.at[m], local_sem.at[4])
-        route_near = wire.copy(pos_hbm.at[1 - s], pos_got.at[m], sibling)
-        route_over = wire.copy(pos_hbm.at[s], pos_got.at[m], facing)
-        route_far = wire.copy(pos_hbm.at[1 - s], pos_got.at[m], (1 - s, d, 1 - m))
-
-        @pl.when(stays)
-        def _():
-            route_local.start()
-            route_near.start()
-
-        @pl.when(jnp.logical_not(stays))
-        def _():
-            route_over.start()
-            route_far.start()
-
-        dec_rows = dec_raw.shape[1] // 2
-        mine = pl.ds(pl.multiple_of(s * dec_rows, 16), dec_rows)
-        away = pl.ds(pl.multiple_of((1 - s) * dec_rows, 16), dec_rows)
-        raw_load = load(dec_hbm.at[:, 0], dec_raw, local_sem.at[5])
-        span = dec_raw.shape[2]
-        sum_loads = [
-            load(dec_hbm.at[0, t, mine], dec_held.at[:, pl.ds(t * span, span)], local_sem.at[5 + t])
-            for t in (1, 2)
+        cells = pos_sum.shape[2]
+        pos_lanes = pos_hbm.shape[-1]
+        span = attn_hbm.shape[-1]
+        blank = (slice(None),) * 4
+        early_loads = [
+            fetch(hbm, dec_held.at[blank + (pl.ds(first, hbm.shape[-1]),)], local_sem.at[4 + i])
+            for i, (hbm, first) in enumerate(
+                ((pos_hbm, 0), (attn_hbm, pos_lanes), (mlp_hbm, pos_lanes + span))
+            )
         ]
-        raw_load.wait()
-        dec_pair = [
-            wire.copy(dec_raw.at[side, away], dec_near.at[side], sibling) for side in range(2)
+        for copy in early_loads:
+            copy.wait()
+        orders = ("yab", "ayb", "yab")
+        tiles = (pos_lanes + 2 * span) // 128
+        cuts = [128 * (tiles * i // 3) for i in range(4)]
+        early_folds = [
+            Fold(
+                wire, chip, dec_held, (dec_box0, dec_box1, dec_box2), pl.ds(low, high - low), "yab",
+                order, False,
+            )
+            for low, high, order in zip(cuts, cuts[1:], orders)
         ]
-        for copy in reversed(dec_pair):
-            copy.start()
+        for fold in early_folds:
+            fold.start()
 
     def transposed(value):
         return jnp.transpose(value.astype(F32)).astype(B16)
@@ -1128,34 +1196,51 @@
             sibling,
         )
         bridge_pair.start()
-        dec_pair[1].wait()
-        dec_near[1] = (dec_near[1].astype(F32) + dec_raw[1, mine].astype(F32)).astype(B16)
-        dec_across = wire.copy(dec_near.at[1], dec_over, facing)
-        dec_across.start()
 
     loads[0].wait()
     step = 512
-    first_up, first_down = 3 * feats + feats, 3 * feats + feats + hidden
-
-    def down(i):
-        cols = pl.ds(pl.multiple_of(i * step, step), step)
-        grads[:, pl.ds(pl.multiple_of(first_down + i * step, 128), step)] = dot_nn(
-            flip[0], h_ref[:, cols]
-        ).astype(B16)
+    first_mlp = 4 * feats
+    steps = hidden // step
+    if cube:
+        away_rows = pl.ds(pl.multiple_of((1 - s) * section, 16), section)
+
+        class Group:
+            def __init__(self, first, size, order):
+                self.lanes = pl.ds(first, size)
+                self.pair = wire.copy(
+                    grads.at[away_rows, self.lanes], near.at[:, self.lanes], sibling
+                )
+                self.pair.start()
+                self.order = order
+
+            def start(self):
+                self.pair.wait()
+                for owner in range(8):
+                    rows = pl.ds(48 * owner, 48)
+                    from_rows = pl.ds(pl.multiple_of(s * section + 48 * owner, 16), 48)
+                    index = (owner % 2,) + Chip.place(owner // 2) + (slice(None), self.lanes)
+                    held[index] = near[rows, self.lanes] + grads[from_rows, self.lanes]
+                self.fold = Fold(
+                    wire, chip, held, (box0, box1, box2), self.lanes, "yab", self.order, False
+                )
+                self.fold.start()
+
+            def end(self):
+                enc_out[:, self.lanes] = self.fold.end()
+
+        mlp_groups = []
+
+    for i in range(steps):
+        cols = pl.ds(i * step, step)
+        grads[:, pl.ds(first_mlp + 2 * i * step, step)] = dot_nn(flip[0], h_ref[:, cols]).astype(B16)
         grad_u = dot_nt(da_ref[...], w_down[cols, :]) * slope[:, cols].astype(F32)
         grad_u = grad_u.astype(B16)
         gu[:, cols] = grad_u
-        grads[:, pl.ds(pl.multiple_of(first_up + i * step, 128), step)] = dot_nn(
-            flip[1], grad_u
-        ).astype(B16)
-
-    each(hidden // step, down)
-
-    if cube:
-        attn_lanes, mlp_lanes = pl.ds(0, first_up), pl.ds(first_up, 2 * hidden)
-        theirs = pl.ds(pl.multiple_of((1 - s) * section, 16), section)
-        mlp_pair = wire.copy(grads.at[theirs, mlp_lanes], near.at[:, mlp_lanes], sibling)
-        mlp_pair.start()
+        grads[:, pl.ds(first_mlp + (2 * i + 1) * step, step)] = dot_nn(flip[1], grad_u).astype(B16)
+        if cube:
+            mlp_groups.append(Group(first_mlp + 2 * i * step, 2 * step, orders[i % 3]))
+            if i:
+                mlp_groups[i - 1].start()
 
     loads[1].wait()
     grad = dot_nt(gu[...], w_up[...])
@@ -1166,84 +1251,7 @@
     gain2_grad = jnp.sum(grad * unit2[...], 0, keepdims=True)
 
     if cube:
-        def pair_sum(lanes):
-            def body(i):
-                rows = pl.ds(pl.multiple_of(i * 48, 16), 48)
-                from_rows = pl.ds(pl.multiple_of(s * section + i * 48, 16), 48)
-                near[rows, lanes] = (
-                    near[rows, lanes].astype(F32) + grads[from_rows, lanes].astype(F32)
-                ).astype(B16)
-
-            each(section // 48, body)
-
-        orders = (("y", "a", "b"), ("a", "b", "y"), ("b", "y", "a"))
-
-        def folds_of(first, size):
-            third = size // 3
-            return [
-                Fold(
-                    wire, me, near, inbox, pl.ds(first + i * third, third), orders[i], rows_eight,
-                    device_of, False,
-                )
-                for i in range(3)
-            ]
-
-        mlp_folds = folds_of(first_up, 2 * hidden)
-        mlp_pair.wait()
-        pair_sum(mlp_lanes)
-        for fold in mlp_folds:
-            fold.start(0)
-
-        dec_pair[0].wait()
-        dec_across.wait()
-        dec_held[:, pl.ds(0, span)] = (
-            dec_near[0].astype(F32) + dec_raw[0, mine].astype(F32) + dec_over[...].astype(F32)
-        ).astype(B16)
-        for copy in sum_loads:
-            copy.wait()
-        side_folds = [
-            Fold(
-                wire, me, dec_held, dec_box, pl.ds(i * (3 * span // 2), 3 * span // 2), order,
-                rows_four, device_of, True,
-            )
-            for i, order in enumerate((("a", "b"), ("b", "a")))
-        ]
-        bridge_pair.wait()
-        bridge_near[...] = (
-            bridge_near[...].astype(F32)
-            + bridge_grad[
-                pl.ds(pl.multiple_of(s * bridge_rows, 16), bridge_rows)
-            ].astype(F32)
-        ).astype(B16)
-        side_folds.append(
-            Fold(
-                wire, me, bridge_near, bridge_box, pl.ds(0, bridge_near.shape[1]), ("a", "b"),
-                rows_four, device_of, True,
-            )
-        )
-
-        @pl.when(stays)
-        def _():
-            route_local.wait()
-            route_near.wait_send()
-            route_over.wait_recv()
-
-        @pl.when(jnp.logical_not(stays))
-        def _():
-            route_over.wait_send()
-            route_far.wait_send()
-            route_near.wait_recv()
-            route_far.wait_recv()
-
-        pos_held[...] = transposed(pos_got[0].astype(F32) + pos_got[1].astype(F32))
-        side_folds.append(
-            Fold(
-                wire, me, pos_held, pos_box, pl.ds(0, pos_held.shape[1]), ("b", "a"), rows_four,
-                device_of, True,
-            )
-        )
-        for fold in side_folds:
-            fold.start(0)
+        mlp_groups[-1].start()
 
     def back_norm(grad, unit, inverse, gain):
         scaled = grad * gain
@@ -1253,7 +1261,7 @@
 
     over.wait()
     whole = dz[...] + part_far[0].astype(F32)
-    dz2 = dy[...] + back_norm(whole, unit2[...], stats[:, 1:2], gain2_ref[...])
+    dz2 = dy[...] + back_norm(whole, unit2[...], stats[:, 1:2], gain2_ref[...][None, :])
     dy[...] = dz2
     grad_a = dz2.astype(B16)
     da_ref[...] = grad_a
@@ -1263,8 +1271,18 @@
     do_ref[...] = dot_nt(grad_a, w_out[...]).astype(B16)
 
     if cube:
-        for fold in side_folds:
-            fold.step(0)
+        out_group = Group(3 * feats, feats, orders[0])
+        bridge_pair.wait()
+        narrow = bridge_near.shape[1]
+        for at in range(4):
+            side_held[Chip.place(at)] = (
+                bridge_near[pl.ds(48 * at, 48)]
+                + bridge_grad[pl.ds(pl.multiple_of(s * bridge_rows + 48 * at, 16), 48)]
+            )
+        bridge_fold = Fold(
+            wire, chip, side_held, (side_box0, side_box1, side_box2), pl.ds(0, narrow), "ab", "ab", True
+        )
+        bridge_fold.start()
 
     masks = head_masks()
     scale = HEAD**-0.5
@@ -1283,6 +1301,12 @@
         for slot in range(3):
             dqkv[slot, :, at] = jnp.where(masks[0], parts[0][slot], parts[1][slot]).astype(B16)
 
+    if cube:
+        out_group.start()
+        for fold in early_folds:
+            fold.step(0)
+        bridge_fold.step(0)
+
     flip[1] = transposed(a_ref[...])
     loads[3].wait()
     total = None
@@ -1315,12 +1339,12 @@
             row += 1
 
     if cube:
-        attn_pair = wire.copy(grads.at[theirs, attn_lanes], near.at[:, attn_lanes], sibling)
-        attn_pair.start()
-
-        small_steps = [sibling, facing] + near_chips
+        attn_groups = [
+            Group(i * feats, feats, order) for i, order in enumerate(orders)
+        ]
         small_copies = [
-            wire.copy(small_out, small_box.at[i], partner) for i, partner in enumerate(small_steps)
+            wire.copy(small_out, small_box.at[i], partner)
+            for i, partner in enumerate([sibling, facing] + chip.near)
         ]
 
         def small_step(i):
@@ -1330,16 +1354,15 @@
                 small_copies[i + 1].start()
 
         small_copies[0].start()
-        for fold in mlp_folds:
-            fold.step(0)
-        for fold in side_folds:
-            fold.step(1)
+        for group in attn_groups:
+            group.start()
+        bridge_fold.step(1)
         small_step(0)
 
     def finish(rows, size):
         whole = dz[rows] + part_far[1, rows].astype(F32)
         unit = unit1[rows]
-        grad = dy[rows] + back_norm(whole, unit, stats[rows][:, 0:1], gain1_ref[...])
+        grad = dy[rows] + back_norm(whole, unit, stats[rows][:, 0:1], gain1_ref[...][None, :])
         for side in range(2):
             tok_part[side, pl.ds(0, size)] = grad[:, side * section : (side + 1) * section]
 
@@ -1361,63 +1384,88 @@
     tok_out[s] = tok_part[s]
 
     if cube:
-        attn_folds = folds_of(0, first_up)
-        attn_pair.wait()
-        pair_sum(attn_lanes)
-        for fold in attn_folds:
-            fold.start(0)
+        for group in mlp_groups:
+            group.fold.step(0)
+        for fold in early_folds:
+            fold.step(1)
         small_step(1)
 
-        def own_rows(value, out):
-            @pl.when(me["y"] == 0)
-            def _():
-                out[...] = value[:24]
-
-            @pl.when(me["y"] == 1)
-            def _():
-                out[...] = value[24:]
-
         slot = (s * 4 + z) * 2 + m
-        bridge_all[slot] = side_folds[2].end().astype(B16)
+        bridge_all[slot] = bridge_fold.end().astype(B16)
         spread = [
             wire.copy(bridge_all.at[slot], bridge_all.at[slot], partner)
-            for partner in [facing]
-            + [
-                (s, 2 * lax.rem(z + k, 4) + me["y"], lax.rem(m + side, 2))
-                for k in (1, 2, 3)
-                for side in range(2)
-            ]
+            for partner in [facing] + others
         ]
         for copy in spread:
             copy.start()
-        for i in range(2):
-            own = pl.ds(i * (3 * span // 2), 3 * span // 2)
-            own_rows(side_folds[i].end(), dec_out.at[:, own])
-        own_rows(side_folds[3].end(), pos_out)
-        for fold in mlp_folds:
-            fold.step(1)
-        for fold in attn_folds:
-            fold.step(0)
+
+        out_group.fold.step(0)
+        for group in attn_groups:
+            group.fold.step(0)
         small_step(2)
+        for group in mlp_groups:
+            group.fold.step(1)
+
+        wholes = jnp.concatenate([fold.end() for fold in early_folds], 1)
+        for half_at in range(2):
+            piece = wholes[24 * half_at : 24 * half_at + 24]
+            pos_sum[half_at] = piece[:, :cells]
+            attn_sum[half_at] = piece[:, pos_lanes : pos_lanes + span]
+            mlp_out[:, pl.ds(half_at * span, span)] = piece[:, pos_lanes + span :]
+        attn_over = wire.copy(attn_sum.at[1], attn_got, facing)
+        attn_over.start()
+        route_near = wire.copy(pos_sum.at[1 - s], pos_got.at[m], sibling)
+        route_over = wire.copy(pos_sum.at[s], pos_got.at[m], facing)
+        route_far = wire.copy(pos_sum.at[1 - s], pos_got.at[m], (1 - s, d, 1 - m))
+
+        @pl.when(stays)
+        def _():
+            route_near.start()
+            pos_got[m] = pos_sum[s]
+
+        @pl.when(jnp.logical_not(stays))
+        def _():
+            route_over.start()
+            route_far.start()
+
+
+        out_group.fold.step(1)
         for copy in spread:
             copy.wait()
         ours = pl.ds(s * 8, 8)
         bridge_pair_all = wire.copy(bridge_all.at[ours], bridge_all.at[ours], sibling)
         bridge_pair_all.start()
-        for fold in mlp_folds:
-            enc_out[:, fold.lanes] = fold.end()
-        for fold in attn_folds:
-            fold.step(1)
+        for group in attn_groups:
+            group.fold.step(1)
         small_step(3)
-        for fold in attn_folds:
-            enc_out[:, fold.lanes] = fold.end()
+        for group in mlp_groups:
+            group.end()
+        attn_over.wait()
+        attn_out[...] = attn_sum[0] + attn_got[...]
+
+        @pl.when(stays)
+        def _():
+            route_near.wait_send()
+            route_over.wait_recv()
+
+        @pl.when(jnp.logical_not(stays))
+        def _():
+            route_over.wait_send()
+            route_far.wait_send()
+            route_near.wait_recv()
+            route_far.wait_recv()
+
+        pos_out[...] = pos_got[0] + pos_got[1]
+        out_group.end()
         small_step(4)
+        for group in attn_groups:
+            group.end()
         bridge_pair_all.wait()
 
     tok_pair.wait()
 
 
-def back(cube, dvis, bridge, gains, saved, small_dec, weights, dec_grads, pos_parts, half, ident):
+def back(cube, dvis, bridge, gains, saved, small_dec, weights, dec_grads, cells, half, ident):
     unit1, unit2, stats, a, triple, probs, o, b, slope, h, enc_half = saved
     qkv, out, up, down = weights
     used, wide = unit1.shape
@@ -1427,36 +1475,41 @@
     whole = pl.BlockSpec(memory_space=VMEM)
     there = pl.BlockSpec(memory_space=pl.ANY)
     shape = jax.ShapeDtypeStruct
-    args = [dvis, bridge, gains[0][None, :], gains[1][None, :], *saved, small_dec, qkv, out, up, down]
+    args = [dvis, bridge, gains[0], gains[1], *saved, small_dec, qkv, out, up, down]
     in_specs = [whole] * 16 + [there] * 4
     outs = [shape((2, half, wide // 2), F32), shape((24, 128), F32)]
     assert 2 * wide + 3 * narrow <= 24 * 128
     grads, bridge_grad = (wide, cols), (wide // 2, narrow)
     scratch = []
     if cube:
-        span = dec_grads.shape[3]
-        cells = pos_parts.shape[1]
-        args += [dec_grads, pos_parts]
-        in_specs += [there] * 2
+        pos, attn, mlp = dec_grads
+        span = attn.shape[1]
+        args += [
+            pos.reshape(2, 2, 2, 48, -1), attn.reshape(2, 2, 2, 48, -1), mlp.reshape(2, 2, 2, 48, -1)
+        ]
+        in_specs += [there] * 3
         outs += [
             shape((48, cols), F32),
-            shape((24, 3 * span), F32),
+            shape((24, 2 * span), F32),
+            shape((24, span), F32),
             shape((24, cells), F32),
             shape((16, 48, narrow), B16),
         ]
+
+        def folded(axes, size):
+            return [VMEM((2,) * (axes - k) + (48, size), B16) for k in range(axes + 1)]
+
         scratch = [
             VMEM((wide // 2, cols), B16),
-            VMEM((7, 48, cols), B16),
-            VMEM((2, narrow, span), B16),
-            VMEM((2, narrow // 2, span), B16),
-            VMEM((narrow // 2, span), B16),
-            VMEM((narrow // 2, 3 * span), B16),
-            VMEM((4, 48, 3 * span), B16),
-            VMEM(pos_parts.shape, B16),
-            VMEM((pos_parts.shape[2], cells), B16),
-            VMEM((4, 48, cells), B16),
+            *folded(3, cols),
+            *folded(3, pos.shape[1] + 2 * span),
+            *folded(2, narrow),
+            VMEM((48, narrow), B16),
+            VMEM((2, 24, cells), F32),
+            VMEM((2, 24, cells), F32),
+            VMEM((2, 24, span), F32),
+            VMEM((24, span), F32),
             VMEM((narrow // 2, narrow), B16),
-            VMEM((4, 48, narrow), B16),
             VMEM((5, 24, 128), F32),
             VMEM(grads, B16),
             VMEM(bridge_grad, B16),
@@ -1478,9 +1531,9 @@
         VMEM((3, used, feats), B16),
         VMEM((2, wide, used), B16),
         VMEM((2, half, wide // 2), F32),
-        pltpu.SemaphoreType.DMA((8,)),
-        pltpu.SemaphoreType.DMA((96,)),
-        pltpu.SemaphoreType.DMA((96,)),
+        pltpu.SemaphoreType.DMA((14,)),
+        pltpu.SemaphoreType.DMA((80,)),
+        pltpu.SemaphoreType.DMA((80,)),
     ]
     return pl.pallas_call(
         functools.partial(back_kernel, cube),
@@ -1491,6 +1544,53 @@
         compiler_params=remote_params(ident),
         name="encoder_back",
     )(*args)
+
+
+def finish_kernel(step, *refs):
+    decoded, tokens, small, enc, mlp, attn, pos, bridge = refs[:8]
+    (
+        decoded_out, tokens_out, e_qkv, e_out, e_up, e_down, one_e, two_e, bridge_out, mask_out,
+        pos_out, d_qkv, d_out, d_up, d_down, one_d, two_d,
+    ) = refs[8:]
+    for i in range(2):
+        decoded_out[i] = jnp.transpose(decoded[i].astype(F32))
+    tokens_out[...] = tokens[...]
+    for source, qkv, out in ((enc, e_qkv, e_out), (attn, d_qkv, d_out)):
+        cols = qkv.shape[2]
+        for slot in range(3):
+            qkv[slot] = source[:, pl.ds(slot * cols, cols)]
+        out[...] = source[:, pl.ds(3 * cols, cols)]
+    first = 4 * e_qkv.shape[2]
+    for i in range(e_up.shape[1] // step):
+        at = pl.ds(i * step, step)
+        e_down[:, at] = enc[:, pl.ds(first + 2 * i * step, step)]
+        e_up[:, at] = enc[:, pl.ds(first + (2 * i + 1) * step, step)]
+    hidden = d_up.shape[1]
+    d_up[...] = mlp[:, :hidden]
+    d_down[...] = mlp[:, hidden:]
+    pos_out[...] = pos[...]
+    pieces = bridge.shape[0] // 2
+    for side in range(2):
+        for piece in range(pieces):
+            rows = pl.ds((side * pieces + piece) * bridge.shape[1], bridge.shape[1])
+            bridge_out[rows] = bridge[2 * piece + side].astype(F32)
+    row = 0
+    for out in (one_e, two_e, one_d, two_d, mask_out):
+        for i in range(out.shape[0] // 128):
+            out[pl.ds(i * 128, 128)] = small[row]
+            row += 1
+
+
+def finish(shapes, parts, step):
+    whole = pl.BlockSpec(memory_space=VMEM)
+    return pl.pallas_call(
+        functools.partial(finish_kernel, step),
+        out_shape=[jax.ShapeDtypeStruct(shape, F32) for shape in shapes],
+        in_specs=[whole] * len(parts),
+        out_specs=[whole] * len(shapes),
+        compiler_params=pltpu.CompilerParams(vmem_limit_bytes=LIMIT),
+        name="finish",
+    )(*parts)
 
 
 def per_device(
@@ -1523,7 +1623,7 @@
     used = -(-LONGEST // 32) * 32
 
     e_weights = (jnp.swapaxes(enc_qkv, 0, 1), enc_attn_out, enc_up, enc_down)
-    d_qkv = jnp.swapaxes(dec_qkv, 0, 1)
+    d_qkv = jnp.transpose(dec_qkv, (1, 2, 0))
     vis, d_qkv_far, d_out_far, pos_far, *saved = encoder(
         clip_lengths[:, 0],
         tokens[:, 0],
@@ -1536,13 +1636,11 @@
         used,
         1,
     )
-    cells = jnp.where(
-        jnp.arange(used) < pick(clip_lengths[:, 0], m), pick(clip_cells[:, 0], m)[:used], -1
-    )
-    decoded, pos_parts, dvis, dec_grads, dec_small = decoder(
+    decoded, dvis, dec_small, *dec_grads = decoder(
         cube,
         vis,
-        cells,
+        clip_lengths[:, 0],
+        clip_cells[:, 0],
         position_embed,
         pos_far,
         mask_token,
@@ -1560,16 +1658,42 @@
         dec_small,
         e_weights,
         dec_grads,
-        pos_parts,
+        position_embed.shape[0],
         half_slots,
         3,
     )
     if cube:
-        enc_final, dec_final, pos_final, bridge_all = rest
-        pieces = bridge_all.reshape(8, 2, -1, dec_wide)
-        bridge_grad = jnp.swapaxes(pieces, 0, 1).reshape(enc_wide, dec_wide)
+        e_own, d_own = enc_wide // owners, dec_wide // owners
+        shapes = [
+            (2, decoded.shape[2], decoded.shape[1]),
+            tokens_grad.shape,
+            (3, e_own, enc_qkv.shape[2]),
+            (e_own, enc_attn_out.shape[0]),
+            (e_own, enc_up.shape[1]),
+            (e_own, enc_down.shape[0]),
+            (enc_wide,),
+            (enc_wide,),
+            (enc_wide, dec_wide),
+            (dec_wide,),
+            (d_own, position_embed.shape[0]),
+            (3, d_own, dec_qkv.shape[2]),
+            (d_own, dec_attn_out.shape[0]),
+            (d_own, dec_up.shape[1]),
+            (d_own, dec_down.shape[0]),
+            (dec_wide,),
+            (dec_wide,),
+        ]
+        outs = list(finish(shapes, (decoded, tokens_grad, small, *rest), 512))
+        outs[0] = jnp.swapaxes(outs[0], 1, 2)[:, None]
+        outs[1] = outs[1][:, None]
+        for i in (2, 11):
+            outs[i] = jnp.swapaxes(outs[i], 0, 1)
+        for i in (3, 5, 10, 12, 14):
+            outs[i] = outs[i].T
+        return tuple(outs)
     else:
         grads, bridge = rest
+        pos_parts, dec_grads = dec_grads
         enc_final = unpack(scatter(pack(grads, owners)[None], 11), enc_wide // owners)
         packed = [
             pack(jnp.concatenate([dec_grads[side, t] for t in range(3)], 1), owners)
@@ -1605,27 +1729,29 @@
     small = small.reshape(-1)[: 2 * enc_wide + 3 * dec_wide]
     one_e, two_e, one_d, two_d, mask_grad = jnp.split(small, cuts)
 
-    def split(final, qkv, out, up):
+    def split(final, qkv, out, up, step):
         cols = qkv.shape[2]
         first = 3 * cols + out.shape[0]
         second = first + up.shape[1]
+        if step:
+            mlp = final[:, first:].reshape(final.shape[0], -1, 2, step)
+            downs, ups = (mlp[:, :, i].reshape(final.shape[0], -1) for i in range(2))
+        else:
+            downs, ups = final[:, second:], final[:, first:second]
         return (
-            final[:, : 3 * cols].reshape(-1, 3, cols),
-            final[:, 3 * cols : first].T,
-            final[:, first:second],
-            final[:, second:].T,
+            final[:, : 3 * cols].reshape(-1, 3, cols), final[:, 3 * cols : first].T, ups, downs.T
         )
 
     return (
         decoded.astype(F32)[:, None],
         tokens_grad[:, None],
-        *split(enc_final, enc_qkv, enc_attn_out, enc_up),
+        *split(enc_final, enc_qkv, enc_attn_out, enc_up, 512),
         one_e,
         two_e,
         bridge_grad.astype(F32),
         mask_grad,
         pos_final.T,
-        *split(dec_final, dec_qkv, dec_attn_out, dec_up),
+        *split(dec_final, dec_qkv, dec_attn_out, dec_up, 0),
         one_d,
         two_d,
     )

time: 246 us -> 201 us (0.82)
  the two profiles are of different devices: /device:TPU:0 before, /device:TPU:11 now
where the time goes in v4:
time: 201 us; the launch traced here: 198 us
  Pallas kernels  196 us (98%)
    pallas_call x1, Pallas kernels, back(): pl.pallas_call(functools.partial(back_kernel, cube), out_shape=outs, in_s...  85.9 us
    pallas_call x1, Pallas kernels, decoder(): pl.pallas_call(functools.partial(dec_kernel, early), out_shape=[item for...  73.2 us
    pallas_call x1, Pallas kernels, encoder(): pl.pallas_call(enc_kernel, out_shape=[item for item, _ in outs], in_specs...  32.8 us
    pallas_call x1, Pallas kernels, finish(): pl.pallas_call(functools.partial(finish_kernel, step), out_shape=[jax.Sha...  4.13 us

profile of v4, /device:TPU:11, one launch (start us, length us, event | category | flops | bytes accessed | tf_op | source)
XLA Modules:
  0.0 197.7 jit_solution(7197037981715695624)
XLA Ops:
  0.7 0.0 copy-start
  0.7 32.8 %encoder.1 = (bf16[160,384]{1,0:T(8,128)(2,1)}, bf16[3,192,384]{2,1,0:T(8,128)(2,1)}, bf16[192,384]{1,0:T(8,128)(2,1)}, bf16[784,384]{1,0:T(8,128)(2,1)}, f32[16...) custom-call(s32[2]{0:T(128)} %bitcast.36, ...), custom_call_target="tpu_custom_call" | custom-call | tf_op jit(solution)/shard_map/encoder/pallas_call | solution.py:1077
  33.5 0.0 copy-done
  33.5 0.6 copy.40
  34.1 73.2 %decoder.1 = (bf16[2,784,192]{2,1,0:T(8,128)(2,1)}, bf16[160,384]{1,0:T(8,128)(2,1)}, f32[8,384]{1,0:T(8,128)}, bf16[384,896]{1,0:T(8,128)(2,1)}, bf16[384,768]{1,0:T(8,128)(2,1)}, /*index=5*/bf16[384,768]{1,0:T(8,128)(2,1)}) custom-call(bf16[160,384]{1,0:T(8,128)(2,1)} %get-tuple-element.62.refs_0_, s32[2]{0:T(128)} %bitcast.37, s32[2,256]{1,0:T(2,128)} %bitcast.35, ...), custom_call_target="tpu_custom_call" | custom-call | tf_op jit(solution)/shard_map/decoder/pallas_call | solution.py:796
  107.3 85.9 %encoder_back.1 = (f32[2,128,384]{2,1,0:T(8,128)}, f32[24,128]{1,0:T(8,128)}, f32[48,4608]{1,0:T(8,128)}, f32[24,1536]{1,0:T(8,128)}, f32[24,768]{1,0:T(8,128)},...) custom-call(bf16[160,384]{1,0:T(8,128)(2,1)} %get-tuple-element.67.refs_0_, bf16[768,384]{1,0:T(8,128)(2,1)} %refs_1_.1, ...), custom_call_target="tpu_custom_call" | custom-call | tf_op jit(solution)/shard_map/encoder_back/pallas_call | solution.py:1538
  193.1 4.1 %finish.1 = (f32[2,192,784]{2,1,0:T(8,128)}, f32[2,128,384]{2,1,0:T(8,128)}, f32[3,48,384]{2,1,0:T(8,128)}, f32[48,384]{1,0:T(8,128)}, f32[48,1536]{1,0:T(8,128)...) custom-call(bf16[2,784,192]{2,1,0:T(8,128)(2,1)} %get-tuple-element., ...), custom_call_target="tpu_custom_call" | custom-call | tf_op jit(solution)/shard_map/finish/pallas_call | solution.py:1586
Async XLA Ops:
  0.7 32.8 %copy-start = (s32[2,1,256]{2,1,0:T(1,128)S(1)}, s32[2,1,256]{2,1,0:T(1,128)}, u32[]{:S(2)}) copy-start(s32[2,1,256]{2,1,0:T(1,128)} %param.21) | copy-start | bytes 6148

commit v5 on v4

--- a/solution.py
+++ b/solution.py
@@ -345,15 +345,15 @@
 def dec_kernel(early, *refs):
     (
         vis_ref, lengths, cells_ref, pos_own, pos_far, mask_ref, gain1_ref, gain2_ref,
-        qkv_own, qkv_far, out_own, out_far, up_hbm, down_hbm, cot_hbm,
-        routed, dvis_out, small_out, *refs,
+        qkv_own, qkv_far, out_own, up_hbm, down_hbm, cot_hbm, enc_hbm,
+        routed, dvis_out, small_out, enc_half, *refs,
     ) = refs
     if early:
         pos_out, attn_out, mlp_out, grad_out, *refs = refs
     else:
         pos_out, grad_out, *refs = refs
     (
-        dec_out, w_up, w_down, cot, z1, unit1, a_ref, q_ref, keys, values, probs, stats,
+        dec_out, out_far, w_up, w_down, cot, z1, unit1, a_ref, q_ref, keys, values, probs, stats,
         o_ref, unit2, b_ref, h_ref, slope, z2, do_ref, flip, dkt, dvt, got_kv,
         dvis_mine, dvis_near, dvis_far, free_sem, local_sem, send_sem, recv_sem,
     ) = refs
@@ -378,18 +378,24 @@
     for load in loads:
         load.start()
     over, share = [], []
-    for hbm, held in ((up_hbm, w_up), (down_hbm, w_down)):
-        half = hbm.shape[0] // 2
+    for own, held in ((out_own, out_far), (up_hbm, w_up.at[1]), (down_hbm, w_down.at[1])):
+        half = own.shape[0] // 2
         mine = pl.ds(s * half, half)
-        over.append(wire.copy(hbm.at[mine], held.at[1, mine], facing))
-        share.append(wire.copy(held.at[1, mine], held.at[1, mine], sibling))
+        over.append(wire.copy(own.at[mine], held.at[mine], facing))
+        share.append(wire.copy(held.at[mine], held.at[mine], sibling))
         over[-1].start()
     cot_over = wire.copy(cot_hbm.at[1 - m], cot, facing)
+    mid = enc_hbm.shape[1] // 2
+    enc_parts = [enc_hbm.at[:, pl.ds(pl.multiple_of(k * mid, 128), mid)] for k in (m, 1 - m)]
+    enc_load = pltpu.make_async_copy(enc_parts[0], enc_half, local_sem.at[6])
+    enc_over = wire.copy(enc_parts[1], enc_half, facing)
 
     @pl.when(stays)
     def _():
         cot_load.start()
         cot_over.start()
+        enc_load.start()
+        enc_over.start()
 
     lane = lax.broadcasted_iota(jnp.int32, (1, 128), 1)
 
@@ -468,6 +474,7 @@
     for copy, other in zip(over, share):
         copy.wait()
         other.start()
+    share[0].wait()
 
     z2[...] = z1[...] + dot_nn(o_ref[0], out_own[...]) + dot_nn(o_ref[1], out_far[...])
 
@@ -481,7 +488,7 @@
     each(length // rows_at, second)
     for load in loads:
         load.wait()
-    for copy in share:
+    for copy in share[1:]:
         copy.wait()
 
     step = 256
@@ -525,10 +532,13 @@
     def _():
         cot_load.wait()
         cot_over.wait_send()
+        enc_load.wait()
+        enc_over.wait_send()
 
     @pl.when(jnp.logical_not(stays))
     def _():
         cot_over.wait_recv()
+        enc_over.wait_recv()
 
     def transposed(value):
         return jnp.transpose(value.astype(F32)).astype(B16)
@@ -730,42 +740,50 @@
     place = jnp.where(cells_col == ids, 1.0, 0.0).astype(B16)
     dvis_mine[...] = dot_nn(place, b_ref[...]).astype(B16)
     dvis_pair = wire.copy(dvis_mine, dvis_near, sibling)
-    dvis_pair.start()
+    dvis_over = wire.copy(dvis_mine, dvis_far, facing)
+    dvis_cross = wire.copy(dvis_mine, dvis_near, beyond)
+
+    @pl.when(stays)
+    def _():
+        dvis_over.start()
+
+    @pl.when(jnp.logical_not(stays))
+    def _():
+        dvis_pair.start()
+        dvis_cross.start()
 
     if early:
         halves = [jnp.transpose(dec_out[half].astype(F32)) for half in range(2)]
         stores.append(stage(0, halves, pos_out, local_sem.at[0]))
-    dvis_pair.wait()
-    dvis_mine[...] = (dvis_mine[...].astype(F32) + dvis_near[...].astype(F32)).astype(B16)
-    dvis_over = wire.copy(dvis_mine, dvis_far, facing)
-
-    @pl.when(stays)
-    def _():
-        dvis_over.start()
-        dvis_out[...] = dvis_mine[...]
-
-    @pl.when(stays)
-    def _():
-        dvis_over.wait_send()
-
-    @pl.when(jnp.logical_not(stays))
-    def _():
-        dvis_over.wait_recv()
-        dvis_out[...] = dvis_far[...]
-
-    if early:
         halves = []
         for side, (held, copy) in zip((1, 0), attn_pairs):
             copy.wait()
             halves.insert(0, held[...].astype(F32) + grad_out[side, 0, mine_grads].astype(F32))
         stores.append(stage(1, halves, attn_out, local_sem.at[2]))
 
+    def dvis_sum(first, second):
+        dvis_out[...] = (first[...].astype(F32) + second[...].astype(F32)).astype(B16)
+
+    @pl.when(stays)
+    def _():
+        dvis_pair.wait_recv()
+        dvis_sum(dvis_mine, dvis_near)
+        dvis_over.wait_send()
+
+    @pl.when(jnp.logical_not(stays))
+    def _():
+        dvis_over.wait_recv()
+        dvis_cross.wait_recv()
+        dvis_sum(dvis_far, dvis_near)
+        dvis_pair.wait_send()
+        dvis_cross.wait_send()
+
     for copy in stores:
         copy.wait()
 
 
-def decoder(early, vis, lengths, cells, pos_own, pos_far, mask, gains, weights, cot, ident):
-    qkv_own, qkv_far, out_own, out_far, up, down = weights
+def decoder(early, vis, lengths, cells, pos_own, pos_far, mask, gains, weights, cot, enc, ident):
+    qkv_own, qkv_far, out_own, up, down = weights
     length, wide = pos_own.shape
     used = vis.shape[0]
     third = wide // 2
@@ -780,6 +798,7 @@
         (jax.ShapeDtypeStruct((2, length, third), B16), there),
         (jax.ShapeDtypeStruct((used, wide), B16), whole),
         (jax.ShapeDtypeStruct((8, wide), F32), whole),
+        (jax.ShapeDtypeStruct((used, enc.shape[1] // 2), B16), there),
     ]
     if early:
         lanes = -(-length // 128) * 128
@@ -798,12 +817,13 @@
         out_shape=[item for item, _ in outs],
         in_specs=[whole, pl.BlockSpec(memory_space=pltpu.SMEM), whole]
         + [there] * 2
-        + [whole] * 7
-        + [there] * 3,
+        + [whole] * 6
+        + [there] * 4,
         out_specs=[spec for _, spec in outs],
         scratch_shapes=[VMEM(grads, B16)] * early
         + [
             VMEM((2, length, third), B16),
+            VMEM(out_own.shape, B16),
             VMEM((2, wide, hidden), B16),
             VMEM((2, hidden, wide), B16),
             VMEM((length, wide), B16),
@@ -830,9 +850,9 @@
             VMEM((used, wide), B16),
             VMEM((used, wide), B16),
             pltpu.SemaphoreType.REGULAR,
-            pltpu.SemaphoreType.DMA((6,)),
-            pltpu.SemaphoreType.DMA((32,)),
-            pltpu.SemaphoreType.DMA((32,)),
+            pltpu.SemaphoreType.DMA((7,)),
+            pltpu.SemaphoreType.DMA((40,)),
+            pltpu.SemaphoreType.DMA((40,)),
         ],
         compiler_params=pltpu.CompilerParams(
             collective_id=ident, has_side_effects=True, vmem_limit_bytes=int(63.9 * 1024) * 1024
@@ -850,10 +870,10 @@
         qkv_own,
         qkv_far,
         out_own,
-        out_far,
         up,
         down,
         cot,
+        enc,
     )
 
 
@@ -879,10 +899,10 @@
 def enc_kernel(*refs):
     (
         length_ref, tok_hbm, qkv_hbm, out_hbm, up_hbm, down_hbm, bridge_ref, gain1_ref, gain2_ref,
-        pos_hbm, dqkv_hbm, dout_hbm,
-        vis_out, dqkv_far, dout_far, pos_far, unit1, unit2, stats, a_ref, triple, probs, o_ref, b_ref,
-        slope, h_ref, enc_half,
-        x_ref, qkv, w_out, w_up, w_down, z2, part_ref, part_far, enc_ref, pos_full, pos_half,
+        pos_hbm, dqkv_hbm,
+        vis_out, dqkv_far, pos_far, enc_ref, unit1, unit2, stats, a_ref, triple, probs, o_ref, b_ref,
+        slope, h_ref,
+        x_ref, qkv, w_out, w_up, w_down, z2, part_ref, part_far, pos_full, pos_half,
         local_sem, send_sem, recv_sem,
     ) = refs
     s, d, m = place_of()
@@ -893,7 +913,10 @@
     rest = used - half
     wire = Wire(send_sem, recv_sem)
 
-    greet([sibling, facing])
+    y = lax.rem(d, 2)
+    beside = (s, d + 1 - 2 * y, m)
+
+    greet([sibling, facing, beside])
     first, last = pl.ds(0, half), pl.ds(half, rest)
     tok_first = wire.copy(tok_hbm.at[s], x_ref.at[first], facing)
     tok_last = wire.copy(tok_hbm.at[s, pl.ds(0, rest)], x_ref.at[last], facing)
@@ -919,13 +942,22 @@
         )
     ]
     pos_load = fetch(pos_hbm, pos_full, local_sem.at[5])
-    over, share = [], []
-    for hbm, held in ((dqkv_hbm, dqkv_far), (dout_hbm, dout_far)):
-        at = (slice(None),) * (len(hbm.shape) - 2)
-        size = hbm.shape[-2] // 2
-        mine = at + (pl.ds(s * size, size),)
-        over.append(wire.copy(hbm.at[mine], held.at[mine], facing))
-        share.append(wire.copy(held.at[mine], held.at[mine], sibling))
+    size = dqkv_hbm.shape[1] // 2
+    mine = (slice(None), pl.ds(s * size, size))
+    over = wire.copy(dqkv_hbm.at[mine], dqkv_far.at[mine], facing)
+    share = wire.copy(dqkv_far.at[mine], dqkv_far.at[mine], sibling)
+
+    low = pos_hbm.shape[0] // 32 * 16
+    pos_parts = [pl.ds(0, low), pl.ds(low, pos_hbm.shape[0] - low)]
+    pos_over = [wire.copy(pos_half.at[part], pos_far.at[part], facing) for part in pos_parts]
+    pos_trade = [wire.copy(pos_far.at[part], pos_far.at[part], beside) for part in pos_parts]
+
+    def by_place(on_stays, act):
+        for part in range(2):
+
+            @pl.when(jnp.logical_and(stays if on_stays else jnp.logical_not(stays), y == part))
+            def _(part=part):
+                act(part)
 
     @pl.when(m == 0)
     def _():
@@ -939,8 +971,14 @@
         tok_last.wait_send()
         tok_first.wait_recv()
 
-    for copy in over:
-        copy.start()
+    over.start()
+    pos_load.wait()
+
+    def send_positions(part):
+        pos_half[pos_parts[part]] = pos_full[pos_parts[part]].astype(B16)
+        pos_over[part].start()
+
+    by_place(True, send_positions)
 
     lane = lax.broadcasted_iota(jnp.int32, (1, 128), 1)
 
@@ -975,14 +1013,6 @@
     attn.start()
     z2[...] = x_ref[...].astype(F32) + part
 
-    pos_load.wait()
-    pos_over = wire.copy(pos_half, pos_far, facing)
-
-    @pl.when(stays)
-    def _():
-        pos_half[...] = pos_full[...].astype(B16)
-        pos_over.start()
-
     attn.wait()
     z = z2[...] + part_far[0].astype(F32)
     z2[...] = z
@@ -1003,53 +1033,54 @@
         slope[:, cols] = (phi + u * bell).astype(B16)
 
     each(w_up.shape[1] // step, up)
+
+    over.wait()
+    share.start()
+
+    def trade_positions(part):
+        pos_over[part].wait_recv()
+        pos_trade[part].start()
+
+    by_place(False, trade_positions)
     loads[3].wait()
     part = dot_nn(h_ref[...], w_down[...])
     z2[...] = z2[...] + part
     part_ref[1] = part.astype(B16)
     mlp = wire.copy(part_ref.at[1], part_far.at[1], facing)
     vis_near = wire.copy(vis_out, vis_out, sibling)
-    mid = wide // 2
-    enc_over = wire.copy(
-        enc_ref.at[:, pl.ds(pl.multiple_of((1 - m) * mid, 128), mid)], enc_half, facing
-    )
 
     @pl.when(stays)
     def _():
         mlp.wait_recv()
         enc = (z2[...] + part_far[1].astype(F32)).astype(B16)
         enc_ref[...] = enc
-        enc_over.start()
         vis_out[...] = dot_nn(enc, bridge_ref[...]).astype(B16)
         vis_near.start()
-        enc_half[...] = enc_ref[:, pl.ds(pl.multiple_of(m * mid, 128), mid)]
 
     @pl.when(jnp.logical_not(stays))
     def _():
         mlp.start()
-
-    for copy, other in zip(over, share):
-        copy.wait()
-        other.start()
+        enc_ref[...] = jnp.zeros(enc_ref.shape, B16)
 
     @pl.when(stays)
     def _():
         vis_near.wait_send()
-        enc_over.wait_send()
-        pos_over.wait_send()
 
     @pl.when(jnp.logical_not(stays))
     def _():
         mlp.wait_send()
         vis_near.wait_recv()
-        enc_over.wait_recv()
-        pos_over.wait_recv()
-
-    for copy in share:
-        copy.wait()
-
-
-def encoder(lengths, tokens, weights, bridge, gains, pos, dqkv, dout, used, ident):
+
+    def finish_positions(part):
+        pos_trade[part].wait_send()
+        pos_trade[1 - part].wait_recv()
+
+    by_place(True, lambda part: pos_over[part].wait_send())
+    by_place(False, finish_positions)
+    share.wait()
+
+
+def encoder(lengths, tokens, weights, bridge, gains, pos, dqkv, used, ident):
     qkv, out, up, down = weights
     wide = tokens.shape[2]
     feats = qkv.shape[2]
@@ -1058,10 +1089,10 @@
     there = pl.BlockSpec(memory_space=pl.ANY)
     shape = jax.ShapeDtypeStruct
     outs = [
-        (shape((used, dout.shape[1]), B16), whole),
+        (shape((used, pos.shape[1]), B16), whole),
         (shape(dqkv.shape, B16), there),
-        (shape(dout.shape, B16), there),
         (shape(pos.shape, B16), there),
+        (shape((used, wide), B16), whole),
         (shape((used, wide), F32), whole),
         (shape((used, wide), F32), whole),
         (shape((used, 128), F32), whole),
@@ -1072,7 +1103,6 @@
         (shape((used, wide), B16), whole),
         (shape((used, hidden), B16), whole),
         (shape((used, hidden), B16), whole),
-        (shape((used, wide // 2), B16), whole),
     ]
     return pl.pallas_call(
         enc_kernel,
@@ -1080,7 +1110,7 @@
         in_specs=[pl.BlockSpec(memory_space=pltpu.SMEM)]
         + [there] * 5
         + [whole] * 3
-        + [there] * 3,
+        + [there] * 2,
         out_specs=[spec for _, spec in outs],
         scratch_shapes=[
             VMEM((used, wide), B16),
@@ -1091,7 +1121,6 @@
             VMEM((used, wide), F32),
             VMEM((2, used, wide), B16),
             VMEM((2, used, wide), B16),
-            VMEM((used, wide), B16),
             VMEM(pos.shape, F32),
             VMEM(pos.shape, B16),
             pltpu.SemaphoreType.DMA((6,)),
@@ -1102,7 +1131,7 @@
         name="encoder",
     )(
         lengths, tokens, qkv, out, up, down, bridge, gains[0], gains[1],
-        pos, dqkv, dout,
+        pos, dqkv,
     )
 
 
@@ -1164,9 +1193,11 @@
         ]
         for copy in early_loads:
             copy.wait()
-        orders = ("yab", "ayb", "yab")
+        orders = ("yab", "ayb", "yab", "yab")
+        mlp_orders = (("yab", "ayb"), ("yab", "ayb"), ("ayb", "yab"))
+        attn_orders = ("yab", "yab", "ayb", "ayb")
         tiles = (pos_lanes + 2 * span) // 128
-        cuts = [128 * (tiles * i // 3) for i in range(4)]
+        cuts = [128 * (tiles * i // 4) for i in range(5)]
         early_folds = [
             Fold(
                 wire, chip, dec_held, (dec_box0, dec_box1, dec_box2), pl.ds(low, high - low), "yab",
@@ -1205,13 +1236,12 @@
         away_rows = pl.ds(pl.multiple_of((1 - s) * section, 16), section)
 
         class Group:
-            def __init__(self, first, size, order):
-                self.lanes = pl.ds(first, size)
+            def __init__(self, first, size, orders):
+                self.lanes, self.orders = pl.ds(first, size), orders
                 self.pair = wire.copy(
                     grads.at[away_rows, self.lanes], near.at[:, self.lanes], sibling
                 )
                 self.pair.start()
-                self.order = order
 
             def start(self):
                 self.pair.wait()
@@ -1220,13 +1250,25 @@
                     from_rows = pl.ds(pl.multiple_of(s * section + 48 * owner, 16), 48)
                     index = (owner % 2,) + Chip.place(owner // 2) + (slice(None), self.lanes)
                     held[index] = near[rows, self.lanes] + grads[from_rows, self.lanes]
-                self.fold = Fold(
-                    wire, chip, held, (box0, box1, box2), self.lanes, "yab", self.order, False
-                )
-                self.fold.start()
+                part = self.lanes.size // len(self.orders)
+                self.folds = [
+                    Fold(
+                        wire, chip, held, (box0, box1, box2), pl.ds(self.lanes.start + i * part, part),
+                        "yab", order, False,
+                    )
+                    for i, order in enumerate(self.orders)
+                ]
+                for fold in self.folds:
+                    fold.start()
+
+            def step(self, k):
+                for fold in self.folds:
+                    fold.step(k)
 
             def end(self):
-                enc_out[:, self.lanes] = self.fold.end()
+                part = self.lanes.size // len(self.folds)
+                for i, fold in enumerate(self.folds):
+                    enc_out[:, pl.ds(self.lanes.start + i * part, part)] = fold.end()
 
         mlp_groups = []
 
@@ -1238,7 +1280,7 @@
         gu[:, cols] = grad_u
         grads[:, pl.ds(first_mlp + (2 * i + 1) * step, step)] = dot_nn(flip[1], grad_u).astype(B16)
         if cube:
-            mlp_groups.append(Group(first_mlp + 2 * i * step, 2 * step, orders[i % 3]))
+            mlp_groups.append(Group(first_mlp + 2 * i * step, 2 * step, mlp_orders[i % 3]))
             if i:
                 mlp_groups[i - 1].start()
 
@@ -1271,7 +1313,7 @@
     do_ref[...] = dot_nt(grad_a, w_out[...]).astype(B16)
 
     if cube:
-        out_group = Group(3 * feats, feats, orders[0])
+        out_group = Group(3 * feats, feats, attn_orders[3:])
         bridge_pair.wait()
         narrow = bridge_near.shape[1]
         for at in range(4):
@@ -1340,7 +1382,7 @@
 
     if cube:
         attn_groups = [
-            Group(i * feats, feats, order) for i, order in enumerate(orders)
+            Group(i * feats, feats, (order,)) for i, order in enumerate(attn_orders[:3])
         ]
         small_copies = [
             wire.copy(small_out, small_box.at[i], partner)
@@ -1384,10 +1426,10 @@
     tok_out[s] = tok_part[s]
 
     if cube:
-        for group in mlp_groups:
-            group.fold.step(0)
         for fold in early_folds:
             fold.step(1)
+        for group in mlp_groups:
+            group.step(0)
         small_step(1)
 
         slot = (s * 4 + z) * 2 + m
@@ -1399,12 +1441,12 @@
         for copy in spread:
             copy.start()
 
-        out_group.fold.step(0)
+        out_group.step(0)
         for group in attn_groups:
-            group.fold.step(0)
+            group.step(0)
         small_step(2)
         for group in mlp_groups:
-            group.fold.step(1)
+            group.step(1)
 
         wholes = jnp.concatenate([fold.end() for fold in early_folds], 1)
         for half_at in range(2):
@@ -1429,14 +1471,14 @@
             route_far.start()
 
 
-        out_group.fold.step(1)
+        out_group.step(1)
         for copy in spread:
             copy.wait()
         ours = pl.ds(s * 8, 8)
         bridge_pair_all = wire.copy(bridge_all.at[ours], bridge_all.at[ours], sibling)
         bridge_pair_all.start()
         for group in attn_groups:
-            group.fold.step(1)
+            group.step(1)
         small_step(3)
         for group in mlp_groups:
             group.end()
@@ -1532,8 +1574,8 @@
         VMEM((2, wide, used), B16),
         VMEM((2, half, wide // 2), F32),
         pltpu.SemaphoreType.DMA((14,)),
-        pltpu.SemaphoreType.DMA((80,)),
-        pltpu.SemaphoreType.DMA((80,)),
+        pltpu.SemaphoreType.DMA((96,)),
+        pltpu.SemaphoreType.DMA((96,)),
     ]
     return pl.pallas_call(
         functools.partial(back_kernel, cube),
@@ -1624,7 +1666,7 @@
 
     e_weights = (jnp.swapaxes(enc_qkv, 0, 1), enc_attn_out, enc_up, enc_down)
     d_qkv = jnp.transpose(dec_qkv, (1, 2, 0))
-    vis, d_qkv_far, d_out_far, pos_far, *saved = encoder(
+    vis, d_qkv_far, pos_far, enc, *saved = encoder(
         clip_lengths[:, 0],
         tokens[:, 0],
         e_weights,
@@ -1632,11 +1674,10 @@
         (enc_gain_one, enc_gain_two),
         position_embed,
         d_qkv,
-        dec_attn_out,
         used,
         1,
     )
-    decoded, dvis, dec_small, *dec_grads = decoder(
+    decoded, dvis, dec_small, enc_half, *dec_grads = decoder(
         cube,
         vis,
         clip_lengths[:, 0],
@@ -1645,8 +1686,9 @@
         pos_far,
         mask_token,
         (dec_gain_one, dec_gain_two),
-        (d_qkv, d_qkv_far, dec_attn_out, d_out_far, dec_up, dec_down),
+        (d_qkv, d_qkv_far, dec_attn_out, dec_up, dec_down),
         cotangent[:, 0],
+        enc,
         2,
     )
     tokens_grad, small, *rest = back(
@@ -1654,7 +1696,7 @@
         dvis,
         bridge_weight,
         (enc_gain_one, enc_gain_two),
-        saved,
+        (*saved, enc_half),
         dec_small,
         e_weights,
         dec_grads,

time: 201 us -> 193 us (0.960)
  the two profiles are of different devices: /device:TPU:11 before, /device:TPU:18 now
where the time goes in v5:
time: 193 us; the launch traced here: 190 us
  Pallas kernels  189 us (98%)
    pallas_call x1, Pallas kernels, back(): pl.pallas_call(functools.partial(back_kernel, cube), out_shape=outs, in_s...  80.8 us
    pallas_call x1, Pallas kernels, decoder(): pl.pallas_call(functools.partial(dec_kernel, early), out_shape=[item for...  71.5 us
    pallas_call x1, Pallas kernels, encoder(): pl.pallas_call(enc_kernel, out_shape=[item for item, _ in outs], in_specs...  32.3 us
    pallas_call x1, Pallas kernels, finish(): pl.pallas_call(functools.partial(finish_kernel, step), out_shape=[jax.Sha...  4.13 us

profile of v5, /device:TPU:18, one launch (start us, length us, event | category | flops | bytes accessed | tf_op | source)
XLA Modules:
  0.0 190.5 jit_solution(9675899947942811209)
XLA Ops:
  0.7 0.0 copy-start
  0.7 32.3 %encoder.1 = (bf16[160,384]{1,0:T(8,128)(2,1)}, bf16[3,192,384]{2,1,0:T(8,128)(2,1)}, bf16[784,384]{1,0:T(8,128)(2,1)}, bf16[160,768]{1,0:T(8,128)(2,1)}, f32[16...) custom-call(s32[2]{0:T(128)} %bitcast.36, ...), custom_call_target="tpu_custom_call" | custom-call | tf_op jit(solution)/shard_map/encoder/pallas_call | solution.py:1107
  33.0 0.0 copy-done
  33.0 0.6 copy.40
  33.6 71.5 %decoder.1 = (bf16[2,784,192]{2,1,0:T(8,128)(2,1)}, bf16[160,384]{1,0:T(8,128)(2,1)}, f32[8,384]{1,0:T(8,128)}, bf16[160,384]{1,0:T(8,128)(2,1)}, bf16[384,896]{...) custom-call(bf16[160,384]{1,0:T(8,128)(2,1)} %get-tuple-element.62.refs_0_, s32[2]{0:T(128)} %bitcast.37, ...), custom_call_target="tpu_custom_call" | custom-call | tf_op jit(solution)/shard_map/decoder/pallas_call | solution.py:815
  105.1 80.8 %encoder_back.1 = (f32[2,128,384]{2,1,0:T(8,128)}, f32[24,128]{1,0:T(8,128)}, f32[48,4608]{1,0:T(8,128)}, f32[24,1536]{1,0:T(8,128)}, f32[24,768]{1,0:T(8,128)},...) custom-call(bf16[160,384]{1,0:T(8,128)(2,1)} %get-tuple-element.67.refs_0_, bf16[768,384]{1,0:T(8,128)(2,1)} %refs_1_.1, ...), custom_call_target="tpu_custom_call" | custom-call | tf_op jit(solution)/shard_map/encoder_back/pallas_call | solution.py:1580
  185.9 4.1 %finish.1 = (f32[2,192,784]{2,1,0:T(8,128)}, f32[2,128,384]{2,1,0:T(8,128)}, f32[3,48,384]{2,1,0:T(8,128)}, f32[48,384]{1,0:T(8,128)}, f32[48,1536]{1,0:T(8,128)...) custom-call(bf16[2,784,192]{2,1,0:T(8,128)(2,1)} %get-tuple-element., ...), custom_call_target="tpu_custom_call" | custom-call | tf_op jit(solution)/shard_map/finish/pallas_call | solution.py:1628
Async XLA Ops:
  0.7 32.3 %copy-start = (s32[2,1,256]{2,1,0:T(1,128)S(1)}, s32[2,1,256]{2,1,0:T(1,128)}, u32[]{:S(2)}) copy-start(s32[2,1,256]{2,1,0:T(1,128)} %param.21) | copy-start | bytes 6148

commit v6 on v5

--- a/solution.py
+++ b/solution.py
@@ -1168,17 +1168,10 @@
     if cube:
         chip = Chip(s, d, m)
         z, y = chip.z, chip.me["y"]
-        others = [(s, 2 * lax.rem(z + k, 4) + y, lax.rem(m + side, 2)) for k in (1, 2, 3) for side in (0, 1)]
+        others = [(s, 2 * lax.rem(z + k, 4) + y, m) for k in (1, 2, 3)]
         greet([sibling, facing, (1 - s, d, 1 - m), chip.near[0]] + others)
     else:
         greet([sibling, facing])
-
-    loads = [
-        fetch(hbm, held, local_sem.at[i])
-        for i, (hbm, held) in enumerate(
-            ((down_hbm, w_down), (up_hbm, w_up), (out_hbm, w_out), (qkv_hbm, qkv))
-        )
-    ]
 
     if cube:
         cells = pos_sum.shape[2]
@@ -1208,6 +1201,13 @@
         for fold in early_folds:
             fold.start()
 
+    loads = [
+        fetch(hbm, held, local_sem.at[i])
+        for i, (hbm, held) in enumerate(
+            ((down_hbm, w_down), (up_hbm, w_up), (out_hbm, w_out), (qkv_hbm, qkv))
+        )
+    ]
+
     def transposed(value):
         return jnp.transpose(value.astype(F32)).astype(B16)
 
@@ -1432,11 +1432,9 @@
             group.step(0)
         small_step(1)
 
-        slot = (s * 4 + z) * 2 + m
-        bridge_all[slot] = bridge_fold.end().astype(B16)
+        bridge_all[s, z, m] = bridge_fold.end().astype(B16)
         spread = [
-            wire.copy(bridge_all.at[slot], bridge_all.at[slot], partner)
-            for partner in [facing] + others
+            wire.copy(bridge_all.at[s, z, m], bridge_all.at[s, z, m], partner) for partner in others
         ]
         for copy in spread:
             copy.start()
@@ -1474,9 +1472,8 @@
         out_group.step(1)
         for copy in spread:
             copy.wait()
-        ours = pl.ds(s * 8, 8)
-        bridge_pair_all = wire.copy(bridge_all.at[ours], bridge_all.at[ours], sibling)
-        bridge_pair_all.start()
+        bridge_over = wire.copy(bridge_all.at[s, :, m], bridge_all.at[s, :, m], facing)
+        bridge_over.start()
         for group in attn_groups:
             group.step(1)
         small_step(3)
@@ -1499,6 +1496,9 @@
 
         pos_out[...] = pos_got[0] + pos_got[1]
         out_group.end()
+        bridge_over.wait()
+        bridge_pair_all = wire.copy(bridge_all.at[s], bridge_all.at[s], sibling)
+        bridge_pair_all.start()
         small_step(4)
         for group in attn_groups:
             group.end()
@@ -1535,7 +1535,7 @@
             shape((24, 2 * span), F32),
             shape((24, span), F32),
             shape((24, cells), F32),
-            shape((16, 48, narrow), B16),
+            shape((2, 4, 2, 48, narrow), B16),
         ]
 
         def folded(axes, size):
@@ -1611,11 +1611,11 @@
     d_up[...] = mlp[:, :hidden]
     d_down[...] = mlp[:, hidden:]
     pos_out[...] = pos[...]
-    pieces = bridge.shape[0] // 2
+    own = bridge.shape[3]
     for side in range(2):
-        for piece in range(pieces):
-            rows = pl.ds((side * pieces + piece) * bridge.shape[1], bridge.shape[1])
-            bridge_out[rows] = bridge[2 * piece + side].astype(F32)
+        for piece in range(8):
+            rows = pl.ds((side * 8 + piece) * own, own)
+            bridge_out[rows] = bridge[piece // 4, piece % 4, side].astype(F32)
     row = 0
     for out in (one_e, two_e, one_d, two_d, mask_out):
         for i in range(out.shape[0] // 128):

time: 193 us -> 191 us (0.990)
  the two profiles are of different devices: /device:TPU:18 before, /device:TPU:17 now
where the time goes in v6:
time: 191 us; the launch traced here: 188 us
  Pallas kernels  186 us (97%)
    pallas_call x1, Pallas kernels, back(): pl.pallas_call(functools.partial(back_kernel, cube), out_shape=outs, in_s...  77.4 us
    pallas_call x1, Pallas kernels, decoder(): pl.pallas_call(functools.partial(dec_kernel, early), out_shape=[item for...  71.4 us
    pallas_call x1, Pallas kernels, encoder(): pl.pallas_call(enc_kernel, out_shape=[item for item, _ in outs], in_specs...  33.1 us
    pallas_call x1, Pallas kernels, finish(): pl.pallas_call(functools.partial(finish_kernel, step), out_shape=[jax.Sha...  4.13 us

profile of v6, /device:TPU:17, one launch (start us, length us, event | category | flops | bytes accessed | tf_op | source)
XLA Modules:
  0.0 187.7 jit_solution(4077328295888443656)
XLA Ops:
  0.7 0.0 copy-start
  0.7 33.1 %encoder.1 = (bf16[160,384]{1,0:T(8,128)(2,1)}, bf16[3,192,384]{2,1,0:T(8,128)(2,1)}, bf16[784,384]{1,0:T(8,128)(2,1)}, bf16[160,768]{1,0:T(8,128)(2,1)}, f32[16...) custom-call(s32[2]{0:T(128)} %bitcast.36, ...), custom_call_target="tpu_custom_call" | custom-call | tf_op jit(solution)/shard_map/encoder/pallas_call | solution.py:1107
  33.8 0.0 copy-done
  33.8 0.6 copy.40
  34.3 71.4 %decoder.1 = (bf16[2,784,192]{2,1,0:T(8,128)(2,1)}, bf16[160,384]{1,0:T(8,128)(2,1)}, f32[8,384]{1,0:T(8,128)}, bf16[160,384]{1,0:T(8,128)(2,1)}, bf16[384,896]{...) custom-call(bf16[160,384]{1,0:T(8,128)(2,1)} %get-tuple-element.62.refs_0_, s32[2]{0:T(128)} %bitcast.37, ...), custom_call_target="tpu_custom_call" | custom-call | tf_op jit(solution)/shard_map/decoder/pallas_call | solution.py:815
  105.8 77.4 %encoder_back.1 = (f32[2,128,384]{2,1,0:T(8,128)}, f32[24,128]{1,0:T(8,128)}, f32[48,4608]{1,0:T(8,128)}, f32[24,1536]{1,0:T(8,128)}, f32[24,768]{1,0:T(8,128)},...) custom-call(bf16[160,384]{1,0:T(8,128)(2,1)} %get-tuple-element.67.refs_0_, bf16[768,384]{1,0:T(8,128)(2,1)} %refs_1_.1, ...), custom_call_target="tpu_custom_call" | custom-call | tf_op jit(solution)/shard_map/encoder_back/pallas_call | solution.py:1580
  183.1 4.1 %finish.1 = (f32[2,192,784]{2,1,0:T(8,128)}, f32[2,128,384]{2,1,0:T(8,128)}, f32[3,48,384]{2,1,0:T(8,128)}, f32[48,384]{1,0:T(8,128)}, f32[48,1536]{1,0:T(8,128)...) custom-call(bf16[2,784,192]{2,1,0:T(8,128)(2,1)} %get-tuple-element., ...), custom_call_target="tpu_custom_call" | custom-call | tf_op jit(solution)/shard_map/finish/pallas_call | solution.py:1628
Async XLA Ops:
  0.7 33.1 %copy-start = (s32[2,1,256]{2,1,0:T(1,128)S(1)}, s32[2,1,256]{2,1,0:T(1,128)}, u32[]{:S(2)}) copy-start(s32[2,1,256]{2,1,0:T(1,128)} %param.21) | copy-start | bytes 6148

commit v7 on v6

--- a/solution.py
+++ b/solution.py
@@ -935,13 +935,13 @@
         tok_last.start()
         own_last.start()
 
+    pos_load = fetch(pos_hbm, pos_full, local_sem.at[5])
     loads = [
         fetch(hbm, held, local_sem.at[i + 1])
         for i, (hbm, held) in enumerate(
             ((qkv_hbm, qkv), (out_hbm, w_out), (up_hbm, w_up), (down_hbm, w_down))
         )
     ]
-    pos_load = fetch(pos_hbm, pos_full, local_sem.at[5])
     size = dqkv_hbm.shape[1] // 2
     mine = (slice(None), pl.ds(s * size, size))
     over = wire.copy(dqkv_hbm.at[mine], dqkv_far.at[mine], facing)

time: 191 us -> 191 us (level)
  no operation moved by 1% of the time
where the time goes in v7:
time: 191 us; the launch traced here: 188 us
  Pallas kernels  186 us (97%)
    pallas_call x1, Pallas kernels, back(): pl.pallas_call(functools.partial(back_kernel, cube), out_shape=outs, in_s...  77.4 us
    pallas_call x1, Pallas kernels, decoder(): pl.pallas_call(functools.partial(dec_kernel, early), out_shape=[item for...  71.4 us
    pallas_call x1, Pallas kernels, encoder(): pl.pallas_call(enc_kernel, out_shape=[item for item, _ in outs], in_specs...  33.1 us
    pallas_call x1, Pallas kernels, finish(): pl.pallas_call(functools.partial(finish_kernel, step), out_shape=[jax.Sha...  4.13 us

profile of v7, /device:TPU:17, one launch (start us, length us, event | category | flops | bytes accessed | tf_op | source)
XLA Modules:
  0.0 187.7 jit_solution(3937907813335198075)
XLA Ops:
  0.7 0.0 copy-start
  0.7 33.1 %encoder.1 = (bf16[160,384]{1,0:T(8,128)(2,1)}, bf16[3,192,384]{2,1,0:T(8,128)(2,1)}, bf16[784,384]{1,0:T(8,128)(2,1)}, bf16[160,768]{1,0:T(8,128)(2,1)}, f32[16...) custom-call(s32[2]{0:T(128)} %bitcast.36, ...), custom_call_target="tpu_custom_call" | custom-call | tf_op jit(solution)/shard_map/encoder/pallas_call | solution.py:1107
  33.8 0.0 copy-done
  33.8 0.6 copy.40
  34.3 71.4 %decoder.1 = (bf16[2,784,192]{2,1,0:T(8,128)(2,1)}, bf16[160,384]{1,0:T(8,128)(2,1)}, f32[8,384]{1,0:T(8,128)}, bf16[160,384]{1,0:T(8,128)(2,1)}, bf16[384,896]{...) custom-call(bf16[160,384]{1,0:T(8,128)(2,1)} %get-tuple-element.62.refs_0_, s32[2]{0:T(128)} %bitcast.37, ...), custom_call_target="tpu_custom_call" | custom-call | tf_op jit(solution)/shard_map/decoder/pallas_call | solution.py:815
  105.8 77.4 %encoder_back.1 = (f32[2,128,384]{2,1,0:T(8,128)}, f32[24,128]{1,0:T(8,128)}, f32[48,4608]{1,0:T(8,128)}, f32[24,1536]{1,0:T(8,128)}, f32[24,768]{1,0:T(8,128)},...) custom-call(bf16[160,384]{1,0:T(8,128)(2,1)} %get-tuple-element.67.refs_0_, bf16[768,384]{1,0:T(8,128)(2,1)} %refs_1_.1, ...), custom_call_target="tpu_custom_call" | custom-call | tf_op jit(solution)/shard_map/encoder_back/pallas_call | solution.py:1580
  183.2 4.1 %finish.1 = (f32[2,192,784]{2,1,0:T(8,128)}, f32[2,128,384]{2,1,0:T(8,128)}, f32[3,48,384]{2,1,0:T(8,128)}, f32[48,384]{1,0:T(8,128)}, f32[48,1536]{1,0:T(8,128)...) custom-call(bf16[2,784,192]{2,1,0:T(8,128)(2,1)} %get-tuple-element., ...), custom_call_target="tpu_custom_call" | custom-call | tf_op jit(solution)/shard_map/finish/pallas_call | solution.py:1628
Async XLA Ops:
  0.7 33.1 %copy-start = (s32[2,1,256]{2,1,0:T(1,128)S(1)}, s32[2,1,256]{2,1,0:T(1,128)}, u32[]{:S(2)}) copy-start(s32[2,1,256]{2,1,0:T(1,128)} %param.21) | copy-start | bytes 6148
